TPU v7x, 32 devices: a whole 2x2x4 slice. The times are simulated.
32 devices in a mesh: dp: 8 (over z, core), mp: 4 (over y, x).
Axes of the slice: x: 2, y: 2, z: 4, core: 2. Of those that a mesh axis runs over, the one named last changes fastest.
Arguments:
- tokens: bfloat16 [8192, 2048], P(('dp', 'mp')), may hold values from -6 to 6
- cotangent: bfloat16 [8192, 2048], P(('dp', 'mp')), may hold values from -6 to 6
- domain: int32 [8], P('dp'), may hold values from 0 to 3
- query_weight: bfloat16 [2048, 2048], P(('dp', 'mp')), may hold values from -0.125 to 0.125
- key_weight: bfloat16 [2048, 2048], P(('dp', 'mp')), may hold values from -0.125 to 0.125
- value_weight: bfloat16 [2048, 4096], P(('dp', 'mp')), may hold values from -0.125 to 0.125
- gate_weight: bfloat16 [2048, 4096], P(('dp', 'mp')), may hold values from -0.125 to 0.125
- output_weight: bfloat16 [4096, 2048], P(('dp', 'mp')), may hold values from -0.1875 to 0.1875
- retention_gain: bfloat16 [2048], P(('dp', 'mp')), may hold values from 0.099609375 to 1.8984375
- retention_bias: bfloat16 [2048], P(('dp', 'mp')), may hold values from -2 to 2
- feedfwd_gain: bfloat16 [2048], P(('dp', 'mp')), may hold values from 0.099609375 to 1.8984375
- feedfwd_bias: bfloat16 [2048], P(('dp', 'mp')), may hold values from -2 to 2
- up_weight: bfloat16 [2048, 4096], P('dp', 'mp'), may hold values from -0.125 to 0.125
- down_weight: bfloat16 [4096, 2048], P('mp', 'dp'), may hold values from -0.1875 to 0.1875
Outputs:
- outputs: bfloat16 [8192, 2048], P(('dp', 'mp'))
- tokens_grad: bfloat16 [8192, 2048], P(('dp', 'mp'))
- query_grad: float32 [2048, 2048], P(('dp', 'mp'))
- key_grad: float32 [2048, 2048], P(('dp', 'mp'))
- value_grad: float32 [2048, 4096], P(('dp', 'mp'))
- gate_grad: float32 [2048, 4096], P(('dp', 'mp'))
- output_grad: float32 [4096, 2048], P(('dp', 'mp'))
- retgain_grad: float32 [2048], P(('dp', 'mp'))
- retbias_grad: float32 [2048], P(('dp', 'mp'))
- ffngain_grad: float32 [2048], P(('dp', 'mp'))
- ffnbias_grad: float32 [2048], P(('dp', 'mp'))
- up_grad: float32 [2048, 4096], P('dp', 'mp')
- down_grad: float32 [4096, 2048], P('mp', 'dp')
All inputs are finite; a program needn't handle non-finite values.
Results may differ from a plain program's by a relative error of at most 0.018.
Values may be sent and summed in bfloat16 or wider, within the bound.
No kernel may reach another device: no remote copies, remote signals or barrier semaphores. Data moves between devices by JAX's collectives and lax.ppermute only.
A program may use at most 448 MiB of HBM per device.

v0:
```python
import jax
import jax.numpy as jnp
from jax import lax
from jax.sharding import PartitionSpec as P

D = 2048
DV = 4096
HEADS = 8
KHEAD = 256
VHEAD = 512
SPAN = 256
DOMAINS = 4


EPSILON = 1e-05


def entering_2(x, axis, combine, identity, reverse):
    count, index = (lax.axis_size(axis), lax.axis_index(axis))
    everything = jax.tree.map(
        lambda part, kind: lax.all_gather(part.astype(kind), axis), x, (jnp.bfloat16, jnp.bfloat16)
    )
    start = jax.tree.map(
        lambda part, zero: jnp.broadcast_to(jnp.asarray(zero, part.dtype), part.shape), x, identity
    )

    def lap(k, before):
        at = count - 1 - k if reverse else k
        reached = at > index if reverse else at < index
        new = combine(
            before, jax.tree.map(lambda part, own: part[at].astype(own.dtype), everything, x)
        )
        return jax.tree.map(lambda a, b: jnp.where(reached, a, b), new, before)

    return lax.fori_loop(0, count, lap, start)


def layer_stats(values):
    center = values - jnp.mean(values, axis=-1, keepdims=True)
    factor = lax.rsqrt(jnp.mean(center * center, axis=-1, keepdims=True) + EPSILON)
    return (center * factor, factor)


def layer_back(grad, normal, factor):
    return factor * (
        grad
        - jnp.mean(grad, axis=-1, keepdims=True)
        - normal * jnp.mean(grad * normal, axis=-1, keepdims=True)
    )


def decay_logs(heads):
    return jnp.log1p(-jnp.exp2(-5.0 - jnp.arange(heads, dtype=jnp.float32)))


def rotation_tables(start, count, width):
    freq = 10000.0 ** (-2.0 * jnp.arange(width // 2, dtype=jnp.float32) / width)
    places = (start + jnp.arange(count, dtype=jnp.int32)).astype(jnp.float32)
    angle = places[:, None] * freq[None, :]
    return (jnp.cos(angle)[:, None, :], jnp.sin(angle)[:, None, :])


def rotate(values, cosine, sine):
    half = values.shape[-1] // 2
    first = values[..., :half]
    second = values[..., half:]
    return jnp.concatenate(
        [first * cosine - second * sine, first * sine + second * cosine], axis=-1
    )


def unrotate(values, cosine, sine):
    half = values.shape[-1] // 2
    first = values[..., :half]
    second = values[..., half:]
    return jnp.concatenate(
        [first * cosine + second * sine, second * cosine - first * sine], axis=-1
    )


def contract_rows(left, right):
    return lax.dot_general(
        left, right, (((0,), (0,)), ((), ())), preferred_element_type=jnp.float32
    )


def contract_cols(left, right):
    return lax.dot_general(
        left, right, (((1,), (1,)), ((), ())), preferred_element_type=jnp.float32
    )


def chain(earlier, later):
    return (later[0] + later[1][..., None, None] * earlier[0], earlier[1] * later[1])


def on_device(
    tokens,
    cotangent,
    domain,
    query_weight,
    key_weight,
    value_weight,
    gate_weight,
    output_weight,
    retention_gain,
    retention_bias,
    feedfwd_gain,
    feedfwd_bias,
    up_weight,
    down_weight,
):
    rows = tokens.shape[0]
    blocks = rows // SPAN
    w_query, w_key, w_value, w_gate, w_output, gain_one, bias_one, gain_two, bias_two = (
        lax.all_gather(query_weight, ("dp", "mp"), axis=0, tiled=True),
        lax.all_gather(key_weight, ("dp", "mp"), axis=0, tiled=True),
        lax.all_gather(value_weight, ("dp", "mp"), axis=0, tiled=True),
        lax.all_gather(gate_weight, ("dp", "mp"), axis=0, tiled=True),
        lax.all_gather(output_weight, ("dp", "mp"), axis=0, tiled=True),
        lax.all_gather(retention_gain, ("dp", "mp"), axis=0, tiled=True),
        lax.all_gather(retention_bias, ("dp", "mp"), axis=0, tiled=True),
        lax.all_gather(feedfwd_gain, ("dp", "mp"), axis=0, tiled=True),
        lax.all_gather(feedfwd_bias, ("dp", "mp"), axis=0, tiled=True),
    )
    classes = jnp.arange(DOMAINS, dtype=jnp.int32)
    member = (domain[0] == classes).astype(jnp.int32)
    counts = lax.psum(member * rows, ("dp", "mp"))
    own_count = jnp.sum(member * counts)
    total = rows * lax.axis_size("dp") * lax.axis_size("mp")
    row_scale = jnp.float32(total) / (DOMAINS * own_count.astype(jnp.float32))
    source = tokens.astype(jnp.float32)
    normal_one, factor_one = layer_stats(source)
    normed_one = (normal_one * gain_one.astype(jnp.float32) + bias_one.astype(jnp.float32)).astype(
        jnp.bfloat16
    )
    query_pre = jnp.dot(normed_one, w_query, preferred_element_type=jnp.float32)
    key_pre = jnp.dot(normed_one, w_key, preferred_element_type=jnp.float32)
    value_pre = jnp.dot(normed_one, w_value, preferred_element_type=jnp.float32)
    gate_pre = jnp.dot(normed_one, w_gate, preferred_element_type=jnp.float32)
    cosine, sine = rotation_tables(lax.axis_index("mp") * rows, rows, KHEAD)
    queries = (
        rotate(query_pre.reshape(rows, HEADS, KHEAD), cosine, sine)
        .astype(jnp.bfloat16)
        .reshape(blocks, SPAN, HEADS, KHEAD)
    )
    keys = (
        rotate(key_pre.reshape(rows, HEADS, KHEAD), cosine, sine)
        .astype(jnp.bfloat16)
        .reshape(blocks, SPAN, HEADS, KHEAD)
    )
    values = value_pre.astype(jnp.bfloat16).reshape(blocks, SPAN, HEADS, VHEAD)
    logs = decay_logs(HEADS)
    places = jnp.arange(SPAN, dtype=jnp.float32)
    spacing = places[:, None] - places[None, :]
    inner_decay = jnp.where(
        spacing[None] >= 0, jnp.exp(jnp.maximum(spacing, 0.0)[None] * logs[:, None, None]), 0.0
    )
    position_decay = jnp.exp(places[:, None] * logs[None, :])[None, :, :, None]
    key_decay = jnp.exp((SPAN - places)[:, None] * logs[None, :])[None, :, :, None]
    block_decay = jnp.exp(SPAN * logs)
    order = jnp.arange(blocks, dtype=jnp.float32)
    key_decayed = (keys.astype(jnp.float32) * key_decay).astype(jnp.bfloat16)
    intra_block_output = jnp.einsum(
        "bmhk,bmhv->bhkv", key_decayed, values, preferred_element_type=jnp.float32
    )
    trailing = jnp.exp(((blocks - 1 - order) * SPAN)[:, None] * logs[None, :])
    summary = jnp.sum(trailing[:, :, None, None] * intra_block_output, axis=0)
    factor = jnp.exp(rows * logs)
    identity = (jnp.zeros_like(summary), jnp.ones_like(factor))
    incoming, _ = entering_2((summary, factor), "mp", chain, identity, False)

    def advance(retention_state, piece):
        return (retention_state * block_decay[:, None, None] + piece, retention_state)

    _, entering = lax.scan(advance, incoming, intra_block_output)
    state_low = entering.astype(jnp.bfloat16)
    scores = jnp.einsum("bnhk,bmhk->bhnm", queries, keys, preferred_element_type=jnp.float32)
    weights = (scores * inner_decay[None]).astype(jnp.bfloat16)
    inner = jnp.einsum("bhnm,bmhv->bnhv", weights, values, preferred_element_type=jnp.float32)
    carried_state = (
        jnp.einsum("bnhk,bhkv->bnhv", queries, state_low, preferred_element_type=jnp.float32)
        * position_decay
    )
    retained = (inner + carried_state).reshape(rows, HEADS, VHEAD)
    grouped, group_factor = layer_stats(retained)
    flat_group = grouped.reshape(rows, DV)
    sigma = jax.nn.sigmoid(gate_pre)
    gated = (gate_pre * sigma * flat_group).astype(jnp.bfloat16)
    middle = source + jnp.dot(gated, w_output, preferred_element_type=jnp.float32)
    normal_two, factor_two = layer_stats(middle)
    normed_two = (normal_two * gain_two.astype(jnp.float32) + bias_two.astype(jnp.float32)).astype(
        jnp.bfloat16
    )
    up_full, down_full = (
        lax.all_gather(up_weight, "dp", axis=0, tiled=True),
        lax.all_gather(down_weight, "dp", axis=1, tiled=True),
    )
    group_rows = lax.all_gather(normed_two, "mp", axis=0, tiled=True)
    hidden_pre = jnp.dot(group_rows, up_full, preferred_element_type=jnp.float32)
    hidden = jax.nn.gelu(hidden_pre).astype(jnp.bfloat16)
    piece = hidden
    feed_sum = lax.psum_scatter(
        jnp.dot(piece, down_full, preferred_element_type=jnp.float32).astype(jnp.bfloat16),
        "mp",
        scatter_dimension=0,
        tiled=True,
    ).astype(jnp.float32)
    outputs = (middle + feed_sum).astype(jnp.bfloat16)
    cotan = cotangent.astype(jnp.float32) * row_scale
    grad_rows = lax.all_gather(cotan.astype(jnp.bfloat16), "mp", axis=0, tiled=True)
    d_hidden = contract_cols(grad_rows, down_full)
    down_part = contract_rows(hidden, grad_rows)
    _, gelu_pull = jax.vjp(jax.nn.gelu, hidden_pre)
    d_pre = gelu_pull(d_hidden)[0].astype(jnp.bfloat16)
    up_part = contract_rows(group_rows, d_pre)
    piece = d_pre
    d_normed_two = lax.psum_scatter(
        contract_cols(piece, up_full), "mp", scatter_dimension=0, tiled=True
    )
    up_grad, down_grad = (
        lax.psum_scatter(
            up_part.astype(jnp.bfloat16), "dp", scatter_dimension=0, tiled=True
        ).astype(jnp.float32),
        lax.psum_scatter(
            down_part.astype(jnp.bfloat16), "dp", scatter_dimension=1, tiled=True
        ).astype(jnp.float32),
    )
    gain_two_part = jnp.sum(d_normed_two * normal_two, axis=0)
    bias_two_part = jnp.sum(d_normed_two, axis=0)
    d_middle = cotan + layer_back(
        d_normed_two * gain_two.astype(jnp.float32), normal_two, factor_two
    )
    d_branch = d_middle.astype(jnp.bfloat16)
    output_part = contract_rows(gated, d_branch)
    d_gated = contract_cols(d_branch, w_output)
    d_grouped = (d_gated * gate_pre * sigma).reshape(rows, HEADS, VHEAD)
    d_gate = (d_gated * flat_group * (sigma + gate_pre * sigma * (1.0 - sigma))).astype(
        jnp.bfloat16
    )
    d_retained = layer_back(d_grouped, grouped, group_factor).reshape(blocks, SPAN, HEADS, VHEAD)
    d_inner = d_retained.astype(jnp.bfloat16)
    d_carried = (d_retained * position_decay).astype(jnp.bfloat16)
    d_weights = jnp.einsum("bnhv,bmhv->bhnm", d_inner, values, preferred_element_type=jnp.float32)
    d_scores = (d_weights * inner_decay[None]).astype(jnp.bfloat16)
    cross_grad = jnp.einsum(
        "bnhk,bnhv->bhkv", queries, d_carried, preferred_element_type=jnp.float32
    )
    leading = jnp.exp((order * SPAN)[:, None] * logs[None, :])
    own_grad = jnp.sum(leading[:, :, None, None] * cross_grad, axis=0)
    outgoing, _ = entering_2((own_grad, factor), "mp", chain, identity, True)

    def retreat(carry, piece):
        return (piece + block_decay[:, None, None] * carry, carry)

    _, following = lax.scan(retreat, outgoing, cross_grad, reverse=True)
    local_grad = following.astype(jnp.bfloat16)
    d_queries = jnp.einsum("bhnm,bmhk->bnhk", d_scores, keys, preferred_element_type=jnp.float32)
    d_queries = d_queries + jnp.einsum(
        "bnhv,bhkv->bnhk", d_carried, state_low, preferred_element_type=jnp.float32
    )
    d_keys = jnp.einsum("bhnm,bnhk->bmhk", d_scores, queries, preferred_element_type=jnp.float32)
    d_keys = d_keys + key_decay * jnp.einsum(
        "bmhv,bhkv->bmhk", values, local_grad, preferred_element_type=jnp.float32
    )
    d_values = jnp.einsum("bhnm,bnhv->bmhv", weights, d_inner, preferred_element_type=jnp.float32)
    d_values = d_values + jnp.einsum(
        "bmhk,bhkv->bmhv", key_decayed, local_grad, preferred_element_type=jnp.float32
    )
    d_query = (
        unrotate(d_queries.reshape(rows, HEADS, KHEAD), cosine, sine)
        .reshape(rows, D)
        .astype(jnp.bfloat16)
    )
    d_key = (
        unrotate(d_keys.reshape(rows, HEADS, KHEAD), cosine, sine)
        .reshape(rows, D)
        .astype(jnp.bfloat16)
    )
    d_value = d_values.reshape(rows, DV).astype(jnp.bfloat16)
    query_part = contract_rows(normed_one, d_query)
    key_part = contract_rows(normed_one, d_key)
    value_part = contract_rows(normed_one, d_value)
    gate_part = contract_rows(normed_one, d_gate)
    d_normed_one = (
        contract_cols(d_query, w_query)
        + contract_cols(d_key, w_key)
        + contract_cols(d_value, w_value)
        + contract_cols(d_gate, w_gate)
    )
    gain_one_part = jnp.sum(d_normed_one * normal_one, axis=0)
    bias_one_part = jnp.sum(d_normed_one, axis=0)
    d_tokens = d_middle + layer_back(
        d_normed_one * gain_one.astype(jnp.float32), normal_one, factor_one
    )
    (
        query_grad,
        key_grad,
        value_grad,
        gate_grad,
        output_grad,
        retgain_grad,
        retbias_grad,
        ffngain_grad,
        ffnbias_grad,
    ) = (
        lax.psum_scatter(query_part, ("dp", "mp"), scatter_dimension=0, tiled=True),
        lax.psum_scatter(key_part, ("dp", "mp"), scatter_dimension=0, tiled=True),
        lax.psum_scatter(value_part, ("dp", "mp"), scatter_dimension=0, tiled=True),
        lax.psum_scatter(gate_part, ("dp", "mp"), scatter_dimension=0, tiled=True),
        lax.psum_scatter(output_part, ("dp", "mp"), scatter_dimension=0, tiled=True),
        lax.psum_scatter(gain_one_part, ("dp", "mp"), scatter_dimension=0, tiled=True),
        lax.psum_scatter(bias_one_part, ("dp", "mp"), scatter_dimension=0, tiled=True),
        lax.psum_scatter(gain_two_part, ("dp", "mp"), scatter_dimension=0, tiled=True),
        lax.psum_scatter(bias_two_part, ("dp", "mp"), scatter_dimension=0, tiled=True),
    )
    return (
        outputs,
        d_tokens.astype(jnp.bfloat16),
        query_grad,
        key_grad,
        value_grad,
        gate_grad,
        output_grad,
        retgain_grad,
        retbias_grad,
        ffngain_grad,
        ffnbias_grad,
        up_grad,
        down_grad,
    )


def solution(mesh):
    return jax.shard_map(
        on_device,
        mesh=mesh,
        in_specs=(
            P(("dp", "mp"), None),
            P(("dp", "mp"), None),
            P("dp"),
            P(("dp", "mp"), None),
            P(("dp", "mp"), None),
            P(("dp", "mp"), None),
            P(("dp", "mp"), None),
            P(("dp", "mp"), None),
            P(("dp", "mp")),
            P(("dp", "mp")),
            P(("dp", "mp")),
            P(("dp", "mp")),
            P("dp", "mp"),
            P("mp", "dp"),
        ),
        out_specs=(
            P(("dp", "mp"), None),
            P(("dp", "mp"), None),
            P(("dp", "mp"), None),
            P(("dp", "mp"), None),
            P(("dp", "mp"), None),
            P(("dp", "mp"), None),
            P(("dp", "mp"), None),
            P(("dp", "mp")),
            P(("dp", "mp")),
            P(("dp", "mp")),
            P(("dp", "mp")),
            P("dp", "mp"),
            P("mp", "dp"),
        ),
        check_vma=False,
    )
```

profile of v0, /device:TPU:0, one launch (start us, length us, event | category | flops | bytes accessed | tf_op | source)
XLA Modules:
  0.0 4093.9 jit_solution(4308227146305654708)
XLA Ops:
  12.9 42.7 %all-reduce.9 = (bf16[2048]{0:T(1024)(128)(2,1)S(1)}, bf16[2048]{0:T(1024)(128)(2,1)S(1)}, bf16[2048]{0:T(1024)(128)(2,1)S(1)}, bf16[2048]{0:T(1024)(128)(2,1)S(1)}) all-reduce(bf16[2048]{0:T(1024)(128)(2,1)S(1)} %dynamic-update-slice.1, bf16[2048]{0:T(1024)(128)(2,1)S(1)} %dynamic-update-slice, ...), channel_id=1, replica_groups=mesh['dp'=8,'mp'=4] {'dp','mp'}, use_global_device_ids=true, to_apply=%add.1 | all-reduce | flops 8192 | bytes 32768
  58.2 33.1 all-gather.19.cloned.1.call-done
  98.0 72.4 %all-gather.21.cloned.1.call-done = bf16[2048,2048]{1,0:T(8,128)(2,1)} async-done(((bf16[64,2048]{1,0:T(8,128)(2,1)}), bf16[2048,2048]{1,0:T(8,128)(2,1)}) %all-gather.21.cloned.1.call-update) | async-done | bytes 8388624 | tf_op jit(solution)/shard_map/all_gather | solution.py:117
  179.5 107.3 %all-gather.17.cloned.1.call-done = bf16[2048,4096]{1,0:T(8,128)(2,1)} async-done(((bf16[64,4096]{1,0:T(8,128)(2,1)}), bf16[2048,4096]{1,0:T(8,128)(2,1)}) %all-gather.17.cloned.1.call-update) | async-done | bytes 16777232 | tf_op jit(solution)/shard_map/all_gather | solution.py:118
  286.8 8.9 convolution_convert_fusion
  300.1 38.8 psum.7
  344.3 8.7 all-gather.2
  359.0 25.4 all-gather.33.cloned.1.call-done
  384.4 22.6 while.40
  394.9 6.2 fusion.125
  401.1 5.9 fusion.125
  415.8 6.1 copy.159
  435.4 66.7 %all-gather.15.cloned.1.call-done = bf16[2048,4096]{1,0:T(8,128)(2,1)} async-done(((bf16[64,4096]{1,0:T(8,128)(2,1)}), bf16[2048,4096]{1,0:T(8,128)(2,1)}) %all-gather.15.cloned.1.call-update) | async-done | bytes 16777232 | tf_op jit(solution)/shard_map/all_gather | solution.py:119
  502.1 16.6 multiply_convert_fusion.4
  518.7 99.2 %all-gather.23.cloned.1.call-done = bf16[4096,2048]{1,0:T(8,128)(2,1)} async-done(((bf16[128,2048]{1,0:T(8,128)(2,1)}), bf16[4096,2048]{1,0:T(8,128)(2,1)}) %all-gather.23.cloned.1.call-update) | async-done | bytes 16777232 | tf_op jit(solution)/shard_map/all_gather | solution.py:120
  617.9 8.8 fusion.85
  628.6 11.4 reduce-scatter.12.cloned.1.call-start
  639.9 31.3 all-gather.31.cloned.1.call-done
  671.2 49.4 %all-gather.29.cloned.1.call-done = bf16[1024,2048]{1,0:T(8,128)(2,1)} async-done(((bf16[1024,256]{1,0:T(8,128)(2,1)}), bf16[1024,2048]{1,0:T(8,128)(2,1)}) %all-gather.29.cloned.1.call-update) | async-done | bytes 4194320 | tf_op jit(solution)/shard_map/all_gather | solution.py:197
  720.7 10.0 fusion.86
  730.6 37.1 all-gather.27.cloned.1.call-done
  767.7 53.7 %all-gather.25.cloned.1.call-done = bf16[1024,2048]{1,0:T(8,128)(2,1)} async-done(((bf16[256,2048]{1,0:T(8,128)(2,1)}), bf16[1024,2048]{1,0:T(8,128)(2,1)}) %all-gather.25.cloned.1.call-update) | async-done | bytes 4194320 | tf_op jit(solution)/shard_map/all_gather | solution.py:199
  821.4 13.4 fusion.8
  836.1 6.9 fusion.87
  843.0 10.3 convolution_convert_fusion.3
  853.4 76.2 %reduce-scatter.12.cloned.1.call-done = f32[256,2048]{1,0:T(8,128)} async-done(((f32[1024,2048]{1,0:T(8,128)}), f32[256,2048]{1,0:T(8,128)}) %reduce-scatter.12.cloned.1.call-update) | async-done | bytes 2097168 | tf_op jit(solution)/shard_map/reduce_scatter | solution.py:218
  932.7 52.7 %reduce-scatter.10.cloned.1.call-done = bf16[256,2048]{1,0:T(8,128)(2,1)} async-done(((bf16[1024,2048]{1,0:T(8,128)(2,1)}), bf16[256,2048]{1,0:T(8,128)(2,1)}) %reduce-scatter.10.cloned.1.call-update) | async-done | bytes 1048592 | tf_op jit(solution)/shard_map/reduce_scatter | solution.py:203
  990.3 16.4 multiply_convert_fusion
  1012.3 8.0 copy.169
  1042.7 8.6 convolution_convert_fusion.2
  1051.4 11.0 convolution_convert_fusion.1
  1073.5 55.5 %all-gather.35.cloned.1.call-done = bf16[32,256,512]{2,1,0:T(8,128)(2,1)} async-done(((bf16[8,256,512]{2,1,0:T(8,128)(2,1)}), bf16[32,256,512]{2,1,0:T(8,128)(2,1)}) %all-gather.35.cloned.1.call-update) | async-done | bytes 8388624 | tf_op jit(solution)/shard_map/all_gather | solution.py:21
  1129.0 22.2 while.41
  1157.3 8.3 fusion.71
  1167.5 8.3 fusion.73
  1177.4 15.3 fusion.59
  1192.7 15.6 fusion.67
  1215.2 13.7 fusion.69
  1233.6 6.2 fusion.88
  1239.8 7.1 convolution_add_fusion.2
  1246.9 13.0 convolution_add_fusion.1
  1259.9 13.8 fusion.23
  1273.7 41.2 %all-reduce.8 = (f32[2048]{0:T(1024)S(1)}, f32[2048]{0:T(1024)S(1)}, f32[2048]{0:T(1024)S(1)}, f32[2048]{0:T(1024)S(1)}) all-reduce(f32[2048]{0:T(1024)S(1)} %get-tuple-element.309, f32[2048]{0:T(1024)S(1)} %get-tuple-element.314, f32[2048]{0:T(1024)S(1)} %copy-done.39, ...), channel_id=11, replica_groups=mesh['dp'=8,'mp'=4] {'dp','mp'}, use_global_device_ids=true, to_apply=%region_26.27.clone | all-reduce | flops 8192 | bytes 65536
  1320.7 270.6 %reduce-scatter.16.cloned.1.call-done = f32[64,2048]{1,0:T(8,128)} async-done(((f32[2048,2048]{1,0:T(8,128)}), f32[64,2048]{1,0:T(8,128)}) %reduce-scatter.16.cloned.1.call-update) | async-done | bytes 524304 | tf_op jit(solution)/shard_map/reduce_scatter | solution.py:308
  1591.3 362.1 %reduce-scatter.14.cloned.1.call-done = f32[64,2048]{1,0:T(8,128)} async-done(((f32[2048,2048]{1,0:T(8,128)}), f32[64,2048]{1,0:T(8,128)}) %reduce-scatter.14.cloned.1.call-update) | async-done | bytes 524304 | tf_op jit(solution)/shard_map/reduce_scatter | solution.py:307
  1953.4 711.9 %reduce-scatter.22.cloned.1.call-done = f32[128,2048]{1,0:T(8,128)} async-done(((f32[4096,2048]{1,0:T(8,128)}), f32[128,2048]{1,0:T(8,128)}) %reduce-scatter.22.cloned.1.call-update) | async-done | bytes 1048592 | tf_op jit(solution)/shard_map/reduce_scatter | solution.py:311
  2665.3 710.9 %reduce-scatter.20.cloned.1.call-done = f32[64,4096]{1,0:T(8,128)} async-done(((f32[2048,4096]{1,0:T(8,128)}), f32[64,4096]{1,0:T(8,128)}) %reduce-scatter.20.cloned.1.call-update) | async-done | bytes 1048592 | tf_op jit(solution)/shard_map/reduce_scatter | solution.py:310
  3376.2 710.7 %reduce-scatter.18.cloned.1.call-done = f32[64,4096]{1,0:T(8,128)} async-done(((f32[2048,4096]{1,0:T(8,128)}), f32[64,4096]{1,0:T(8,128)}) %reduce-scatter.18.cloned.1.call-update) | async-done | bytes 1048592 | tf_op jit(solution)/shard_map/reduce_scatter | solution.py:309
  (234 shorter events, 169.9 us)
Async XLA Ops:
  7.2 50.0 %copy-start.5 = (bf16[256,2048]{1,0:T(8,128)(2,1)S(1)}, bf16[256,2048]{1,0:T(8,128)(2,1)}, u32[]{:S(2)}) copy-start(bf16[256,2048]{1,0:T(8,128)(2,1)} %param.18) | copy-start | bytes 3145732
  7.2 84.2 %all-gather.19.cloned.1.call-start = ((), (), s32[]{:S(2)}) async-start(), calls=%async_computation.11 | async-start | bytes 8650752 | tf_op jit(solution)/shard_map/all_gather | solution.py:116
  7.9 162.5 %all-gather.21.cloned.1.call-start = ((), (), s32[]{:S(2)}) async-start(), calls=%async_computation.12 | async-start | bytes 8650752 | tf_op jit(solution)/shard_map/all_gather | solution.py:117
  8.7 278.1 %all-gather.17.cloned.1.call-start = ((), (), s32[]{:S(2)}) async-start(), calls=%async_computation.10 | async-start | bytes 17301504 | tf_op jit(solution)/shard_map/all_gather | solution.py:118
  9.4 375.0 %all-gather.33.cloned.1.call-start = ((), (), s32[]{:S(2)}) async-start(), calls=%async_computation.27 | async-start | bytes 10485760 | tf_op jit(solution)/shard_map/all_gather | solution.py:21
  55.6 297.4 %copy-start.41 = (f32[8]{0:T(128)}, f32[8]{0:T(128)S(1)}, u32[]{:S(2)}) copy-start(f32[8]{0:T(128)S(1)} %negate_log-plus-one_fusion) | copy-start | bytes 100
  57.7 238.1 %copy-start.37 = (f32[256,8]{0,1:T(8,128)}, f32[256,8]{0,1:T(8,128)S(1)}, u32[]{:S(2)}) copy-start(f32[256,8]{0,1:T(8,128)S(1)} %get-tuple-element.365) | copy-start | bytes 24580
  58.2 119.1 %copy-start.29 = (f32[256,128]{1,0:T(8,128)}, f32[256,128]{1,0:T(8,128)S(1)}, u32[]{:S(2)}) copy-start(f32[256,128]{1,0:T(8,128)S(1)} %get-tuple-element.363) | copy-start | bytes 393220
  58.2 119.1 %copy-start.31 = (f32[256,128]{1,0:T(8,128)}, f32[256,128]{1,0:T(8,128)S(1)}, u32[]{:S(2)}) copy-start(f32[256,128]{1,0:T(8,128)S(1)} %get-tuple-element.364) | copy-start | bytes 393220
  286.8 9.0 copy-start.17
  286.8 9.0 copy-start.20
  295.7 59.5 %copy-start.7 = (bf16[256,4096]{1,0:T(8,128)(2,1)}, bf16[256,4096]{1,0:T(8,128)(2,1)S(1)}, u32[]{:S(2)}) copy-start(bf16[256,4096]{1,0:T(8,128)(2,1)S(1)} %convolution_convert_fusion) | copy-start | bytes 6291460
  298.2 203.9 %all-gather.15.cloned.1.call-start = ((), (), s32[]{:S(2)}) async-start(), calls=%async_computation.9 | async-start | bytes 17301504 | tf_op jit(solution)/shard_map/all_gather | solution.py:119
  298.8 319.1 %all-gather.23.cloned.1.call-start = ((), (), s32[]{:S(2)}) async-start(), calls=%async_computation.13 | async-start | bytes 17301504 | tf_op jit(solution)/shard_map/all_gather | solution.py:120
  299.4 371.9 %all-gather.31.cloned.1.call-start = ((), (), s32[]{:S(2)}) async-start(), calls=%async_computation.18 | async-start | bytes 5242880 | tf_op jit(solution)/shard_map/all_gather | solution.py:211
  342.6 378.0 %all-gather.29.cloned.1.call-start = ((), (), s32[]{:S(2)}) async-start(), calls=%async_computation.16 | async-start | bytes 4718592 | tf_op jit(solution)/shard_map/all_gather | solution.py:197
  343.4 424.3 %all-gather.27.cloned.1.call-start = ((), (), s32[]{:S(2)}) async-start(), calls=%async_computation.15 | async-start | bytes 4718592 | tf_op jit(solution)/shard_map/all_gather | solution.py:196
  344.1 477.3 %all-gather.25.cloned.1.call-start = ((), (), s32[]{:S(2)}) async-start(), calls=%async_computation.14 | async-start | bytes 5242880 | tf_op jit(solution)/shard_map/all_gather | solution.py:199
  344.2 11.0 copy-start.33
  344.3 10.9 copy-start.35
  384.4 22.6 copy-start.11
  384.4 22.6 copy-start.14
  628.6 301.0 %reduce-scatter.12.cloned.1.call-start = ((), (), s32[]{:S(2)}) async-start(), calls=%async_computation.19 | async-start | bytes 10485760 | tf_op jit(solution)/shard_map/reduce_scatter | solution.py:218
  821.4 14.7 copy-start.43
  843.0 142.4 %reduce-scatter.10.cloned.1.call-start = ((), (), s32[]{:S(2)}) async-start(), calls=%async_computation.17 | async-start | bytes 5242880 | tf_op jit(solution)/shard_map/reduce_scatter | solution.py:203
  853.3 275.6 %all-gather.35.cloned.1.call-start = ((), (), s32[]{:S(2)}) async-start(), calls=%async_computation.28 | async-start | bytes 10485760 | tf_op jit(solution)/shard_map/all_gather | solution.py:21
  1032.3 6.5 copy-start.12
  1032.3 6.5 copy-start.15
  1041.2 187.8 %reduce-scatter.24.cloned.1.call-start = ((), (), s32[]{:S(2)}) async-start(), calls=%async_computation.25 | async-start | bytes 4718592 | tf_op jit(solution)/shard_map/reduce_scatter | solution.py:222
  1051.3 180.2 %reduce-scatter.26.cloned.1.call-start = ((), (), s32[]{:S(2)}) async-start(), calls=%async_computation.26 | async-start | bytes 4718592 | tf_op jit(solution)/shard_map/reduce_scatter | solution.py:225
  1062.4 528.8 %reduce-scatter.16.cloned.1.call-start = ((), (), s32[]{:S(2)}) async-start(), calls=%async_computation.21 | async-start | bytes 17301504 | tf_op jit(solution)/shard_map/reduce_scatter | solution.py:308
  1064.0 5.3 copy-start.3
  1129.0 22.2 copy-start.38
  1151.2 3.9 copy-start.9
  1151.2 3.9 copy-start.30
  1151.2 3.9 copy-start.32
  1157.3 8.3 copy-start.24
  1165.6 787.7 %reduce-scatter.14.cloned.1.call-start = ((), (), s32[]{:S(2)}) async-start(), calls=%async_computation.20 | async-start | bytes 17301504 | tf_op jit(solution)/shard_map/reduce_scatter | solution.py:307
  1167.5 8.3 copy-start.26
  1175.8 1489.5 %reduce-scatter.22.cloned.1.call-start = ((), (), s32[]{:S(2)}) async-start(), calls=%async_computation.24 | async-start | bytes 34603008 | tf_op jit(solution)/shard_map/reduce_scatter | solution.py:311
  1192.7 2183.5 %reduce-scatter.20.cloned.1.call-start = ((), (), s32[]{:S(2)}) async-start(), calls=%async_computation.23 | async-start | bytes 34603008 | tf_op jit(solution)/shard_map/reduce_scatter | solution.py:310
  1208.4 2878.4 %reduce-scatter.18.cloned.1.call-start = ((), (), s32[]{:S(2)}) async-start(), calls=%async_computation.22 | async-start | bytes 34603008 | tf_op jit(solution)/shard_map/reduce_scatter | solution.py:309
  1208.5 3.9 copy-start
  1208.5 4.0 copy-start.19
  1208.5 4.2 copy-start.22
  1233.6 6.2 copy-start.25
  1259.9 13.8 copy-start.39
  1259.9 13.8 copy-start.40
  (18 other events, 31.6 us)
Sparse Core Ops, SparseCore 0:
  10.9 80.4 all-gather.18
  94.2 76.1 all-gather.20
  173.3 113.4 all-gather.16
  298.3 86.0 all-gather.32
  387.1 114.9 all-gather.14
  504.8 113.0 all-gather.22
  620.3 50.8 all-gather.30
  672.8 47.7 all-gather.28
  722.3 45.3 all-gather.26
  769.9 51.4 all-gather.24
  843.1 86.4 reduce-scatter.11
  932.6 52.6 reduce-scatter.9
  1041.3 87.6 all-gather.34
  1131.1 50.0 reduce-scatter.23
  1183.3 48.1 reduce-scatter.25
  1234.2 357.0 reduce-scatter.15
  1594.0 359.3 reduce-scatter.13
  1956.1 709.1 reduce-scatter.21
  2668.2 707.9 reduce-scatter.19
  3378.9 707.9 reduce-scatter.17
where the time goes:
time: 4100 us; the launch traced here: 4090 us
  waiting for transfers between devices  3530 us (86%)
  matrix products  254 us (6%)
  blocking collectives  131 us (3%)
  other arithmetic  83.1 us (2%)
  local copies, waits for them, and re-layouts  64.8 us (2%)
    reduce_scatter x1, waiting for transfers between devices, on_device(): lax.psum_scatter(output_part, ('dp', 'mp'), scatter_dimension=0, tiled=True)  712 us
    reduce_scatter x1, waiting for transfers between devices, on_device(): lax.psum_scatter(gate_part, ('dp', 'mp'), scatter_dimension=0, tiled=True)  711 us
    reduce_scatter x1, waiting for transfers between devices, on_device(): lax.psum_scatter(value_part, ('dp', 'mp'), scatter_dimension=0, tiled=True)  711 us
    reduce_scatter x1, waiting for transfers between devices, on_device(): lax.psum_scatter(query_part, ('dp', 'mp'), scatter_dimension=0, tiled=True)  362 us
    reduce_scatter x1, waiting for transfers between devices, on_device(): lax.psum_scatter(key_part, ('dp', 'mp'), scatter_dimension=0, tiled=True)  271 us
    all_gather x1, waiting for transfers between devices, on_device(): lax.all_gather(value_weight, ('dp', 'mp'), axis=0, tiled=True)  107 us
    all_gather x1, waiting for transfers between devices, on_device(): lax.all_gather(output_weight, ('dp', 'mp'), axis=0, tiled=True)  99.2 us
    unnamed x2, blocking collectives  84 us
  transfers between devices with their start and end apart: 20, of which 19 were waited for; matrix products, arithmetic and copies ran while one was open for 7% of the time, Pallas kernels for 0%

commit v1 on v0

v1 whole, which is shorter than its diff:
```python
import functools

import jax
import jax.numpy as jnp
from jax import lax
from jax.experimental import pallas as pl
from jax.experimental.pallas import tpu as pltpu
from jax.sharding import PartitionSpec as P

D = 2048
DV = 4096
HEADS = 8
KHEAD = 256
VHEAD = 512
SPAN = 256
DOMAINS = 4


EPSILON = 1e-05
F32 = jnp.float32
BF16 = jnp.bfloat16


def layer_stats(values):
    center = values - jnp.mean(values, axis=-1, keepdims=True)
    factor = lax.rsqrt(jnp.mean(center * center, axis=-1, keepdims=True) + EPSILON)
    return (center * factor, factor)


def layer_back(grad, normal, factor):
    return factor * (
        grad
        - jnp.mean(grad, axis=-1, keepdims=True)
        - normal * jnp.mean(grad * normal, axis=-1, keepdims=True)
    )


def decay_logs(heads):
    return jnp.log1p(-jnp.exp2(-5.0 - jnp.arange(heads, dtype=jnp.float32)))


def rotation_tables(count, width):
    freq = 10000.0 ** (-2.0 * jnp.arange(width // 2, dtype=jnp.float32) / width)
    places = jnp.arange(count, dtype=jnp.int32).astype(jnp.float32)
    angle = places[:, None] * freq[None, :]
    return (jnp.cos(angle), jnp.sin(angle))


def dot(left, right):
    return jnp.dot(left, right, preferred_element_type=F32)


def contract_rows(left, right):
    return lax.dot_general(
        left, right, (((0,), (0,)), ((), ())), preferred_element_type=F32
    )


def contract_cols(left, right):
    return lax.dot_general(
        left, right, (((1,), (1,)), ((), ())), preferred_element_type=F32
    )


def rotate(values, cosine, sine):
    half = values.shape[-1] // 2
    first, second = values[:, :half], values[:, half:]
    return jnp.concatenate(
        [first * cosine - second * sine, first * sine + second * cosine], axis=-1
    )


def unrotate(values, cosine, sine):
    half = values.shape[-1] // 2
    first, second = values[:, :half], values[:, half:]
    return jnp.concatenate(
        [first * cosine + second * sine, second * cosine - first * sine], axis=-1
    )


def head_forward(h, heads, pre_ref, cosine, sine, inner_decay, place_decay, state_low):
    q_at, k_at = h * KHEAD, (heads + h) * KHEAD
    v_at, g_at = 2 * heads * KHEAD + h * VHEAD, 2 * heads * KHEAD + (heads + h) * VHEAD
    query = rotate(pre_ref[:, q_at : q_at + KHEAD], cosine, sine).astype(BF16)
    key = rotate(pre_ref[:, k_at : k_at + KHEAD], cosine, sine).astype(BF16)
    value = pre_ref[:, v_at : v_at + VHEAD].astype(BF16)
    gate = pre_ref[:, g_at : g_at + VHEAD]
    weights = (contract_cols(query, key) * inner_decay).astype(BF16)
    retained = dot(weights, value) + dot(query, state_low) * place_decay
    grouped, factor = layer_stats(retained)
    return query, key, value, gate, weights, grouped, factor


def retention_forward_kernel(
    heads, order_ref, block_ref, pre_ref, cos_ref, sin_ref, inner_ref, place_ref, key_ref,
    gated_ref, low_ref, state,
):
    @pl.when(pl.program_id(0) == 0)
    def _():
        state[...] = jnp.zeros_like(state)

    cosine, sine = cos_ref[...], sin_ref[...]
    for h in range(heads):
        before = state[h]
        state_low = before.astype(BF16)
        low_ref[0, h] = state_low
        query, key, value, gate, weights, grouped, factor = head_forward(
            h, heads, pre_ref, cosine, sine, inner_ref[h], place_ref[h], state_low
        )
        gated = gate * jax.nn.sigmoid(gate) * grouped
        gated_ref[:, h * VHEAD : (h + 1) * VHEAD] = gated.astype(BF16)
        key_scaled = (key.astype(F32) * key_ref[h]).astype(BF16)
        state[h] = before * block_ref[h] + contract_rows(key_scaled, value)


def retention_backward_kernel(
    heads, order_ref, block_ref, pre_ref, cos_ref, sin_ref, inner_ref, place_ref, key_ref,
    low_ref, grad_ref, out_ref, state,
):
    @pl.when(pl.program_id(0) == 0)
    def _():
        state[...] = jnp.zeros_like(state)

    cosine, sine = cos_ref[...], sin_ref[...]
    for h in range(heads):
        state_low = low_ref[0, h]
        inner_decay, place_decay, key_decay = inner_ref[h], place_ref[h], key_ref[h]
        query, key, value, gate, weights, grouped, factor = head_forward(
            h, heads, pre_ref, cosine, sine, inner_decay, place_decay, state_low
        )
        q_at, k_at = h * KHEAD, (heads + h) * KHEAD
        v_at, g_at = 2 * heads * KHEAD + h * VHEAD, 2 * heads * KHEAD + (heads + h) * VHEAD
        d_gated = grad_ref[:, h * VHEAD : (h + 1) * VHEAD]
        sigma = jax.nn.sigmoid(gate)
        swish = gate * sigma
        out_ref[:, g_at : g_at + VHEAD] = (
            d_gated * grouped * (sigma + swish * (1.0 - sigma))
        ).astype(BF16)
        d_retained = layer_back(d_gated * swish, grouped, factor)
        d_inner = d_retained.astype(BF16)
        d_carried = (d_retained * place_decay).astype(BF16)
        d_scores = (contract_cols(d_inner, value) * inner_decay).astype(BF16)
        after = state[h]
        local_grad = after.astype(BF16)
        key_scaled = (key.astype(F32) * key_decay).astype(BF16)
        d_query = dot(d_scores, key) + contract_cols(d_carried, state_low)
        d_key = contract_rows(d_scores, query) + key_decay * contract_cols(value, local_grad)
        d_value = contract_rows(weights, d_inner) + dot(key_scaled, local_grad)
        out_ref[:, q_at : q_at + KHEAD] = unrotate(d_query, cosine, sine).astype(BF16)
        out_ref[:, k_at : k_at + KHEAD] = unrotate(d_key, cosine, sine).astype(BF16)
        out_ref[:, v_at : v_at + VHEAD] = d_value.astype(BF16)
        state[h] = after * block_ref[h] + contract_rows(query, d_carried)


def decays(heads, first):
    logs = lax.dynamic_slice(decay_logs(HEADS), (first,), (heads,))
    places = jnp.arange(SPAN, dtype=F32)
    spacing = places[:, None] - places[None, :]
    inner = jnp.where(
        spacing[None] >= 0, jnp.exp(jnp.maximum(spacing, 0.0)[None] * logs[:, None, None]), 0.0
    )
    place = jnp.exp(places[None, :] * logs[:, None])[:, :, None]
    key = jnp.exp((SPAN - places)[None, :] * logs[:, None])[:, :, None]
    return inner, place, key, jnp.exp(SPAN * logs)


def retention_call(heads, blocks, order, pre, tables, decay, extra):
    backward = bool(extra)
    wide, narrow = pre.shape[1], heads * VHEAD
    at = (lambda t: blocks - 1 - t) if backward else (lambda t: t)
    row = lambda t, order, *_: (order[at(t)], 0)
    place = lambda t, *_: (at(t), 0)
    whole = lambda t, *_: (0, 0, 0)
    low_spec = pl.BlockSpec((1, heads, KHEAD, VHEAD), lambda t, *_: (at(t), 0, 0, 0))
    in_specs = [
        pl.BlockSpec((SPAN, wide), row),
        pl.BlockSpec((SPAN, KHEAD // 2), place),
        pl.BlockSpec((SPAN, KHEAD // 2), place),
        pl.BlockSpec((heads, SPAN, SPAN), whole),
        pl.BlockSpec((heads, SPAN, 1), whole),
        pl.BlockSpec((heads, SPAN, 1), whole),
    ]
    inner, place_decay, key_decay, block_decay = decay
    if backward:
        in_specs += [low_spec, pl.BlockSpec((SPAN, narrow), row)]
        out_specs = pl.BlockSpec((SPAN, wide), row)
        out_shape = jax.ShapeDtypeStruct(pre.shape, BF16)
        body = retention_backward_kernel
    else:
        out_specs = (pl.BlockSpec((SPAN, narrow), row), low_spec)
        out_shape = (
            jax.ShapeDtypeStruct((pre.shape[0], narrow), BF16),
            jax.ShapeDtypeStruct((blocks, heads, KHEAD, VHEAD), BF16),
        )
        body = retention_forward_kernel
    products = (15 if backward else 7) * SPAN * SPAN * SPAN * 2 * heads * blocks
    return pl.pallas_call(
        functools.partial(body, heads),
        grid_spec=pltpu.PrefetchScalarGridSpec(
            num_scalar_prefetch=2,
            grid=(blocks,),
            in_specs=in_specs,
            out_specs=out_specs,
            scratch_shapes=[pltpu.VMEM((heads, KHEAD, VHEAD), F32)],
        ),
        out_shape=out_shape,
        compiler_params=pltpu.CompilerParams(vmem_limit_bytes=48 * 1024 * 1024),
        cost_estimate=pl.CostEstimate(
            flops=products, bytes_accessed=pre.size * (6 if backward else 5), transcendentals=0
        ),
        name="retention_backward" if backward else "retention_forward",
    )(order, block_decay, pre, *tables, inner, place_decay, key_decay, *extra)


def on_device(
    tokens,
    cotangent,
    domain,
    query_weight,
    key_weight,
    value_weight,
    gate_weight,
    output_weight,
    retention_gain,
    retention_bias,
    feedfwd_gain,
    feedfwd_bias,
    up_weight,
    down_weight,
):
    dp, mp = lax.axis_size("dp"), lax.axis_size("mp")
    here = lax.axis_index("mp")
    masks = range(mp)
    rows = tokens.shape[0]
    total = rows * mp
    blocks = total // SPAN
    heads = HEADS // mp
    part = query_weight.shape[0]
    own = part * mp

    def swap(x, mask):
        if mask == 0:
            return x
        return lax.ppermute(x, "mp", [(s, s ^ mask) for s in range(mp)])

    def spread(x):
        return [swap(x, m) for m in masks]

    def collect(pieces):
        received = [swap(pieces[m].astype(BF16), m).astype(F32) for m in masks[1:]]
        return functools.reduce(jnp.add, received, pieces[0].astype(F32))

    def by_index(pieces):
        stacked = jnp.stack(pieces)
        return [
            lax.dynamic_index_in_dim(stacked, here ^ m, 0, keepdims=False) for m in masks
        ]

    thin = jnp.stack(
        [retention_gain, retention_bias, feedfwd_gain, feedfwd_bias]
        + [jnp.broadcast_to(domain.astype(BF16), (part,))],
        axis=1,
    )
    thin = jnp.pad(thin, ((0, 0), (0, 128 - thin.shape[1])))

    def columns(weight, target):
        width = weight.shape[1] // mp
        return lax.dynamic_slice(weight, (0, target * width), (part, width))

    pieces = []
    for m in masks:
        target = here ^ m
        pieces.append(
            jnp.concatenate(
                [columns(w, target) for w in (query_weight, key_weight, value_weight, gate_weight)]
                + [thin],
                axis=1,
            )
        )
    pieces = by_index([swap(pieces[m], m) for m in masks])
    packed = jnp.concatenate(pieces, axis=0)
    wide = packed.shape[1] - 128
    thin_all = lax.all_gather(packed[:, wide : wide + 8], "dp", axis=0, tiled=True)
    gain_one, bias_one, gain_two, bias_two = (thin_all[:, n].astype(F32)[None] for n in range(4))
    w_in = lax.all_gather(packed[:, :wide], "dp", axis=0, tiled=True)

    shuffle = [(b, (b % dp) * mp + b // dp) for b in range(dp * mp)]
    w_out = lax.all_gather(
        lax.ppermute(output_weight, ("dp", "mp"), shuffle), "dp", axis=0, tiled=True
    )
    w_up = lax.all_gather(up_weight, "dp", axis=0, tiled=True)
    w_down = lax.all_gather(down_weight.T, "dp", axis=0, tiled=True)

    source_rows = jnp.concatenate(spread(tokens), axis=0)
    cotan_rows = jnp.concatenate(spread(cotangent), axis=0)

    domains = thin_all[::own, 4]
    own_count = jnp.sum((domains == domain[0].astype(BF16)).astype(F32)) * (rows * mp)
    row_scale = F32(rows * dp * mp) / (DOMAINS * own_count)

    tables = rotation_tables(total, KHEAD)
    decay = decays(heads, here * heads)
    block_order = (
        (jnp.arange(mp, dtype=jnp.int32) ^ here)[:, None] * (rows // SPAN)
        + jnp.arange(rows // SPAN, dtype=jnp.int32)[None]
    ).reshape(-1)

    normal_rows, _ = layer_stats(source_rows.astype(F32))
    normed_one = (normal_rows * gain_one + bias_one).astype(BF16)
    pre = dot(normed_one, w_in)
    gated, state_low = retention_call(heads, blocks, block_order, pre, tables, decay, ())

    def by_piece(x):
        return [x[m * rows : (m + 1) * rows] for m in masks]

    source = tokens.astype(F32)
    middle = source + collect([dot(piece, w_out) for piece in by_piece(gated)])
    normal_two, factor_two = layer_stats(middle)
    normed_two = (normal_two * gain_two + bias_two).astype(BF16)
    normed_rows = jnp.concatenate(spread(normed_two), axis=0)
    hidden_pre = dot(normed_rows, w_up)
    hidden = jax.nn.gelu(hidden_pre).astype(BF16)
    feed_sum = collect([contract_cols(piece, w_down) for piece in by_piece(hidden)])
    outputs = (middle + feed_sum).astype(BF16)

    grad_rows = (cotan_rows.astype(F32) * row_scale).astype(BF16)
    d_hidden = dot(grad_rows, w_down)
    _, gelu_pull = jax.vjp(jax.nn.gelu, hidden_pre)
    d_pre = gelu_pull(d_hidden)[0].astype(BF16)
    d_normed_two = collect([contract_cols(piece, w_up) for piece in by_piece(d_pre)])
    down_part = contract_rows(grad_rows, hidden).astype(BF16)
    up_part = contract_rows(normed_rows, d_pre).astype(BF16)

    cotan = cotangent.astype(F32) * row_scale
    d_middle = cotan + layer_back(d_normed_two * gain_two, normal_two, factor_two)
    branch_rows = jnp.concatenate(spread(d_middle.astype(BF16)), axis=0)
    d_gated = contract_cols(branch_rows, w_out)
    output_part = contract_rows(gated, branch_rows).astype(BF16)
    d_in = retention_call(
        heads, blocks, block_order, pre, tables, decay, (state_low, d_gated)
    )
    in_part = contract_rows(normed_one, d_in).astype(BF16)
    d_normed_one = collect([contract_cols(piece, w_in) for piece in by_piece(d_in)])
    normal_one, factor_one = layer_stats(source)
    d_tokens = d_middle + layer_back(d_normed_one * gain_one, normal_one, factor_one)

    scatter = functools.partial(
        lax.psum_scatter, axis_name="dp", scatter_dimension=0, tiled=True
    )
    down_grad = scatter(down_part).astype(F32).T
    up_grad = scatter(up_part).astype(F32)
    unshuffle = [(target, at) for at, target in shuffle]
    output_grad = lax.ppermute(scatter(output_part), ("dp", "mp"), unshuffle).astype(F32)
    in_grad = scatter(in_part)
    pieces = by_index([in_grad[m * part : (m + 1) * part] for m in masks])
    pieces = by_index([swap(pieces[m], m) for m in masks])
    grads, at = [], 0
    for weight in (query_weight, key_weight, value_weight, gate_weight):
        width = weight.shape[1] // mp
        grads.append(
            jnp.concatenate([p[:, at : at + width] for p in pieces], axis=1).astype(F32)
        )
        at += width

    thin_grads = jnp.stack(
        [
            jnp.sum(d_normed_one * normal_one, axis=0),
            jnp.sum(d_normed_one, axis=0),
            jnp.sum(d_normed_two * normal_two, axis=0),
            jnp.sum(d_normed_two, axis=0),
        ],
        axis=0,
    )
    thin_grads = lax.psum_scatter(
        thin_grads, ("dp", "mp"), scatter_dimension=1, tiled=True
    )
    return (
        outputs,
        d_tokens.astype(BF16),
        *grads,
        output_grad,
        *(thin_grads[n] for n in range(4)),
        up_grad,
        down_grad,
    )


def solution(mesh):
    return jax.shard_map(
        on_device,
        mesh=mesh,
        in_specs=(
            P(("dp", "mp"), None),
            P(("dp", "mp"), None),
            P("dp"),
            P(("dp", "mp"), None),
            P(("dp", "mp"), None),
            P(("dp", "mp"), None),
            P(("dp", "mp"), None),
            P(("dp", "mp"), None),
            P(("dp", "mp")),
            P(("dp", "mp")),
            P(("dp", "mp")),
            P(("dp", "mp")),
            P("dp", "mp"),
            P("mp", "dp"),
        ),
        out_specs=(
            P(("dp", "mp"), None),
            P(("dp", "mp"), None),
            P(("dp", "mp"), None),
            P(("dp", "mp"), None),
            P(("dp", "mp"), None),
            P(("dp", "mp"), None),
            P(("dp", "mp"), None),
            P(("dp", "mp")),
            P(("dp", "mp")),
            P(("dp", "mp")),
            P(("dp", "mp")),
            P("dp", "mp"),
            P("mp", "dp"),
        ),
        check_vma=False,
    )
```

time: 4100 us -> 929 us (0.23)
  waiting for transfers between devices: 3530 us -> 566 us
  blocking collectives: 131 us -> 22.7 us
  matrix products: 254 us -> 159 us
  starting transfers between devices: 12.1 us -> 85.1 us
  other arithmetic: 83.1 us -> 28.1 us
    reduce_scatter x9 -> x4, waiting for transfers between devices: 2900 us -> 96.5 us  [the longest x1 48.4 us: on_device(): down_grad = scatter(down_part).astype(F32).T]
    all_gather x11 -> x4, waiting for transfers between devices: 631 us -> 50.5 us  [the longest x1 31.8 us: on_device(): w_in = lax.all_gather(packed[:, :wide], 'dp', axis=0, tiled=True)]
    ppermute x0 -> x32, waiting for transfers between devices: none -> 300 us  [the longest x30 300 us: swap(): return lax.ppermute(x, 'mp', [(s, s ^ mask) for s in range(mp)])]
    unnamed x20 -> x10, waiting for transfers between devices: 4.71 us -> 119 us
    ppermute x0 -> x32, starting transfers between devices: none -> 84.3 us  [the longest x30 81.9 us: swap(): return lax.ppermute(x, 'mp', [(s, s ^ mask) for s in range(mp)])]
    unnamed x2 -> x0, blocking collectives: 84 us -> none
    dot_general x19 -> x7, matrix products: 100 us -> 51.5 us  [dot(): return jnp.dot(left, right, preferred_element_type=F32)]
    select_n x8 -> x1, other arithmetic: 44.5 us -> 0.16 us  [decays(): jnp.where(spacing[None] >= 0, jnp.exp(jnp.maximum(spacing, 0.0)[None] * l...]
  transfers between devices with their start and end apart: 20 -> 41, of which waited for: 19 -> 25; matrix products, arithmetic and copies ran while one was open for 7% -> 18% of each run, Pallas kernels for 0% -> 3%
where the time goes in v1:
time: 929 us; the launch traced here: 925 us
  waiting for transfers between devices  566 us (61%)
  matrix products  159 us (17%)
  starting transfers between devices  85.1 us (9%)
  other arithmetic  28.1 us (3%)
  local copies, waits for them, and re-layouts  24.3 us (3%)
  Pallas kernels  23.7 us (3%)
  blocking collectives  22.7 us (2%)
  between operations  16.2 us (2%)
    ppermute x30, waiting for transfers between devices, swap(): return lax.ppermute(x, 'mp', [(s, s ^ mask) for s in range(mp)])  300 us
    unnamed x10, waiting for transfers between devices  119 us
    ppermute x30, starting transfers between devices, swap(): return lax.ppermute(x, 'mp', [(s, s ^ mask) for s in range(mp)])  81.9 us
    dot_general x13, matrix products, contract_cols(): lax.dot_general(left, right, (((1,), (1,)), ((), ())), preferred_element_...  62.2 us
    dot_general x7, matrix products, dot(): return jnp.dot(left, right, preferred_element_type=F32)  51.5 us
    reduce_scatter x1, waiting for transfers between devices, on_device(): down_grad = scatter(down_part).astype(F32).T  48.4 us
    reduce_scatter x1, waiting for transfers between devices, on_device(): up_grad = scatter(up_part).astype(F32)  48.1 us
    dot_general x4, matrix products, contract_rows(): lax.dot_general(left, right, (((0,), (0,)), ((), ())), preferred_element_...  44.8 us
  transfers between devices with their start and end apart: 41, of which 25 were waited for; matrix products, arithmetic and copies ran while one was open for 18% of the time, Pallas kernels for 3%

profile of v1, /device:TPU:0, one launch (start us, length us, event | category | flops | bytes accessed | tf_op | source)
XLA Modules:
  0.0 924.8 jit_solution(13369458749670230038)
XLA Ops:
  13.1 3.0 collective-permute-start.3
  17.6 8.8 collective-permute-done.3
  26.4 9.4 %collective-permute-done.4 = bf16[64,3200]{1,0:T(8,128)(2,1)S(1)} collective-permute-done((bf16[64,3200]{1,0:T(8,128)(2,1)S(1)}, bf16[64,3200]{1,0:T(8,128)(2,1)S(1)}, u32[]{:S(2)}, u32[]{:S(2)}) %collective-permute-start.4) | collective-permute-done | bytes 409632 | tf_op jit(solution)/shard_map/ppermute | solution.py:244
  41.1 45.6 %collective-permute-start = (bf16[256,2048]{1,0:T(8,128)(2,1)S(1)}, bf16[256,2048]{1,0:T(8,128)(2,1)}, u32[]{:S(2)}, u32[]{:S(2)}) collective-permute-start(bf16[256,2048]{1,0:T(8,128)(2,1)S(1)} %copy-done.7), channel_id=1, source_target_pairs={{0,1},{1,0},{2,3},{3,2},{4,5},{5,4},{6,7},{7,6},{8,9},{9,8},{10,11... | collective-permute-start | bytes 3145736 | tf_op jit(solution)/shard_map/ppermute | solution.py:244
  91.5 22.7 %all_gather.15 = bf16[2048,8]{1,0:T(8,128)(2,1)S(1)} all-gather(bf16[256,8]{1,0:T(8,128)(2,1)S(1)} %pad_maximum_fusion.13), channel_id=1, replica_groups=mesh['dp'=8,'mp'=4] {'dp'}, dimensions={0}, use_global_device_ids=true | all-gather | bytes 36864 | tf_op jit(solution)/shard_map/all_gather | solution.py:283
  115.4 16.7 %collective-permute-done.1 = bf16[256,2048]{1,0:T(8,128)(2,1)} collective-permute-done((bf16[256,2048]{1,0:T(8,128)(2,1)S(1)}, bf16[256,2048]{1,0:T(8,128)(2,1)}, u32[]{:S(2)}, u32[]{:S(2)}) %collective-permute-start.1) | collective-permute-done | bytes 1048608 | tf_op jit(solution)/shard_map/ppermute | solution.py:244
  132.1 2.2 convert_reduce_fusion
  134.4 2.9 fusion.2
  137.3 31.8 %all-gather.5.cloned.1.call-done = bf16[2048,3072]{1,0:T(8,128)(2,1)} async-done(((bf16[256,3072]{1,0:T(8,128)(2,1)}), bf16[2048,3072]{1,0:T(8,128)(2,1)}) %all-gather.5.cloned.1.call-update) | async-done | bytes 12582928 | tf_op jit(solution)/shard_map/all_gather | solution.py:285
  169.1 19.9 %fusion.64.pre_ref = f32[1024,3072]{1,0:T(8,128)} fusion(bf16[2048,3072]{1,0:T(8,128)(2,1)} %all-gather.5.cloned.1.call-done, f32[2048]{0:T(1024)S(1)} %get-tuple-element.92, f32[2048]{0:T(1024)S(1)} %get-tuple-element.93, f32[1024]{0:T(1024)S(1)} %add_rsqrt_fusion, f32[1024]{0:T(1024)S(1)} %broadcast_multiply_fusion, ...), kind=kOutput, calls=%fused_computation.173 | convolution fusion | flops 12912164864 | bytes 29384704 | tf_op jit(solution)/shard_map/dot_general | solution.py:50
  189.0 8.4 retention_forward.1
  198.7 18.8 %all-gather.7.cloned.1.call-done = bf16[1024,2048]{1,0:T(8,128)(2,1)} async-done(((bf16[128,2048]{1,0:T(8,128)(2,1)}), bf16[1024,2048]{1,0:T(8,128)(2,1)}) %all-gather.7.cloned.1.call-update) | async-done | bytes 4194320 | tf_op jit(solution)/shard_map/all_gather | solution.py:288
  217.5 3.7 convolution_convert_fusion.12
  227.5 19.8 %collective-permute-done.7 = bf16[256,2048]{1,0:T(8,128)(2,1)S(1)} collective-permute-done((bf16[256,2048]{1,0:T(8,128)(2,1)S(1)}, bf16[256,2048]{1,0:T(8,128)(2,1)S(1)}, u32[]{:S(2)}, u32[]{:S(2)}) %collective-permute-start.7) | collective-permute-done | bytes 1048608 | tf_op jit(solution)/shard_map/ppermute | solution.py:244
  247.3 24.3 %collective-permute-done.8 = bf16[256,2048]{1,0:T(8,128)(2,1)S(1)} collective-permute-done((bf16[256,2048]{1,0:T(8,128)(2,1)S(1)}, bf16[256,2048]{1,0:T(8,128)(2,1)S(1)}, u32[]{:S(2)}, u32[]{:S(2)}) %collective-permute-start.8) | collective-permute-done | bytes 1048608 | tf_op jit(solution)/shard_map/ppermute | solution.py:244
  284.4 18.3 %collective-permute-done.10 = bf16[256,2048]{1,0:T(8,128)(2,1)} collective-permute-done((bf16[256,2048]{1,0:T(8,128)(2,1)}, bf16[256,2048]{1,0:T(8,128)(2,1)}, u32[]{:S(2)}, u32[]{:S(2)}) %collective-permute-start.10) | collective-permute-done | bytes 1048608 | tf_op jit(solution)/shard_map/ppermute | solution.py:244
  304.3 21.3 %collective-permute-done.11 = bf16[256,2048]{1,0:T(8,128)(2,1)} collective-permute-done((bf16[256,2048]{1,0:T(8,128)(2,1)}, bf16[256,2048]{1,0:T(8,128)(2,1)}, u32[]{:S(2)}, u32[]{:S(2)}) %collective-permute-start.11) | collective-permute-done | bytes 1048608 | tf_op jit(solution)/shard_map/ppermute | solution.py:244
  326.2 11.2 %multiply_convert_fusion.1 = (bf16[1024,1024]{1,0:T(8,128)(2,1)}, f32[1024,1024]{1,0:T(8,128)}) fusion(bf16[2048,1024]{1,0:T(8,128)(2,1)} %all-gather.9.cloned.1.call-done, bf16[256,2048]{1,0:T(8,128)(2,1)} %collective-permute-done.12, bf16[256,2048]{1,0:T(8,128)(2,1)} %collective-permute-done.11, bf16[256,2048]{1,0:T(8,128)(2,1)} %collective-permute-done.10, ...), kind=kOutput, calls=%fused_computation.22 | convolution fusion | flops 4321181696 | bytes 14680064 | tf_op jit(solution)/shard_map/dot_general | solution.py:50
  337.3 10.4 %collective-permute-done.16 = bf16[256,2048]{1,0:T(8,128)(2,1)} collective-permute-done((bf16[256,2048]{1,0:T(8,128)(2,1)}, bf16[256,2048]{1,0:T(8,128)(2,1)}, u32[]{:S(2)}, u32[]{:S(2)}) %collective-permute-start.16) | collective-permute-done | bytes 1048608 | tf_op jit(solution)/shard_map/ppermute | solution.py:244
  347.8 20.0 %collective-permute-done.17 = bf16[256,2048]{1,0:T(8,128)(2,1)} collective-permute-done((bf16[256,2048]{1,0:T(8,128)(2,1)}, bf16[256,2048]{1,0:T(8,128)(2,1)}, u32[]{:S(2)}, u32[]{:S(2)}) %collective-permute-start.17) | collective-permute-done | bytes 1048608 | tf_op jit(solution)/shard_map/ppermute | solution.py:244
  369.2 12.2 %fusion.12 = bf16[1024,1024]{1,0:T(8,128)(2,1)S(1)} fusion(f32[1024,1024]{1,0:T(8,128)} %get-tuple-element.161, bf16[2048,1024]{0,1:T(8,128)(2,1)} %all-gather.11.cloned.1.call-done, bf16[256,2048]{1,0:T(8,128)(2,1)} %collective-permute-done.18, bf16[256,2048]{1,0:T(8,128)(2,1)} %collective-permute-done.17, bf16[256,2048]{1,0:T(8,128)(2,1)} %collective-permute-done.16, ...), kind=kOutput, calls=%fused_computation.18 | convolution fusion | flops 4336910336 | bytes 14680068 | tf_op jit(solution)/shard_map/dot_general | solution.py:50
  389.0 19.9 %collective-permute-done.19 = bf16[256,2048]{1,0:T(8,128)(2,1)S(1)} collective-permute-done((bf16[256,2048]{1,0:T(8,128)(2,1)S(1)}, bf16[256,2048]{1,0:T(8,128)(2,1)S(1)}, u32[]{:S(2)}, u32[]{:S(2)}) %collective-permute-start.19) | collective-permute-done | bytes 1048608 | tf_op jit(solution)/shard_map/ppermute | solution.py:244
  408.9 21.7 %collective-permute-done.20 = bf16[256,2048]{1,0:T(8,128)(2,1)S(1)} collective-permute-done((bf16[256,2048]{1,0:T(8,128)(2,1)S(1)}, bf16[256,2048]{1,0:T(8,128)(2,1)S(1)}, u32[]{:S(2)}, u32[]{:S(2)}) %collective-permute-start.20) | collective-permute-done | bytes 1048608 | tf_op jit(solution)/shard_map/ppermute | solution.py:244
  430.6 2.4 multiply_reduce_fusion
  433.0 3.7 fusion.66
  440.2 22.6 %collective-permute-done.22 = bf16[256,2048]{1,0:T(8,128)(2,1)S(1)} collective-permute-done((bf16[256,2048]{1,0:T(8,128)(2,1)S(1)}, bf16[256,2048]{1,0:T(8,128)(2,1)S(1)}, u32[]{:S(2)}, u32[]{:S(2)}) %collective-permute-start.22) | collective-permute-done | bytes 1048608 | tf_op jit(solution)/shard_map/ppermute | solution.py:244
  462.8 16.5 %collective-permute-done.23 = bf16[256,2048]{1,0:T(8,128)(2,1)S(1)} collective-permute-done((bf16[256,2048]{1,0:T(8,128)(2,1)S(1)}, bf16[256,2048]{1,0:T(8,128)(2,1)S(1)}, u32[]{:S(2)}, u32[]{:S(2)}) %collective-permute-start.23) | collective-permute-done | bytes 1048608 | tf_op jit(solution)/shard_map/ppermute | solution.py:244
  481.4 6.6 convolution_convert_fusion.3
  488.1 10.1 %fusion.34.grad_ref = f32[1024,1024]{1,0:T(8,128)} fusion(bf16[1024,2048]{1,0:T(8,128)(2,1)} %all-gather.7.cloned.1.call-done, bf16[256,2048]{1,0:T(8,128)(2,1)} %copy-done.25, bf16[256,2048]{1,0:T(8,128)(2,1)} %copy-done.24, bf16[256,2048]{1,0:T(8,128)(2,1)} %copy-done.22, bf16[256,2048]{1,0:T(8,128)(2,1)} %copy-done.16), kind=kOutput, calls=%fused_computation.85 | convolution fusion | flops 4311744512 | bytes 12582912 | tf_op jit(solution)/shard_map/dot_general | solution.py:60
  498.2 15.3 %retention_backward.1 = bf16[1024,3072]{1,0:T(8,128)(2,1)} custom-call(s32[4]{0:T(128)S(1)} %iota_xor_fusion.order_ref, f32[2]{0:T(128)S(1)} %get-tuple-element.96.block_ref, f32[1024,3072]{1,0:T(8,128)} %fusion.64.pre_ref, f32[1024,128]{1,0:T(8,128)S(1)} %get-tuple-element.155.cos_ref, f32[1024,128]{1,0:T(8,128)S(1)} %get-tuple-element.154.sin_ref, ...), custom_call_target="tpu_custom_call" | custom-call | flops 4026531840 | bytes 18874368 | tf_op jit(solution)/shard_map/retention_backward/pallas_call | solution.py:197
  513.5 19.8 %convolution_convert_fusion = bf16[2048,3072]{1,0:T(8,128)(2,1)} fusion(bf16[1024,3072]{1,0:T(8,128)(2,1)} %retention_backward.1, f32[2048]{0:T(1024)S(1)} %get-tuple-element.92, f32[2048]{0:T(1024)S(1)} %get-tuple-element.93, f32[1024]{0:T(1024)S(1)} %add_rsqrt_fusion, f32[1024]{0:T(1024)S(1)} %broadcast_multiply_fusion, ...), kind=kOutput, calls=%fused_computation | convolution fusion | flops 12918456320 | bytes 23093248 | tf_op jit(solution)/shard_map/dot_general | solution.py:54
  533.6 8.8 convolution_convert_fusion.15
  543.6 9.1 convolution_convert_fusion.14
  552.7 2.2 collective-permute-start.26
  554.9 7.9 convolution_convert_fusion.13
  564.2 2.8 collective-permute-done.25
  567.0 27.6 %collective-permute-done.26 = bf16[256,2048]{1,0:T(8,128)(2,1)S(1)} collective-permute-done((bf16[256,2048]{1,0:T(8,128)(2,1)S(1)}, bf16[256,2048]{1,0:T(8,128)(2,1)S(1)}, u32[]{:S(2)}, u32[]{:S(2)}) %collective-permute-start.26) | collective-permute-done | bytes 1048608 | tf_op jit(solution)/shard_map/ppermute | solution.py:244
  595.6 11.2 %fusion.25 = (f32[2048]{0:T(1024)S(1)}, f32[256]{0:T(256)S(1)}, f32[256]{0:T(256)S(1)}, f32[2048]{0:T(1024)S(1)}, f32[256,2048]{1,0:T(8,128)}) fusion(bf16[256,2048]{1,0:T(8,128)(2,1)S(1)} %copy-done.7, f32[256]{0:T(256)S(1)} %add_rsqrt_fusion.1, f32[256]{0:T(256)S(1)} %broadcast_multiply_fusion.3, f32[2048]{0:T(1024)S(1)} %get-tuple-element.93, ...), kind=kOutput, calls=%fused_computation.54 | convolution fusion | flops 3229609472 | bytes 20475904 | tf_op jit(solution)/shard_map/dot_general | solution.py:60
  608.2 9.5 %convolution_convert_fusion.1 = bf16[2048,1024]{1,0:T(8,128)(2,1)} fusion(bf16[1024,1024]{1,0:T(8,128)(2,1)} %get-tuple-element.160, bf16[256,2048]{1,0:T(8,128)(2,1)} %collective-permute-done.18, bf16[256,2048]{1,0:T(8,128)(2,1)} %collective-permute-done.17, bf16[256,2048]{1,0:T(8,128)(2,1)} %collective-permute-done.16, bf16[256,2048]{1,0:T(8,128)(2,1)} %param.15, ...), kind=kOutput, calls=%fused_computation.23 | convolution fusion | flops 4318035968 | bytes 10485764 | tf_op jit(solution)/shard_map/dot_general | solution.py:54
  619.4 8.8 convolution_convert_fusion.2
  629.9 3.6 convolution_convert_fusion.9
  639.8 19.9 %collective-permute-done.13 = bf16[256,2048]{1,0:T(8,128)(2,1)S(1)} collective-permute-done((bf16[256,2048]{1,0:T(8,128)(2,1)S(1)}, bf16[256,2048]{1,0:T(8,128)(2,1)S(1)}, u32[]{:S(2)}, u32[]{:S(2)}) %collective-permute-start.13) | collective-permute-done | bytes 1048608 | tf_op jit(solution)/shard_map/ppermute | solution.py:244
  659.6 16.9 %collective-permute-done.14 = bf16[256,2048]{1,0:T(8,128)(2,1)S(1)} collective-permute-done((bf16[256,2048]{1,0:T(8,128)(2,1)S(1)}, bf16[256,2048]{1,0:T(8,128)(2,1)S(1)}, u32[]{:S(2)}, u32[]{:S(2)}) %collective-permute-start.14) | collective-permute-done | bytes 1048608 | tf_op jit(solution)/shard_map/ppermute | solution.py:244
  676.6 2.7 add_convert_fusion
  687.3 2.5 collective-permute-start.29
  689.9 118.3 %reduce-scatter.16.cloned.1.call-done = f32[64,4]{1,0:T(8,128)} async-done(((f32[2048,4]{1,0:T(8,128)}), f32[64,4]{1,0:T(8,128)}) %reduce-scatter.16.cloned.1.call-update) | async-done | bytes 1040
  811.5 48.4 %reduce-scatter.14.cloned.1.call-done = bf16[256,1024]{1,0:T(8,128)(2,1)} async-done(((bf16[2048,1024]{1,0:T(8,128)(2,1)}), bf16[256,1024]{1,0:T(8,128)(2,1)}) %reduce-scatter.14.cloned.1.call-update) | async-done | bytes 524304 | tf_op jit(solution)/shard_map/reduce_scatter | solution.py:350
  862.4 48.1 %reduce-scatter.12.cloned.1.call-done = bf16[256,1024]{1,0:T(8,128)(2,1)} async-done(((bf16[2048,1024]{1,0:T(8,128)(2,1)}), bf16[256,1024]{1,0:T(8,128)(2,1)}) %reduce-scatter.12.cloned.1.call-update) | async-done | bytes 524304 | tf_op jit(solution)/shard_map/reduce_scatter | solution.py:351
  (204 shorter events, 90.1 us)
Async XLA Ops:
  7.2 161.9 %all-gather.5.cloned.1.call-start = ((), (), s32[]{:S(2)}) async-start(), calls=%async_computation.5 | async-start | bytes 14155776 | tf_op jit(solution)/shard_map/all_gather | solution.py:285
  13.1 13.3 %collective-permute-start.3 = (bf16[64,3200]{1,0:T(8,128)(2,1)S(1)}, bf16[64,3200]{1,0:T(8,128)(2,1)S(1)}, u32[]{:S(2)}, u32[]{:S(2)}) collective-permute-start(bf16[64,3200]{1,0:T(8,128)(2,1)S(1)} %get-tuple-element.151), channel_id=1, source_target_pairs={{0,1},{1,0},{2,3},{3,2},{4,5},{5,4},{6,7},{7,6},{8,9},{9,8},{10,11... | collective-permute-start | bytes 1228808 | tf_op jit(solution)/shard_map/ppermute | solution.py:244
  16.1 19.7 %collective-permute-start.4 = (bf16[64,3200]{1,0:T(8,128)(2,1)S(1)}, bf16[64,3200]{1,0:T(8,128)(2,1)S(1)}, u32[]{:S(2)}, u32[]{:S(2)}) collective-permute-start(bf16[64,3200]{1,0:T(8,128)(2,1)S(1)} %get-tuple-element.152), channel_id=1, source_target_pairs={{0,2},{1,3},{2,0},{3,1},{4,6},{5,7},{6,4},{7,5},{8,10},{9,11},{10,... | collective-permute-start | bytes 1228808 | tf_op jit(solution)/shard_map/ppermute | solution.py:244
  17.6 18.2 %collective-permute-start.5 = (bf16[64,3200]{1,0:T(8,128)(2,1)S(1)}, bf16[64,3200]{1,0:T(8,128)(2,1)S(1)}, u32[]{:S(2)}, u32[]{:S(2)}) collective-permute-start(bf16[64,3200]{1,0:T(8,128)(2,1)S(1)} %get-tuple-element.153), channel_id=1, source_target_pairs={{0,3},{1,2},{2,1},{3,0},{4,7},{5,6},{6,5},{7,4},{8,11},{9,10},{10,... | collective-permute-start | bytes 1228808 | tf_op jit(solution)/shard_map/ppermute | solution.py:244
  38.7 178.8 %all-gather.7.cloned.1.call-start = ((), (), s32[]{:S(2)}) async-start(), calls=%async_computation.6 | async-start | bytes 4718592 | tf_op jit(solution)/shard_map/all_gather | solution.py:288
  38.8 0.7 collective-permute-start.6
  40.3 264.0 %all-gather.9.cloned.1.call-start = ((), (), s32[]{:S(2)}) async-start(), calls=%async_computation.7 | async-start | bytes 4718592 | tf_op jit(solution)/shard_map/all_gather | solution.py:291
  41.0 328.1 %all-gather.11.cloned.1.call-start = ((), (), s32[]{:S(2)}) async-start(), calls=%async_computation.8 | async-start | bytes 4718592 | tf_op jit(solution)/shard_map/all_gather | solution.py:292
  41.1 74.3 %collective-permute-start = (bf16[256,2048]{1,0:T(8,128)(2,1)S(1)}, bf16[256,2048]{1,0:T(8,128)(2,1)}, u32[]{:S(2)}, u32[]{:S(2)}) collective-permute-start(bf16[256,2048]{1,0:T(8,128)(2,1)S(1)} %copy-done.7), channel_id=1, source_target_pairs={{0,1},{1,0},{2,3},{3,2},{4,5},{5,4},{6,7},{7,6},{8,9},{9,8},{10,11... | collective-permute-start | bytes 3145736 | tf_op jit(solution)/shard_map/ppermute | solution.py:244
  86.7 45.5 %collective-permute-start.1 = (bf16[256,2048]{1,0:T(8,128)(2,1)S(1)}, bf16[256,2048]{1,0:T(8,128)(2,1)}, u32[]{:S(2)}, u32[]{:S(2)}) collective-permute-start(bf16[256,2048]{1,0:T(8,128)(2,1)S(1)} %copy-done.7), channel_id=1, source_target_pairs={{0,2},{1,3},{2,0},{3,1},{4,6},{5,7},{6,4},{7,5},{8,10},{9,11},{10,... | collective-permute-start | bytes 3145736 | tf_op jit(solution)/shard_map/ppermute | solution.py:244
  86.7 45.5 %collective-permute-start.2 = (bf16[256,2048]{1,0:T(8,128)(2,1)S(1)}, bf16[256,2048]{1,0:T(8,128)(2,1)}, u32[]{:S(2)}, u32[]{:S(2)}) collective-permute-start(bf16[256,2048]{1,0:T(8,128)(2,1)S(1)} %copy-done.7), channel_id=1, source_target_pairs={{0,3},{1,2},{2,1},{3,0},{4,7},{5,6},{6,5},{7,4},{8,11},{9,10},{10,... | collective-permute-start | bytes 3145736 | tf_op jit(solution)/shard_map/ppermute | solution.py:244
  88.2 592.9 %reduce-scatter.10.cloned.1.call-start = ((), (), s32[]{:S(2)}) async-start(), calls=%async_computation.10 | async-start | bytes 4718592 | tf_op jit(solution)/shard_map/reduce_scatter | solution.py:353
  221.3 26.1 %collective-permute-start.7 = (bf16[256,2048]{1,0:T(8,128)(2,1)S(1)}, bf16[256,2048]{1,0:T(8,128)(2,1)S(1)}, u32[]{:S(2)}, u32[]{:S(2)}) collective-permute-start(bf16[256,2048]{1,0:T(8,128)(2,1)S(1)} %convolution_convert_fusion.12), channel_id=1, source_target_pairs={{0,1},{1,0},{2,3},{3,2},{4,5},{5,4},{6,7},{7,6},{8,9},{9,8},{10,11... | collective-permute-start | bytes 3145736 | tf_op jit(solution)/shard_map/ppermute | solution.py:244
  224.1 47.6 %collective-permute-start.8 = (bf16[256,2048]{1,0:T(8,128)(2,1)S(1)}, bf16[256,2048]{1,0:T(8,128)(2,1)S(1)}, u32[]{:S(2)}, u32[]{:S(2)}) collective-permute-start(bf16[256,2048]{1,0:T(8,128)(2,1)S(1)} %convolution_convert_fusion.11), channel_id=1, source_target_pairs={{0,2},{1,3},{2,0},{3,1},{4,6},{5,7},{6,4},{7,5},{8,10},{9,11},{10,... | collective-permute-start | bytes 3145736 | tf_op jit(solution)/shard_map/ppermute | solution.py:244
  226.9 44.8 %collective-permute-start.9 = (bf16[256,2048]{1,0:T(8,128)(2,1)S(1)}, bf16[256,2048]{1,0:T(8,128)(2,1)S(1)}, u32[]{:S(2)}, u32[]{:S(2)}) collective-permute-start(bf16[256,2048]{1,0:T(8,128)(2,1)S(1)} %convolution_convert_fusion.10), channel_id=1, source_target_pairs={{0,3},{1,2},{2,1},{3,0},{4,7},{5,6},{6,5},{7,4},{8,11},{9,10},{10,... | collective-permute-start | bytes 3145736 | tf_op jit(solution)/shard_map/ppermute | solution.py:244
  276.4 26.4 %collective-permute-start.10 = (bf16[256,2048]{1,0:T(8,128)(2,1)}, bf16[256,2048]{1,0:T(8,128)(2,1)}, u32[]{:S(2)}, u32[]{:S(2)}) collective-permute-start(bf16[256,2048]{1,0:T(8,128)(2,1)} %add_convert_fusion.1), channel_id=1, source_target_pairs={{0,1},{1,0},{2,3},{3,2},{4,5},{5,4},{6,7},{7,6},{8,9},{9,8},{10,11... | collective-permute-start | bytes 3145736 | tf_op jit(solution)/shard_map/ppermute | solution.py:244
  277.0 48.6 %collective-permute-start.11 = (bf16[256,2048]{1,0:T(8,128)(2,1)}, bf16[256,2048]{1,0:T(8,128)(2,1)}, u32[]{:S(2)}, u32[]{:S(2)}) collective-permute-start(bf16[256,2048]{1,0:T(8,128)(2,1)} %add_convert_fusion.1), channel_id=1, source_target_pairs={{0,2},{1,3},{2,0},{3,1},{4,6},{5,7},{6,4},{7,5},{8,10},{9,11},{10,... | collective-permute-start | bytes 3145736 | tf_op jit(solution)/shard_map/ppermute | solution.py:244
  278.5 47.7 %collective-permute-start.12 = (bf16[256,2048]{1,0:T(8,128)(2,1)}, bf16[256,2048]{1,0:T(8,128)(2,1)}, u32[]{:S(2)}, u32[]{:S(2)}) collective-permute-start(bf16[256,2048]{1,0:T(8,128)(2,1)} %add_convert_fusion.1), channel_id=1, source_target_pairs={{0,3},{1,2},{2,1},{3,0},{4,7},{5,6},{6,5},{7,4},{8,11},{9,10},{10,... | collective-permute-start | bytes 3145736 | tf_op jit(solution)/shard_map/ppermute | solution.py:244
  279.8 67.9 %collective-permute-start.16 = (bf16[256,2048]{1,0:T(8,128)(2,1)}, bf16[256,2048]{1,0:T(8,128)(2,1)}, u32[]{:S(2)}, u32[]{:S(2)}) collective-permute-start(bf16[256,2048]{1,0:T(8,128)(2,1)} %param.15), channel_id=1, source_target_pairs={{0,1},{1,0},{2,3},{3,2},{4,5},{5,4},{6,7},{7,6},{8,9},{9,8},{10,11... | collective-permute-start | bytes 3145736 | tf_op jit(solution)/shard_map/ppermute | solution.py:244
  280.5 87.3 %collective-permute-start.17 = (bf16[256,2048]{1,0:T(8,128)(2,1)}, bf16[256,2048]{1,0:T(8,128)(2,1)}, u32[]{:S(2)}, u32[]{:S(2)}) collective-permute-start(bf16[256,2048]{1,0:T(8,128)(2,1)} %param.15), channel_id=1, source_target_pairs={{0,2},{1,3},{2,0},{3,1},{4,6},{5,7},{6,4},{7,5},{8,10},{9,11},{10,... | collective-permute-start | bytes 3145736 | tf_op jit(solution)/shard_map/ppermute | solution.py:244
  302.8 66.4 %collective-permute-start.18 = (bf16[256,2048]{1,0:T(8,128)(2,1)}, bf16[256,2048]{1,0:T(8,128)(2,1)}, u32[]{:S(2)}, u32[]{:S(2)}) collective-permute-start(bf16[256,2048]{1,0:T(8,128)(2,1)} %param.15), channel_id=1, source_target_pairs={{0,3},{1,2},{2,1},{3,0},{4,7},{5,6},{6,5},{7,4},{8,11},{9,10},{10,... | collective-permute-start | bytes 3145736 | tf_op jit(solution)/shard_map/ppermute | solution.py:244
  381.4 49.1 %copy-start.27 = (bf16[1024,1024]{1,0:T(8,128)(2,1)}, bf16[1024,1024]{1,0:T(8,128)(2,1)S(1)}, u32[]{:S(2)}) copy-start(bf16[1024,1024]{1,0:T(8,128)(2,1)S(1)} %fusion.12) | copy-start | bytes 6291460
  382.8 26.2 %collective-permute-start.19 = (bf16[256,2048]{1,0:T(8,128)(2,1)S(1)}, bf16[256,2048]{1,0:T(8,128)(2,1)S(1)}, u32[]{:S(2)}, u32[]{:S(2)}) collective-permute-start(bf16[256,2048]{1,0:T(8,128)(2,1)S(1)} %convolution_convert_fusion.6), channel_id=1, source_target_pairs={{0,1},{1,0},{2,3},{3,2},{4,5},{5,4},{6,7},{7,6},{8,9},{9,8},{10,11... | collective-permute-start | bytes 3145736 | tf_op jit(solution)/shard_map/ppermute | solution.py:244
  384.9 45.7 %copy-start.5 = (f32[256,2048]{1,0:T(8,128)S(1)}, f32[256,2048]{1,0:T(8,128)}, u32[]{:S(2)}) copy-start(f32[256,2048]{1,0:T(8,128)} %copy-done.4) | copy-start | bytes 6291460
  384.9 45.6 %collective-permute-start.20 = (bf16[256,2048]{1,0:T(8,128)(2,1)S(1)}, bf16[256,2048]{1,0:T(8,128)(2,1)S(1)}, u32[]{:S(2)}, u32[]{:S(2)}) collective-permute-start(bf16[256,2048]{1,0:T(8,128)(2,1)S(1)} %convolution_convert_fusion.5), channel_id=1, source_target_pairs={{0,2},{1,3},{2,0},{3,1},{4,6},{5,7},{6,4},{7,5},{8,10},{9,11},{10,... | collective-permute-start | bytes 3145736 | tf_op jit(solution)/shard_map/ppermute | solution.py:244
  387.7 42.8 %collective-permute-start.21 = (bf16[256,2048]{1,0:T(8,128)(2,1)S(1)}, bf16[256,2048]{1,0:T(8,128)(2,1)S(1)}, u32[]{:S(2)}, u32[]{:S(2)}) collective-permute-start(bf16[256,2048]{1,0:T(8,128)(2,1)S(1)} %convolution_convert_fusion.4), channel_id=1, source_target_pairs={{0,3},{1,2},{2,1},{3,0},{4,7},{5,6},{6,5},{7,4},{8,11},{9,10},{10,... | collective-permute-start | bytes 3145736 | tf_op jit(solution)/shard_map/ppermute | solution.py:244
  433.0 48.4 %copy-start.3 = (bf16[1024,1024]{1,0:T(8,128)(2,1)S(1)}, bf16[1024,1024]{1,0:T(8,128)(2,1)}, u32[]{:S(2)}) copy-start(bf16[1024,1024]{1,0:T(8,128)(2,1)} %copy-done.1) | copy-start | bytes 6291460
  436.7 43.6 %copy-start.16 = (bf16[256,2048]{1,0:T(8,128)(2,1)}, bf16[256,2048]{1,0:T(8,128)(2,1)S(1)}, u32[]{:S(2)}) copy-start(bf16[256,2048]{1,0:T(8,128)(2,1)S(1)} %get-tuple-element.94) | copy-start | bytes 3145732
  436.7 26.1 %collective-permute-start.22 = (bf16[256,2048]{1,0:T(8,128)(2,1)S(1)}, bf16[256,2048]{1,0:T(8,128)(2,1)S(1)}, u32[]{:S(2)}, u32[]{:S(2)}) collective-permute-start(bf16[256,2048]{1,0:T(8,128)(2,1)S(1)} %get-tuple-element.94), channel_id=1, source_target_pairs={{0,1},{1,0},{2,3},{3,2},{4,5},{5,4},{6,7},{7,6},{8,9},{9,8},{10,11... | collective-permute-start | bytes 3145736 | tf_op jit(solution)/shard_map/ppermute | solution.py:244
  437.8 41.5 %collective-permute-start.23 = (bf16[256,2048]{1,0:T(8,128)(2,1)S(1)}, bf16[256,2048]{1,0:T(8,128)(2,1)S(1)}, u32[]{:S(2)}, u32[]{:S(2)}) collective-permute-start(bf16[256,2048]{1,0:T(8,128)(2,1)S(1)} %get-tuple-element.94), channel_id=1, source_target_pairs={{0,2},{1,3},{2,0},{3,1},{4,6},{5,7},{6,4},{7,5},{8,10},{9,11},{10,... | collective-permute-start | bytes 3145736 | tf_op jit(solution)/shard_map/ppermute | solution.py:244
  438.4 42.0 %collective-permute-start.24 = (bf16[256,2048]{1,0:T(8,128)(2,1)S(1)}, bf16[256,2048]{1,0:T(8,128)(2,1)S(1)}, u32[]{:S(2)}, u32[]{:S(2)}) collective-permute-start(bf16[256,2048]{1,0:T(8,128)(2,1)S(1)} %get-tuple-element.94), channel_id=1, source_target_pairs={{0,3},{1,2},{2,1},{3,0},{4,7},{5,6},{6,5},{7,4},{8,11},{9,10},{10,... | collective-permute-start | bytes 3145736 | tf_op jit(solution)/shard_map/ppermute | solution.py:244
  488.0 194.8 %reduce-scatter.8.cloned.1.call-start = ((), (), s32[]{:S(2)}) async-start(), calls=%async_computation.9 | async-start | bytes 14155776 | tf_op jit(solution)/shard_map/reduce_scatter | solution.py:354
  533.4 274.8 %reduce-scatter.16.cloned.1.call-start = ((), (), s32[]{:S(2)}) async-start(), calls=%async_computation.13 | async-start | bytes 1081344
  542.4 24.6 %collective-permute-start.25 = (bf16[256,2048]{1,0:T(8,128)(2,1)S(1)}, bf16[256,2048]{1,0:T(8,128)(2,1)S(1)}, u32[]{:S(2)}, u32[]{:S(2)}) collective-permute-start(bf16[256,2048]{1,0:T(8,128)(2,1)S(1)} %convolution_convert_fusion.15), channel_id=1, source_target_pairs={{0,1},{1,0},{2,3},{3,2},{4,5},{5,4},{6,7},{7,6},{8,9},{9,8},{10,11... | collective-permute-start | bytes 3145736 | tf_op jit(solution)/shard_map/ppermute | solution.py:244
  552.7 41.9 %collective-permute-start.26 = (bf16[256,2048]{1,0:T(8,128)(2,1)S(1)}, bf16[256,2048]{1,0:T(8,128)(2,1)S(1)}, u32[]{:S(2)}, u32[]{:S(2)}) collective-permute-start(bf16[256,2048]{1,0:T(8,128)(2,1)S(1)} %convolution_convert_fusion.14), channel_id=1, source_target_pairs={{0,2},{1,3},{2,0},{3,1},{4,6},{5,7},{6,4},{7,5},{8,10},{9,11},{10,... | collective-permute-start | bytes 3145736 | tf_op jit(solution)/shard_map/ppermute | solution.py:244
  562.7 32.9 %collective-permute-start.27 = (bf16[256,2048]{1,0:T(8,128)(2,1)}, bf16[256,2048]{1,0:T(8,128)(2,1)}, u32[]{:S(2)}, u32[]{:S(2)}) collective-permute-start(bf16[256,2048]{1,0:T(8,128)(2,1)} %convolution_convert_fusion.13), channel_id=1, source_target_pairs={{0,3},{1,2},{2,1},{3,0},{4,7},{5,6},{6,5},{7,4},{8,11},{9,10},{10,... | collective-permute-start | bytes 3145736 | tf_op jit(solution)/shard_map/ppermute | solution.py:244
  608.2 251.7 %reduce-scatter.14.cloned.1.call-start = ((), (), s32[]{:S(2)}) async-start(), calls=%async_computation.12 | async-start | bytes 4718592 | tf_op jit(solution)/shard_map/reduce_scatter | solution.py:350
  617.8 292.7 %reduce-scatter.12.cloned.1.call-start = ((), (), s32[]{:S(2)}) async-start(), calls=%async_computation.11 | async-start | bytes 4718592 | tf_op jit(solution)/shard_map/reduce_scatter | solution.py:351
  633.5 26.2 %collective-permute-start.13 = (bf16[256,2048]{1,0:T(8,128)(2,1)S(1)}, bf16[256,2048]{1,0:T(8,128)(2,1)S(1)}, u32[]{:S(2)}, u32[]{:S(2)}) collective-permute-start(bf16[256,2048]{1,0:T(8,128)(2,1)S(1)} %convolution_convert_fusion.9), channel_id=1, source_target_pairs={{0,1},{1,0},{2,3},{3,2},{4,5},{5,4},{6,7},{7,6},{8,9},{9,8},{10,11... | collective-permute-start | bytes 3145736 | tf_op jit(solution)/shard_map/ppermute | solution.py:244
  636.0 40.6 %copy-start.6 = (f32[256,2048]{1,0:T(8,128)S(1)}, f32[256,2048]{1,0:T(8,128)}, u32[]{:S(2)}) copy-start(f32[256,2048]{1,0:T(8,128)} %copy-done.4) | copy-start | bytes 6291460
  636.0 40.6 %collective-permute-start.14 = (bf16[256,2048]{1,0:T(8,128)(2,1)S(1)}, bf16[256,2048]{1,0:T(8,128)(2,1)S(1)}, u32[]{:S(2)}, u32[]{:S(2)}) collective-permute-start(bf16[256,2048]{1,0:T(8,128)(2,1)S(1)} %convolution_convert_fusion.8), channel_id=1, source_target_pairs={{0,2},{1,3},{2,0},{3,1},{4,6},{5,7},{6,4},{7,5},{8,10},{9,11},{10,... | collective-permute-start | bytes 3145736 | tf_op jit(solution)/shard_map/ppermute | solution.py:244
  637.7 41.6 %copy-start.9 = (f32[256,2048]{1,0:T(8,128)S(1)}, f32[256,2048]{1,0:T(8,128)}, u32[]{:S(2)}) copy-start(f32[256,2048]{1,0:T(8,128)} %get-tuple-element.95) | copy-start | bytes 6291460
  637.7 41.6 %copy-start.15 = (f32[256,2048]{1,0:T(8,128)S(1)}, f32[256,2048]{1,0:T(8,128)}, u32[]{:S(2)}) copy-start(f32[256,2048]{1,0:T(8,128)} %get-tuple-element.163) | copy-start | bytes 6291460
  637.7 38.9 %collective-permute-start.15 = (bf16[256,2048]{1,0:T(8,128)(2,1)S(1)}, bf16[256,2048]{1,0:T(8,128)(2,1)S(1)}, u32[]{:S(2)}, u32[]{:S(2)}) collective-permute-start(bf16[256,2048]{1,0:T(8,128)(2,1)S(1)} %convolution_convert_fusion.7), channel_id=1, source_target_pairs={{0,3},{1,2},{2,1},{3,0},{4,7},{5,6},{6,5},{7,4},{8,11},{9,10},{10,... | collective-permute-start | bytes 3145736 | tf_op jit(solution)/shard_map/ppermute | solution.py:244
  681.1 231.5 %collective-permute-start.31 = (bf16[128,2048]{1,0:T(8,128)(2,1)}, bf16[128,2048]{1,0:T(8,128)(2,1)S(1)}, u32[]{:S(2)}, u32[]{:S(2)}) collective-permute-start(bf16[128,2048]{1,0:T(8,128)(2,1)} %reduce-scatter.10.cloned.1.call-done), channel_id=1, source_target_pairs={{0,0},{4,1},{8,2},{12,3},{16,4},{20,5},{24,6},{28,7},{1,8},{5,9},{... | collective-permute-start | bytes 1572872 | tf_op jit(solution)/shard_map/ppermute | solution.py:353
  685.5 228.2 %collective-permute-start.28 = (bf16[64,3072]{1,0:T(8,128)(2,1)}, bf16[64,3072]{1,0:T(8,128)(2,1)S(1)}, u32[]{:S(2)}, u32[]{:S(2)}) collective-permute-start(bf16[64,3072]{1,0:T(8,128)(2,1)} %get-tuple-element.109), channel_id=1, source_target_pairs={{0,1},{1,0},{2,3},{3,2},{4,5},{5,4},{6,7},{7,6},{8,9},{9,8},{10,11... | collective-permute-start | bytes 1179656 | tf_op jit(solution)/shard_map/ppermute | solution.py:244
  687.3 226.4 %collective-permute-start.29 = (bf16[64,3072]{1,0:T(8,128)(2,1)}, bf16[64,3072]{1,0:T(8,128)(2,1)S(1)}, u32[]{:S(2)}, u32[]{:S(2)}) collective-permute-start(bf16[64,3072]{1,0:T(8,128)(2,1)} %get-tuple-element.108), channel_id=1, source_target_pairs={{0,2},{1,3},{2,0},{3,1},{4,6},{5,7},{6,4},{7,5},{8,10},{9,11},{10,... | collective-permute-start | bytes 1179656 | tf_op jit(solution)/shard_map/ppermute | solution.py:244
  689.9 223.8 %collective-permute-start.30 = (bf16[64,3072]{1,0:T(8,128)(2,1)S(1)}, bf16[64,3072]{1,0:T(8,128)(2,1)S(1)}, u32[]{:S(2)}, u32[]{:S(2)}) collective-permute-start(bf16[64,3072]{1,0:T(8,128)(2,1)S(1)} %get-tuple-element.107), channel_id=1, source_target_pairs={{0,3},{1,2},{2,1},{3,0},{4,7},{5,6},{6,5},{7,4},{8,11},{9,10},{10,... | collective-permute-start | bytes 1179656 | tf_op jit(solution)/shard_map/ppermute | solution.py:244
  (24 other events, 155.8 us)
Sparse Core Ops, SparseCore 0:
  38.8 130.1 all-gather.4
  171.2 46.2 all-gather.6
  219.1 45.8 all-gather.8
  266.5 46.5 all-gather.10
  488.1 49.0 reduce-scatter.9
  539.4 127.3 reduce-scatter.7
  669.7 138.4 reduce-scatter.15
  810.6 49.2 reduce-scatter.13
  862.3 48.1 reduce-scatter.11

commit v2 on v1

--- a/solution.py
+++ b/solution.py
@@ -212,6 +212,128 @@
     )(order, block_decay, pre, *tables, inner, place_decay, key_decay, *extra)
 
 
+def product_kernel(contract, a_ref, b_ref, *out_refs):
+    result = lax.dot_general(
+        a_ref[...], b_ref[...], (contract, ((), ())), preferred_element_type=F32
+    )
+    step = result.shape[0] // len(out_refs)
+    for n, out_ref in enumerate(out_refs):
+        out_ref[...] = result[n * step : (n + 1) * step].astype(BF16)
+
+
+def row_product(a, b, transposed, parts, column=0):
+    rows, depth = a.shape
+    width = b.shape[0] if transposed else b.shape[1]
+    tile = min(512, width)
+    if transposed:
+        b_spec = pl.BlockSpec((tile, depth), lambda n: (n, column))
+    else:
+        b_spec = pl.BlockSpec((depth, tile), lambda n: (0, n))
+    return pl.pallas_call(
+        functools.partial(product_kernel, ((1,), (1 if transposed else 0,))),
+        grid=(width // tile,),
+        in_specs=[pl.BlockSpec((rows, depth), lambda n: (0, 0)), b_spec],
+        out_specs=[pl.BlockSpec((rows // parts, tile), lambda n: (0, n))] * parts,
+        out_shape=[jax.ShapeDtypeStruct((rows // parts, width), BF16)] * parts,
+        compiler_params=pltpu.CompilerParams(vmem_limit_bytes=48 * 1024 * 1024),
+        cost_estimate=pl.CostEstimate(
+            flops=2 * rows * depth * width,
+            bytes_accessed=2 * (rows * depth + depth * width + rows * width),
+            transcendentals=0,
+        ),
+        name="row_product",
+    )(a, b)
+
+
+def feed_kernel(
+    steps, normed_ref, grad_ref, up_ref, down_ref, up_row_ref, hidden_ref, pre_ref, *out_refs
+):
+    step = pl.program_id(0)
+
+    @pl.when(step < steps)
+    def _():
+        u = dot(normed_ref[...], up_ref[...])
+        d_hidden = dot(grad_ref[...], down_ref[...])
+        scale = 0.7978845608028654
+        square = u * u
+        t = jnp.tanh(scale * u * (1.0 + 0.044715 * square))
+        half = 0.5 * (1.0 + t)
+        hidden_ref[...] = (u * half).astype(BF16)
+        slope = half + 0.5 * scale * u * (1.0 - t * t) * (1.0 + 3 * 0.044715 * square)
+        tile = u.shape[1]
+        pre_ref[:, pl.ds(pl.multiple_of(step * tile, tile), tile)] = (d_hidden * slope).astype(BF16)
+
+    @pl.when(step >= steps)
+    def _():
+        result = contract_cols(pre_ref[...], up_row_ref[...])
+        count = result.shape[0] // len(out_refs)
+        for n, out_ref in enumerate(out_refs):
+            out_ref[...] = result[n * count : (n + 1) * count].astype(BF16)
+
+
+def feed_call(normed, grad, both, parts):
+    rows, depth = normed.shape
+    width = both.shape[1] // 2
+    tile, out_tile = min(256, width), min(512, depth)
+    steps, out_steps = width // tile, depth // out_tile
+    first = lambda n: jnp.minimum(n, steps - 1)
+    second = lambda n: jnp.maximum(n - steps, 0)
+    whole = pl.BlockSpec((rows, depth), lambda n: (0, 0))
+    return pl.pallas_call(
+        functools.partial(feed_kernel, steps),
+        grid=(steps + out_steps,),
+        in_specs=[
+            whole,
+            whole,
+            pl.BlockSpec((depth, tile), lambda n: (0, first(n))),
+            pl.BlockSpec((depth, tile), lambda n: (0, steps + first(n))),
+            pl.BlockSpec((out_tile, width), lambda n: (second(n), 0)),
+        ],
+        out_specs=[
+            pl.BlockSpec((rows, tile), lambda n: (0, first(n))),
+            pl.BlockSpec((rows, width), lambda n: (0, 0)),
+        ]
+        + [pl.BlockSpec((rows // parts, out_tile), lambda n: (0, second(n)))] * parts,
+        out_shape=[jax.ShapeDtypeStruct((rows, width), BF16)] * 2
+        + [jax.ShapeDtypeStruct((rows // parts, depth), BF16)] * parts,
+        compiler_params=pltpu.CompilerParams(vmem_limit_bytes=56 * 1024 * 1024),
+        cost_estimate=pl.CostEstimate(
+            flops=6 * rows * depth * width,
+            bytes_accessed=4 * (rows * depth + depth * width + rows * width),
+            transcendentals=rows * width,
+        ),
+        name="feed_forward",
+    )(normed, grad, both, both, both)
+
+
+def feed_grads_kernel(normed_ref, grad_ref, hidden_ref, pre_ref, out_ref):
+    width = hidden_ref.shape[1]
+    out_ref[:, :width] = contract_rows(normed_ref[...], pre_ref[...]).astype(BF16)
+    out_ref[:, width:] = contract_rows(grad_ref[...], hidden_ref[...]).astype(BF16)
+
+
+def feed_grads(normed, grad, hidden, d_pre):
+    rows, depth = normed.shape
+    width = hidden.shape[1]
+    tile = min(512, depth)
+    slab = pl.BlockSpec((rows, tile), lambda n: (0, n))
+    whole = pl.BlockSpec((rows, width), lambda n: (0, 0))
+    return pl.pallas_call(
+        feed_grads_kernel,
+        grid=(depth // tile,),
+        in_specs=[slab, slab, whole, whole],
+        out_specs=pl.BlockSpec((tile, 2 * width), lambda n: (n, 0)),
+        out_shape=jax.ShapeDtypeStruct((depth, 2 * width), BF16),
+        compiler_params=pltpu.CompilerParams(vmem_limit_bytes=48 * 1024 * 1024),
+        cost_estimate=pl.CostEstimate(
+            flops=4 * rows * depth * width,
+            bytes_accessed=4 * (rows * depth + depth * width + rows * width),
+            transcendentals=0,
+        ),
+        name="feed_grads",
+    )(normed, grad, hidden, d_pre)
+
+
 def on_device(
     tokens,
     cotangent,
@@ -237,6 +359,9 @@
     heads = HEADS // mp
     part = query_weight.shape[0]
     own = part * mp
+    square = mp == 4
+    parts = 2 * mp if square else mp
+    together = lax.optimization_barrier
 
     def swap(x, mask):
         if mask == 0:
@@ -244,11 +369,80 @@
         return lax.ppermute(x, "mp", [(s, s ^ mask) for s in range(mp)])
 
     def spread(x):
-        return [swap(x, m) for m in masks]
-
-    def collect(pieces):
-        received = [swap(pieces[m].astype(BF16), m).astype(F32) for m in masks[1:]]
-        return functools.reduce(jnp.add, received, pieces[0].astype(F32))
+        if not square:
+            return jnp.concatenate([swap(x, m) for m in masks], axis=0)
+        half = x.shape[0] // 2
+        a, b = x[:half], x[half:]
+        a1, b2 = swap(a, 1), swap(b, 2)
+        a2, b1 = swap(a, 2), swap(b, 1)
+        a3, b3 = swap(a1, 2), swap(b2, 1)
+        return jnp.concatenate([a, b, a1, b1, a2, b2, a3, b3], axis=0)
+
+    def collect(pieces, meanwhile=()):
+        if not square:
+            received = [swap(pieces[m], m) for m in masks[1:]]
+            *received, meanwhile = together((*received, meanwhile))
+            received = [r.astype(F32) for r in received]
+            return functools.reduce(jnp.add, received, pieces[0].astype(F32)), meanwhile
+        a0, b0, a1, b1, a2, b2, a3, b3 = pieces
+        a3, b3 = swap(a3, 1), swap(b3, 2)
+        a1, b2 = swap(a1, 1), swap(b2, 2)
+        a3, b3, meanwhile = together((a3, b3, meanwhile))
+        a2 = swap((a2.astype(F32) + a3.astype(F32)).astype(BF16), 2)
+        b1 = swap((b1.astype(F32) + b3.astype(F32)).astype(BF16), 1)
+        total = jnp.concatenate(
+            [
+                a0.astype(F32) + a1.astype(F32) + a2.astype(F32),
+                b0.astype(F32) + b1.astype(F32) + b2.astype(F32),
+            ],
+            axis=0,
+        )
+        return total, meanwhile
+
+    def shuffle(x, back=False):
+        flat = [(b, (b % dp) * mp + b // dp) for b in range(dp * mp)]
+        if not (dp == 8 and square):
+            pairs = [(d, s) for s, d in flat] if back else flat
+            return lambda late: lax.ppermute(x, ("dp", "mp"), pairs)
+        first, second = ([], []), ([], [])
+        for z in range(4):
+            for c in range(2):
+                for j in range(4):
+                    plane = 2 * c + j // 2
+                    start, middle = (2 * z + c) * 4 + j, (2 * plane + z % 2) * 4 + j
+                    first[z // 2].append((start, middle))
+                    second[z // 2].append((middle, (2 * plane + j % 2) * 4 + z))
+        flipped = lambda pairs: [(d, s) for s, d in pairs]
+        move = lambda v, pairs: lax.ppermute(v, ("dp", "mp"), pairs)
+        if not back:
+            low, high = (move(x, pairs) for pairs in first)
+
+            def finish(late):
+                a, b, late = together((low, high, late))
+                return jnp.where(here < 2, move(a, second[0]), move(b, second[1]))
+
+            return finish
+        low, high = (move(x, flipped(pairs)) for pairs in second)
+        upper = lax.axis_index("dp") >= 4
+
+        def finish_back(late):
+            a, b, late = together((low, high, late))
+            return jnp.where(upper, move(b, flipped(first[1])), move(a, flipped(first[0])))
+
+        return finish_back
+
+    def scatter_small(x):
+        cur = x.reshape(dp, mp, x.shape[-1])
+        for dim, name in ((1, "mp"), (0, "dp")):
+            index = lax.axis_index(name)
+            while cur.shape[dim] > 1:
+                count = cur.shape[dim] // 2
+                bit = (index // count) % 2
+                mine = lax.dynamic_slice_in_dim(cur, bit * count, count, dim)
+                other = lax.dynamic_slice_in_dim(cur, (1 - bit) * count, count, dim)
+                pairs = [(s, s ^ count) for s in range(lax.axis_size(name))]
+                cur = mine + lax.ppermute(other, name, pairs)
+        return cur.reshape(-1)
 
     def by_index(pieces):
         stacked = jnp.stack(pieces)
@@ -256,12 +450,11 @@
             lax.dynamic_index_in_dim(stacked, here ^ m, 0, keepdims=False) for m in masks
         ]
 
-    thin = jnp.stack(
+    thin = jnp.concatenate(
         [retention_gain, retention_bias, feedfwd_gain, feedfwd_bias]
-        + [jnp.broadcast_to(domain.astype(BF16), (part,))],
-        axis=1,
-    )
-    thin = jnp.pad(thin, ((0, 0), (0, 128 - thin.shape[1])))
+        + [jnp.broadcast_to(domain.astype(BF16), (part,))]
+    )
+    thin = lax.all_gather(thin[None], "dp", axis=0, tiled=True)
 
     def columns(weight, target):
         width = weight.shape[1] // mp
@@ -272,29 +465,24 @@
         target = here ^ m
         pieces.append(
             jnp.concatenate(
-                [columns(w, target) for w in (query_weight, key_weight, value_weight, gate_weight)]
-                + [thin],
+                [columns(w, target) for w in (query_weight, key_weight, value_weight, gate_weight)],
                 axis=1,
             )
         )
-    pieces = by_index([swap(pieces[m], m) for m in masks])
-    packed = jnp.concatenate(pieces, axis=0)
-    wide = packed.shape[1] - 128
-    thin_all = lax.all_gather(packed[:, wide : wide + 8], "dp", axis=0, tiled=True)
-    gain_one, bias_one, gain_two, bias_two = (thin_all[:, n].astype(F32)[None] for n in range(4))
-    w_in = lax.all_gather(packed[:, :wide], "dp", axis=0, tiled=True)
-
-    shuffle = [(b, (b % dp) * mp + b // dp) for b in range(dp * mp)]
-    w_out = lax.all_gather(
-        lax.ppermute(output_weight, ("dp", "mp"), shuffle), "dp", axis=0, tiled=True
-    )
-    w_up = lax.all_gather(up_weight, "dp", axis=0, tiled=True)
-    w_down = lax.all_gather(down_weight.T, "dp", axis=0, tiled=True)
-
-    source_rows = jnp.concatenate(spread(tokens), axis=0)
-    cotan_rows = jnp.concatenate(spread(cotangent), axis=0)
-
-    domains = thin_all[::own, 4]
+    *pieces, thin = together((*(swap(pieces[m], m) for m in masks), thin))
+    packed = jnp.concatenate(by_index(pieces), axis=0)
+    w_in = lax.all_gather(packed, "dp", axis=0, tiled=True)
+
+    finish = shuffle(output_weight)
+    tokens_late, cotangent_late, packed = together((tokens, cotangent, packed))
+    thin = jnp.stack(by_index([swap(thin, m) for m in masks]))
+    source_rows = spread(tokens_late)
+    cotan_rows = spread(cotangent_late)
+    shuffled = finish(packed)
+    thin = thin.reshape(mp, dp, 5, part).transpose(2, 1, 0, 3).reshape(5, dp * own)
+    gain_one, bias_one, gain_two, bias_two = (thin[n].astype(F32)[None] for n in range(4))
+
+    domains = thin[4, ::own]
     own_count = jnp.sum((domains == domain[0].astype(BF16)).astype(F32)) * (rows * mp)
     row_scale = F32(rows * dp * mp) / (DOMAINS * own_count)
 
@@ -307,51 +495,55 @@
 
     normal_rows, _ = layer_stats(source_rows.astype(F32))
     normed_one = (normal_rows * gain_one + bias_one).astype(BF16)
+    grad_rows = (cotan_rows.astype(F32) * row_scale).astype(BF16)
+    normed_one, grad_rows, tables, decay = together((normed_one, grad_rows, tables, decay))
+    w_out = lax.all_gather(shuffled, "dp", axis=0, tiled=True)
+    w_feed = lax.all_gather(
+        jnp.concatenate([up_weight, down_weight.T], axis=1), "dp", axis=0, tiled=True
+    )
+
     pre = dot(normed_one, w_in)
     gated, state_low = retention_call(heads, blocks, block_order, pre, tables, decay, ())
 
-    def by_piece(x):
-        return [x[m * rows : (m + 1) * rows] for m in masks]
-
     source = tokens.astype(F32)
-    middle = source + collect([dot(piece, w_out) for piece in by_piece(gated)])
+    middle = source + collect(row_product(gated, w_out, False, parts))[0]
     normal_two, factor_two = layer_stats(middle)
     normed_two = (normal_two * gain_two + bias_two).astype(BF16)
-    normed_rows = jnp.concatenate(spread(normed_two), axis=0)
-    hidden_pre = dot(normed_rows, w_up)
-    hidden = jax.nn.gelu(hidden_pre).astype(BF16)
-    feed_sum = collect([contract_cols(piece, w_down) for piece in by_piece(hidden)])
-    outputs = (middle + feed_sum).astype(BF16)
-
-    grad_rows = (cotan_rows.astype(F32) * row_scale).astype(BF16)
-    d_hidden = dot(grad_rows, w_down)
-    _, gelu_pull = jax.vjp(jax.nn.gelu, hidden_pre)
-    d_pre = gelu_pull(d_hidden)[0].astype(BF16)
-    d_normed_two = collect([contract_cols(piece, w_up) for piece in by_piece(d_pre)])
-    down_part = contract_rows(grad_rows, hidden).astype(BF16)
-    up_part = contract_rows(normed_rows, d_pre).astype(BF16)
+    normed_rows = spread(normed_two)
+    hidden, d_pre, *pieces = feed_call(normed_rows, grad_rows, w_feed, parts)
+    *pieces, hidden, d_pre = together((*pieces, hidden, d_pre))
+    feed_part = feed_grads(normed_rows, grad_rows, hidden, d_pre)
+    d_normed_two, feed_part = collect(pieces, feed_part)
+    scatter = functools.partial(
+        lax.psum_scatter, axis_name="dp", scatter_dimension=0, tiled=True
+    )
+    feed_grad = scatter(feed_part)
 
     cotan = cotangent.astype(F32) * row_scale
     d_middle = cotan + layer_back(d_normed_two * gain_two, normal_two, factor_two)
-    branch_rows = jnp.concatenate(spread(d_middle.astype(BF16)), axis=0)
+    branch_rows = spread(d_middle.astype(BF16))
     d_gated = contract_cols(branch_rows, w_out)
-    output_part = contract_rows(gated, branch_rows).astype(BF16)
     d_in = retention_call(
         heads, blocks, block_order, pre, tables, decay, (state_low, d_gated)
     )
+    d_in, branch_rows, feed_grad = together((d_in, branch_rows, feed_grad))
+    output_part = contract_rows(gated, branch_rows).astype(BF16)
+    d_in, output_part = together((d_in, output_part))
     in_part = contract_rows(normed_one, d_in).astype(BF16)
-    d_normed_one = collect([contract_cols(piece, w_in) for piece in by_piece(d_in)])
+    d_in, in_part, hidden = together((d_in, in_part, hidden))
+    d_normed_one, _ = collect(row_product(d_in, w_in, True, parts))
     normal_one, factor_one = layer_stats(source)
     d_tokens = d_middle + layer_back(d_normed_one * gain_one, normal_one, factor_one)
 
-    scatter = functools.partial(
-        lax.psum_scatter, axis_name="dp", scatter_dimension=0, tiled=True
-    )
-    down_grad = scatter(down_part).astype(F32).T
-    up_grad = scatter(up_part).astype(F32)
-    unshuffle = [(target, at) for at, target in shuffle]
-    output_grad = lax.ppermute(scatter(output_part), ("dp", "mp"), unshuffle).astype(F32)
+    feed_sum, _ = collect(row_product(hidden, w_feed, True, parts, 1))
+    outputs = (middle + feed_sum).astype(BF16)
+
+    width = up_weight.shape[1]
+    up_grad = feed_grad[:, :width].astype(F32)
+    down_grad = feed_grad[:, width:].astype(F32).T
+    finish = shuffle(scatter(output_part), True)
     in_grad = scatter(in_part)
+    output_grad = finish(in_grad).astype(F32)
     pieces = by_index([in_grad[m * part : (m + 1) * part] for m in masks])
     pieces = by_index([swap(pieces[m], m) for m in masks])
     grads, at = [], 0
@@ -371,9 +563,8 @@
         ],
         axis=0,
     )
-    thin_grads = lax.psum_scatter(
-        thin_grads, ("dp", "mp"), scatter_dimension=1, tiled=True
-    )
+    thin_grads = thin_grads.reshape(4, dp * mp, part).transpose(1, 0, 2).reshape(dp * mp, 4 * part)
+    thin_grads = scatter_small(thin_grads).reshape(4, part)
     return (
         outputs,
         d_tokens.astype(BF16),

time: 929 us -> 662 us (0.71)
  waiting for transfers between devices: 566 us -> 285 us
  matrix products: 159 us -> 54.3 us
  Pallas kernels: 23.7 us -> 94.7 us
  other arithmetic: 28.1 us -> 58.6 us
  local copies, waits for them, and re-layouts: 24.3 us -> 40.3 us
    ppermute x30 -> x57, waiting for transfers between devices: 300 us -> 176 us  [swap(): return lax.ppermute(x, 'mp', [(s, s ^ mask) for s in range(mp)])]
    unnamed x10 -> x6, waiting for transfers between devices: 119 us -> 0.1 us
    reduce_scatter x3 -> x2, waiting for transfers between devices: 96.5 us -> 9.82 us  [the longest x1 9.8 us: on_device(): feed_grad = scatter(feed_part)]
    pallas_call x0 -> x5, Pallas kernels: none -> 71.2 us  [the longest x3 34.9 us: row_product(): pl.pallas_call(functools.partial(product_kernel, ((1,), (1 if transposed...]
    dot_general x13 -> x1, matrix products: 62.2 us -> 6.34 us  [contract_cols(): lax.dot_general(left, right, (((1,), (1,)), ((), ())), preferred_element_...]
    reduce_scatter x1, waiting for transfers between devices: 0.01 us -> 51 us  [on_device(): in_grad = scatter(in_part)]
    all_gather x4 -> x3, waiting for transfers between devices: 50.5 us -> 6.27 us  [the longest x1 6.27 us: on_device(): w_out = lax.all_gather(shuffled, 'dp', axis=0, tiled=True)]
    ppermute x2 -> x13, waiting for transfers between devices: 0.01 us -> 41.9 us  [the longest x8 37.6 us: shuffle(): move = lambda v, pairs: lax.ppermute(v, ('dp', 'mp'), pairs)]
  transfers between devices with their start and end apart: 41 -> 76, of which waited for: 25 -> 35; matrix products, arithmetic and copies ran while one was open for 18% -> 20% of each run, Pallas kernels for 3% -> 11%
where the time goes in v2:
time: 662 us; the launch traced here: 652 us
  waiting for transfers between devices  285 us (43%)
  Pallas kernels  94.7 us (14%)
  starting transfers between devices  84.7 us (13%)
  other arithmetic  58.6 us (9%)
  matrix products  54.3 us (8%)
  local copies, waits for them, and re-layouts  40.3 us (6%)
  between operations  17.7 us (3%)
  blocking collectives  16.5 us (2%)
    ppermute x57, waiting for transfers between devices, swap(): return lax.ppermute(x, 'mp', [(s, s ^ mask) for s in range(mp)])  176 us
    ppermute x57, starting transfers between devices, swap(): return lax.ppermute(x, 'mp', [(s, s ^ mask) for s in range(mp)])  68.5 us
    reduce_scatter x1, waiting for transfers between devices, on_device(): in_grad = scatter(in_part)  51 us
    ppermute x8, waiting for transfers between devices, shuffle(): move = lambda v, pairs: lax.ppermute(v, ('dp', 'mp'), pairs)  37.6 us
    pallas_call x3, Pallas kernels, row_product(): pl.pallas_call(functools.partial(product_kernel, ((1,), (1 if transposed...  34.9 us
    dot_general x2, matrix products, contract_rows(): lax.dot_general(left, right, (((0,), (0,)), ((), ())), preferred_element_...  29 us
    unnamed x97, local copies, waits for them, and re-layouts  28.7 us
    pallas_call x1, Pallas kernels, feed_call(): pl.pallas_call(functools.partial(feed_kernel, steps), grid=(steps + out_s...  23.9 us
  transfers between devices with their start and end apart: 76, of which 35 were waited for; matrix products, arithmetic and copies ran while one was open for 20% of the time, Pallas kernels for 11%

profile of v2, /device:TPU:0, one launch (start us, length us, event | category | flops | bytes accessed | tf_op | source)
XLA Modules:
  0.0 651.6 jit_solution(1370128234886853691)
XLA Ops:
  9.9 3.0 collective-permute-start
  16.9 16.5 %all-reduce = bf16[2560]{0:T(1024)(128)(2,1)S(1)} all-reduce(bf16[2560]{0:T(1024)(128)(2,1)S(1)} %dynamic-update-slice), channel_id=2, replica_groups=mesh['dp'=8,'mp'=4] {'dp'}, use_global_device_ids=true, to_apply=%add | all-reduce | flops 2560 | bytes 10240
  38.0 30.4 %collective-permute-done.19 = bf16[128,2048]{1,0:T(8,128)(2,1)} collective-permute-done((bf16[128,2048]{1,0:T(8,128)(2,1)S(1)}, bf16[128,2048]{1,0:T(8,128)(2,1)}, u32[]{:S(2)}, u32[]{:S(2)}) %collective-permute-start.19) | collective-permute-done | bytes 524320 | tf_op jit(solution)/shard_map/ppermute | solution.py:416
  71.5 7.1 %collective-permute-done.21 = bf16[128,2048]{1,0:T(8,128)(2,1)S(1)} collective-permute-done((bf16[128,2048]{1,0:T(8,128)(2,1)}, bf16[128,2048]{1,0:T(8,128)(2,1)S(1)}, u32[]{:S(2)}, u32[]{:S(2)}) %collective-permute-start.21) | collective-permute-done | bytes 524320 | tf_op jit(solution)/shard_map/ppermute | solution.py:416
  85.5 6.0 collective-permute-start.3
  91.5 3.3 collective-permute-start.5
  102.8 4.4 collective-permute-done.11
  114.1 8.2 %collective-permute-done.4 = bf16[128,2048]{1,0:T(8,128)(2,1)} collective-permute-done((bf16[128,2048]{1,0:T(8,128)(2,1)}, bf16[128,2048]{1,0:T(8,128)(2,1)}, u32[]{:S(2)}, u32[]{:S(2)}) %collective-permute-start.4) | collective-permute-done | bytes 524320 | tf_op jit(solution)/shard_map/ppermute | solution.py:369
  130.4 3.0 collective-permute-done.12
  133.9 10.8 %collective-permute-done.13 = bf16[128,2048]{1,0:T(8,128)(2,1)S(1)} collective-permute-done((bf16[128,2048]{1,0:T(8,128)(2,1)}, bf16[128,2048]{1,0:T(8,128)(2,1)S(1)}, u32[]{:S(2)}, u32[]{:S(2)}) %collective-permute-start.13) | collective-permute-done | bytes 524320 | tf_op jit(solution)/shard_map/ppermute | solution.py:369
  146.8 9.5 %collective-permute-done.7 = bf16[128,2048]{1,0:T(8,128)(2,1)S(1)} collective-permute-done((bf16[128,2048]{1,0:T(8,128)(2,1)S(1)}, bf16[128,2048]{1,0:T(8,128)(2,1)S(1)}, u32[]{:S(2)}, u32[]{:S(2)}) %collective-permute-start.7) | collective-permute-done | bytes 524320 | tf_op jit(solution)/shard_map/ppermute | solution.py:369
  158.0 3.0 convert_reduce_fusion
  162.7 3.4 collective-permute-done.16
  166.2 3.1 multiply_convert_fusion.grad_ref
  169.3 3.3 fusion.5
  172.6 19.0 %fusion.43.pre_ref = f32[1024,3072]{1,0:T(8,128)} fusion(bf16[1024,2048]{1,0:T(8,128)(2,1)} %fusion.5, bf16[2048,3072]{1,0:T(8,128)(2,1)} %all-gather.5.cloned.1.call-done.b_ref), kind=kOutput, calls=%fused_computation.204 | convolution fusion | flops 12884901888 | bytes 29360128 | tf_op jit(solution)/shard_map/dot_general | solution.py:50
  191.6 8.3 %retention_forward.1 = (bf16[1024,1024]{1,0:T(8,128)(2,1)S(1)}, bf16[4,2,256,512]{3,2,1,0:T(8,128)(2,1)}) custom-call(s32[4]{0:T(128)S(1)} %iota_xor_fusion.order_ref, f32[2]{0:T(128)S(1)} %get-tuple-element.102.block_ref, f32[1024,3072]{1,0:T(8,128)} %fusion.43.pre_ref, f32[1024,128]{1,0:T(8,128)S(1)} %get-tuple-element.104.cos_ref, ...), custom_call_target="tpu_custom_call" | custom-call | flops 1879048192 | bytes 15728640 | tf_op jit(solution)/shard_map/retention_forward/pallas_call | solution.py:197
  201.2 6.3 all-gather.7.cloned.1.call-done.b_ref
  207.5 8.0 %row_product.3 = (bf16[128,2048]{1,0:T(8,128)(2,1)S(1)}, bf16[128,2048]{1,0:T(8,128)(2,1)S(1)}, bf16[128,2048]{1,0:T(8,128)(2,1)}, bf16[128,2048]{1,0:T(8,128)(2...) custom-call(bf16[1024,1024]{1,0:T(8,128)(2,1)} %copy-done.3, ...), custom_call_target="tpu_custom_call" | custom-call | flops 4294967296 | bytes 10485760 | tf_op jit(solution)/shard_map/row_product/pallas_call | solution.py:232
  219.8 10.4 %collective-permute-done.23 = bf16[128,2048]{1,0:T(8,128)(2,1)S(1)} collective-permute-done((bf16[128,2048]{1,0:T(8,128)(2,1)S(1)}, bf16[128,2048]{1,0:T(8,128)(2,1)S(1)}, u32[]{:S(2)}, u32[]{:S(2)}) %collective-permute-start.23) | collective-permute-done | bytes 524320 | tf_op jit(solution)/shard_map/ppermute | solution.py:369
  235.8 7.3 %collective-permute-done.27 = bf16[128,2048]{1,0:T(8,128)(2,1)} collective-permute-done((bf16[128,2048]{1,0:T(8,128)(2,1)}, bf16[128,2048]{1,0:T(8,128)(2,1)}, u32[]{:S(2)}, u32[]{:S(2)}) %collective-permute-start.27) | collective-permute-done | bytes 524320 | tf_op jit(solution)/shard_map/ppermute | solution.py:369
  243.0 9.0 %collective-permute-done.26 = bf16[128,2048]{1,0:T(8,128)(2,1)} collective-permute-done((bf16[128,2048]{1,0:T(8,128)(2,1)}, bf16[128,2048]{1,0:T(8,128)(2,1)}, u32[]{:S(2)}, u32[]{:S(2)}) %collective-permute-start.26) | collective-permute-done | bytes 524320 | tf_op jit(solution)/shard_map/ppermute | solution.py:369
  261.7 10.8 %collective-permute-done.28 = bf16[128,2048]{1,0:T(8,128)(2,1)S(1)} collective-permute-done((bf16[128,2048]{1,0:T(8,128)(2,1)S(1)}, bf16[128,2048]{1,0:T(8,128)(2,1)S(1)}, u32[]{:S(2)}, u32[]{:S(2)}) %collective-permute-start.28) | collective-permute-done | bytes 524320 | tf_op jit(solution)/shard_map/ppermute | solution.py:369
  276.3 7.5 %collective-permute-done.29 = bf16[128,2048]{1,0:T(8,128)(2,1)S(1)} collective-permute-done((bf16[128,2048]{1,0:T(8,128)(2,1)S(1)}, bf16[128,2048]{1,0:T(8,128)(2,1)S(1)}, u32[]{:S(2)}, u32[]{:S(2)}) %collective-permute-start.29) | collective-permute-done | bytes 524320 | tf_op jit(solution)/shard_map/ppermute | solution.py:369
  286.9 7.7 %collective-permute-done.32 = bf16[128,2048]{1,0:T(8,128)(2,1)S(1)} collective-permute-done((bf16[128,2048]{1,0:T(8,128)(2,1)S(1)}, bf16[128,2048]{1,0:T(8,128)(2,1)S(1)}, u32[]{:S(2)}, u32[]{:S(2)}) %collective-permute-start.32) | collective-permute-done | bytes 524320 | tf_op jit(solution)/shard_map/ppermute | solution.py:369
  296.2 23.9 %feed_forward.1 = (bf16[1024,1024]{1,0:T(8,128)(2,1)}, bf16[1024,1024]{1,0:T(8,128)(2,1)}, bf16[128,2048]{1,0:T(8,128)(2,1)}, bf16[128,2048]{1,0:T(8,128)(2,1)},...) custom-call(bf16[1024,2048]{1,0:T(8,128)(2,1)} %constant_dynamic-upd, ...), custom_call_target="tpu_custom_call" | custom-call | flops 12884901888 | bytes 20971520 | tf_op jit(solution)/shard_map/feed_forward/pallas_call | solution.py:282
  325.4 12.4 %feed_grads.1 = bf16[2048,2048]{1,0:T(8,128)(2,1)} custom-call(bf16[1024,2048]{1,0:T(8,128)(2,1)} %constant_dynamic-update-slice_fusion.14.normed_ref, bf16[1024,2048]{1,0:T(8,128)(2,1)} %multiply_convert_fusion.grad_ref, bf16[1024,1024]{1,0:T(8,128)(2,1)S(1)} %copy-done.7, bf16[1024,1024]{1,0:T(8,128)(2,1)S(1)} %copy-done.8), custom_call_target="tpu_custom_call" | custom-call | flops 8589934592 | bytes 20971520 | tf_op jit(solution)/shard_map/feed_grads/pallas_call | solution.py:321
  345.6 8.2 %collective-permute-done.39 = bf16[128,2048]{1,0:T(8,128)(2,1)S(1)} collective-permute-done((bf16[128,2048]{1,0:T(8,128)(2,1)}, bf16[128,2048]{1,0:T(8,128)(2,1)S(1)}, u32[]{:S(2)}, u32[]{:S(2)}) %collective-permute-start.39) | collective-permute-done | bytes 524320 | tf_op jit(solution)/shard_map/ppermute | solution.py:369
  353.8 8.2 %collective-permute-done.38 = bf16[128,2048]{1,0:T(8,128)(2,1)S(1)} collective-permute-done((bf16[128,2048]{1,0:T(8,128)(2,1)S(1)}, bf16[128,2048]{1,0:T(8,128)(2,1)S(1)}, u32[]{:S(2)}, u32[]{:S(2)}) %collective-permute-start.38) | collective-permute-done | bytes 524320 | tf_op jit(solution)/shard_map/ppermute | solution.py:369
  369.9 10.8 %collective-permute-done.40 = bf16[128,2048]{1,0:T(8,128)(2,1)S(1)} collective-permute-done((bf16[128,2048]{1,0:T(8,128)(2,1)S(1)}, bf16[128,2048]{1,0:T(8,128)(2,1)S(1)}, u32[]{:S(2)}, u32[]{:S(2)}) %collective-permute-start.40) | collective-permute-done | bytes 524320 | tf_op jit(solution)/shard_map/ppermute | solution.py:369
  383.7 8.3 %collective-permute-done.41 = bf16[128,2048]{1,0:T(8,128)(2,1)S(1)} collective-permute-done((bf16[128,2048]{1,0:T(8,128)(2,1)S(1)}, bf16[128,2048]{1,0:T(8,128)(2,1)S(1)}, u32[]{:S(2)}, u32[]{:S(2)}) %collective-permute-start.41) | collective-permute-done | bytes 524320 | tf_op jit(solution)/shard_map/ppermute | solution.py:369
  393.5 6.4 collective-permute-done.44
  400.1 6.3 fusion.44.grad_ref
  406.4 15.3 %retention_backward.1.a_ref = bf16[1024,3072]{1,0:T(8,128)(2,1)} custom-call(s32[4]{0:T(128)S(1)} %iota_xor_fusion.order_ref, f32[2]{0:T(128)S(1)} %get-tuple-element.102.block_ref, f32[1024,3072]{1,0:T(8,128)} %fusion.43.pre_ref, f32[1024,128]{1,0:T(8,128)S(1)} %get-tuple-element.104.cos_ref, f32[1024,128]{1,0:T(8,128)S(1)} %get-tuple-element.105.sin_ref, ...), custom_call_target="tpu_custom_call" | custom-call | flops 4026531840 | bytes 18874368 | tf_op jit(solution)/shard_map/retention_backward/pallas_call | solution.py:197
  421.7 9.8 %reduce-scatter.4.cloned.1.call-done = bf16[256,2048]{1,0:T(8,128)(2,1)} async-done(((bf16[2048,2048]{1,0:T(8,128)(2,1)}), bf16[256,2048]{1,0:T(8,128)(2,1)}) %reduce-scatter.4.cloned.1.call-update) | async-done | bytes 1048592 | tf_op jit(solution)/shard_map/reduce_scatter | solution.py:520
  431.5 9.4 %convolution_convert_fusion.1 = bf16[1024,2048]{1,0:T(8,128)(2,1)} fusion(bf16[1024,1024]{1,0:T(8,128)(2,1)} %copy-done.3, bf16[1024,2048]{1,0:T(8,128)(2,1)} %copy-done.25), kind=kOutput, calls=%fused_computation.10 | convolution fusion | flops 4297064448 | bytes 10485760 | tf_op jit(solution)/shard_map/dot_general | solution.py:54
  440.9 19.6 %convolution_convert_fusion = bf16[2048,3072]{1,0:T(8,128)(2,1)} fusion(bf16[1024,2048]{1,0:T(8,128)(2,1)} %fusion.5, bf16[1024,3072]{1,0:T(8,128)(2,1)} %retention_backward.1.a_ref), kind=kOutput, calls=%fused_computation | convolution fusion | flops 12891193344 | bytes 23068672 | tf_op jit(solution)/shard_map/dot_general | solution.py:54
  460.6 8.1 %row_product.4 = (bf16[128,2048]{1,0:T(8,128)(2,1)S(1)}, bf16[128,2048]{1,0:T(8,128)(2,1)S(1)}, bf16[128,2048]{1,0:T(8,128)(2,1)}, bf16[128,2048]{1,0:T(8,128)(2...) custom-call(bf16[1024,1024]{1,0:T(8,128)(2,1)} %get-tuple-element.15, ...), custom_call_target="tpu_custom_call" | custom-call | flops 4294967296 | bytes 10485760 | tf_op jit(solution)/shard_map/row_product/pallas_call | solution.py:232
  472.5 18.8 %row_product.5 = (bf16[128,2048]{1,0:T(8,128)(2,1)S(1)}, bf16[128,2048]{1,0:T(8,128)(2,1)S(1)}, bf16[128,2048]{1,0:T(8,128)(2,1)S(1)}, bf16[128,2048]{1,0:T(8,12...) custom-call(bf16[1024,3072]{1,0:T(8,128)(2,1)} %retention_backward.1, ...), custom_call_target="tpu_custom_call" | custom-call | flops 12884901888 | bytes 23068672 | tf_op jit(solution)/shard_map/row_product/pallas_call | solution.py:232
  497.3 2.8 convert_bitcast_fusion
  504.8 4.2 collective-permute-done.53
  519.0 13.6 %collective-permute-done.57 = bf16[128,2048]{1,0:T(8,128)(2,1)S(1)} collective-permute-done((bf16[128,2048]{1,0:T(8,128)(2,1)}, bf16[128,2048]{1,0:T(8,128)(2,1)S(1)}, u32[]{:S(2)}, u32[]{:S(2)}) %collective-permute-start.57) | collective-permute-done | bytes 524320 | tf_op jit(solution)/shard_map/ppermute | solution.py:369
  536.4 7.4 %collective-permute-done.55 = bf16[128,2048]{1,0:T(8,128)(2,1)S(1)} collective-permute-done((bf16[128,2048]{1,0:T(8,128)(2,1)S(1)}, bf16[128,2048]{1,0:T(8,128)(2,1)S(1)}, u32[]{:S(2)}, u32[]{:S(2)}) %collective-permute-start.55) | collective-permute-done | bytes 524320 | tf_op jit(solution)/shard_map/ppermute | solution.py:369
  545.1 2.8 fusion.16
  548.8 3.6 fusion.15
  568.1 51.0 %reduce-scatter.6.cloned.1.call-done = bf16[256,3072]{1,0:T(8,128)(2,1)} async-done(((bf16[2048,3072]{1,0:T(8,128)(2,1)}), bf16[256,3072]{1,0:T(8,128)(2,1)}) %reduce-scatter.6.cloned.1.call-update) | async-done | bytes 1572880 | tf_op jit(solution)/shard_map/reduce_scatter | solution.py:545
  627.6 6.3 collective-permute-done.60
  633.9 5.1 collective-permute-done.59
  (347 shorter events, 162.6 us)
Async XLA Ops:
  7.2 165.4 %all-gather.5.cloned.1.call-start = ((), (), s32[]{:S(2)}) async-start(), calls=%async_computation.3 | async-start | bytes 14155776 | tf_op jit(solution)/shard_map/all_gather | solution.py:474
  9.9 23.6 %collective-permute-start = (bf16[64,3072]{1,0:T(8,128)(2,1)S(1)}, bf16[64,3072]{1,0:T(8,128)(2,1)S(1)}, u32[]{:S(2)}, u32[]{:S(2)}) collective-permute-start(bf16[64,3072]{1,0:T(8,128)(2,1)S(1)} %pad_maximum_fusion.8), channel_id=1, source_target_pairs={{0,1},{1,0},{2,3},{3,2},{4,5},{5,4},{6,7},{7,6},{8,9},{9,8},{10,11... | collective-permute-start | bytes 1179656 | tf_op jit(solution)/shard_map/ppermute | solution.py:369
  12.9 20.6 %collective-permute-start.1 = (bf16[64,3072]{1,0:T(8,128)(2,1)S(1)}, bf16[64,3072]{1,0:T(8,128)(2,1)S(1)}, u32[]{:S(2)}, u32[]{:S(2)}) collective-permute-start(bf16[64,3072]{1,0:T(8,128)(2,1)S(1)} %pad_maximum_fusion.9), channel_id=1, source_target_pairs={{0,2},{1,3},{2,0},{3,1},{4,6},{5,7},{6,4},{7,5},{8,10},{9,11},{10,... | collective-permute-start | bytes 1179656 | tf_op jit(solution)/shard_map/ppermute | solution.py:369
  14.5 19.0 %collective-permute-start.2 = (bf16[64,3072]{1,0:T(8,128)(2,1)S(1)}, bf16[64,3072]{1,0:T(8,128)(2,1)S(1)}, u32[]{:S(2)}, u32[]{:S(2)}) collective-permute-start(bf16[64,3072]{1,0:T(8,128)(2,1)S(1)} %pad_maximum_fusion.10), channel_id=1, source_target_pairs={{0,3},{1,2},{2,1},{3,0},{4,7},{5,6},{6,5},{7,4},{8,11},{9,10},{10,... | collective-permute-start | bytes 1179656 | tf_op jit(solution)/shard_map/ppermute | solution.py:369
  35.2 172.3 %all-gather.7.cloned.1.call-start = ((), (), s32[]{:S(2)}) async-start(), calls=%async_computation.4 | async-start | bytes 4718592 | tf_op jit(solution)/shard_map/all_gather | solution.py:500
  36.7 31.7 %collective-permute-start.19 = (bf16[128,2048]{1,0:T(8,128)(2,1)S(1)}, bf16[128,2048]{1,0:T(8,128)(2,1)}, u32[]{:S(2)}, u32[]{:S(2)}) collective-permute-start(bf16[128,2048]{1,0:T(8,128)(2,1)S(1)} %copy-done.33), channel_id=1, source_target_pairs={{16,0},{17,1},{18,10},{19,11},{20,16},{21,17},{22,26},{23,27},{24,... | collective-permute-start | bytes 1572872 | tf_op jit(solution)/shard_map/ppermute | solution.py:416
  79.5 216.8 %all-gather.9.cloned.1.call-start = ((), (), s32[]{:S(2)}) async-start(), calls=%async_computation.5 | async-start | bytes 9437184 | tf_op jit(solution)/shard_map/all_gather | solution.py:501
  80.8 350.7 %reduce-scatter.4.cloned.1.call-start = ((), (), s32[]{:S(2)}) async-start(), calls=%async_computation.6 | async-start | bytes 9437184 | tf_op jit(solution)/shard_map/reduce_scatter | solution.py:520
  85.5 26.0 %collective-permute-start.3 = (bf16[128,2048]{1,0:T(8,128)(2,1)}, bf16[128,2048]{1,0:T(8,128)(2,1)S(1)}, u32[]{:S(2)}, u32[]{:S(2)}) collective-permute-start(bf16[128,2048]{1,0:T(8,128)(2,1)} %get-tuple-element.265), channel_id=1, source_target_pairs={{0,1},{1,0},{2,3},{3,2},{4,5},{5,4},{6,7},{7,6},{8,9},{9,8},{10,11... | collective-permute-start | bytes 1572872 | tf_op jit(solution)/shard_map/ppermute | solution.py:369
  91.5 33.1 %collective-permute-start.5 = (bf16[128,2048]{1,0:T(8,128)(2,1)}, bf16[128,2048]{1,0:T(8,128)(2,1)}, u32[]{:S(2)}, u32[]{:S(2)}) collective-permute-start(bf16[128,2048]{1,0:T(8,128)(2,1)} %get-tuple-element.265), channel_id=1, source_target_pairs={{0,2},{1,3},{2,0},{3,1},{4,6},{5,7},{6,4},{7,5},{8,10},{9,11},{10,... | collective-permute-start | bytes 1572872 | tf_op jit(solution)/shard_map/ppermute | solution.py:369
  107.6 18.9 %collective-permute-start.6 = (bf16[128,2048]{1,0:T(8,128)(2,1)}, bf16[128,2048]{1,0:T(8,128)(2,1)}, u32[]{:S(2)}, u32[]{:S(2)}) collective-permute-start(bf16[128,2048]{1,0:T(8,128)(2,1)} %get-tuple-element.264), channel_id=1, source_target_pairs={{0,2},{1,3},{2,0},{3,1},{4,6},{5,7},{6,4},{7,5},{8,10},{9,11},{10,... | collective-permute-start | bytes 1572872 | tf_op jit(solution)/shard_map/ppermute | solution.py:369
  107.8 25.6 %collective-permute-start.12 = (bf16[128,2048]{1,0:T(8,128)(2,1)}, bf16[128,2048]{1,0:T(8,128)(2,1)S(1)}, u32[]{:S(2)}, u32[]{:S(2)}) collective-permute-start(bf16[128,2048]{1,0:T(8,128)(2,1)} %get-tuple-element.263), channel_id=1, source_target_pairs={{0,1},{1,0},{2,3},{3,2},{4,5},{5,4},{6,7},{7,6},{8,9},{9,8},{10,11... | collective-permute-start | bytes 1572872 | tf_op jit(solution)/shard_map/ppermute | solution.py:369
  111.5 35.2 %collective-permute-start.14 = (bf16[128,2048]{1,0:T(8,128)(2,1)}, bf16[128,2048]{1,0:T(8,128)(2,1)S(1)}, u32[]{:S(2)}, u32[]{:S(2)}) collective-permute-start(bf16[128,2048]{1,0:T(8,128)(2,1)} %get-tuple-element.263), channel_id=1, source_target_pairs={{0,2},{1,3},{2,0},{3,1},{4,6},{5,7},{6,4},{7,5},{8,10},{9,11},{10,... | collective-permute-start | bytes 1572872 | tf_op jit(solution)/shard_map/ppermute | solution.py:369
  122.3 22.4 %collective-permute-start.13 = (bf16[128,2048]{1,0:T(8,128)(2,1)}, bf16[128,2048]{1,0:T(8,128)(2,1)S(1)}, u32[]{:S(2)}, u32[]{:S(2)}) collective-permute-start(bf16[128,2048]{1,0:T(8,128)(2,1)} %get-tuple-element.262), channel_id=1, source_target_pairs={{0,1},{1,0},{2,3},{3,2},{4,5},{5,4},{6,7},{7,6},{8,9},{9,8},{10,11... | collective-permute-start | bytes 1572872 | tf_op jit(solution)/shard_map/ppermute | solution.py:369
  124.6 20.5 %collective-permute-start.15 = (bf16[128,2048]{1,0:T(8,128)(2,1)}, bf16[128,2048]{1,0:T(8,128)(2,1)S(1)}, u32[]{:S(2)}, u32[]{:S(2)}) collective-permute-start(bf16[128,2048]{1,0:T(8,128)(2,1)} %get-tuple-element.262), channel_id=1, source_target_pairs={{0,2},{1,3},{2,0},{3,1},{4,6},{5,7},{6,4},{7,5},{8,10},{9,11},{10,... | collective-permute-start | bytes 1572872 | tf_op jit(solution)/shard_map/ppermute | solution.py:369
  126.5 29.9 %collective-permute-start.7 = (bf16[128,2048]{1,0:T(8,128)(2,1)S(1)}, bf16[128,2048]{1,0:T(8,128)(2,1)S(1)}, u32[]{:S(2)}, u32[]{:S(2)}) collective-permute-start(bf16[128,2048]{1,0:T(8,128)(2,1)S(1)} %collective-permute-done.3), channel_id=1, source_target_pairs={{0,2},{1,3},{2,0},{3,1},{4,6},{5,7},{6,4},{7,5},{8,10},{9,11},{10,... | collective-permute-start | bytes 1572872 | tf_op jit(solution)/shard_map/ppermute | solution.py:369
  133.4 23.8 %collective-permute-start.8 = (bf16[128,2048]{1,0:T(8,128)(2,1)}, bf16[128,2048]{1,0:T(8,128)(2,1)S(1)}, u32[]{:S(2)}, u32[]{:S(2)}) collective-permute-start(bf16[128,2048]{1,0:T(8,128)(2,1)} %collective-permute-done.6), channel_id=1, source_target_pairs={{0,1},{1,0},{2,3},{3,2},{4,5},{5,4},{6,7},{7,6},{8,9},{9,8},{10,11... | collective-permute-start | bytes 1572872 | tf_op jit(solution)/shard_map/ppermute | solution.py:369
  144.6 21.5 %collective-permute-start.16 = (bf16[128,2048]{1,0:T(8,128)(2,1)S(1)}, bf16[128,2048]{1,0:T(8,128)(2,1)S(1)}, u32[]{:S(2)}, u32[]{:S(2)}) collective-permute-start(bf16[128,2048]{1,0:T(8,128)(2,1)S(1)} %collective-permute-done.12), channel_id=1, source_target_pairs={{0,2},{1,3},{2,0},{3,1},{4,6},{5,7},{6,4},{7,5},{8,10},{9,11},{10,... | collective-permute-start | bytes 1572872 | tf_op jit(solution)/shard_map/ppermute | solution.py:369
  145.1 21.1 %collective-permute-start.17 = (bf16[128,2048]{1,0:T(8,128)(2,1)S(1)}, bf16[128,2048]{1,0:T(8,128)(2,1)S(1)}, u32[]{:S(2)}, u32[]{:S(2)}) collective-permute-start(bf16[128,2048]{1,0:T(8,128)(2,1)S(1)} %collective-permute-done.15), channel_id=1, source_target_pairs={{0,1},{1,0},{2,3},{3,2},{4,5},{5,4},{6,7},{7,6},{8,9},{9,8},{10,11... | collective-permute-start | bytes 1572872 | tf_op jit(solution)/shard_map/ppermute | solution.py:369
  218.6 24.4 %collective-permute-start.27 = (bf16[128,2048]{1,0:T(8,128)(2,1)}, bf16[128,2048]{1,0:T(8,128)(2,1)}, u32[]{:S(2)}, u32[]{:S(2)}) collective-permute-start(bf16[128,2048]{1,0:T(8,128)(2,1)} %get-tuple-element.121), channel_id=1, source_target_pairs={{0,2},{1,3},{2,0},{3,1},{4,6},{5,7},{6,4},{7,5},{8,10},{9,11},{10,... | collective-permute-start | bytes 1572872 | tf_op jit(solution)/shard_map/ppermute | solution.py:369
  219.2 34.3 %collective-permute-start.22 = (bf16[128,2048]{1,0:T(8,128)(2,1)}, bf16[128,2048]{1,0:T(8,128)(2,1)}, u32[]{:S(2)}, u32[]{:S(2)}) collective-permute-start(bf16[128,2048]{1,0:T(8,128)(2,1)} %get-tuple-element.113), channel_id=1, source_target_pairs={{0,1},{1,0},{2,3},{3,2},{4,5},{5,4},{6,7},{7,6},{8,9},{9,8},{10,11... | collective-permute-start | bytes 1572872 | tf_op jit(solution)/shard_map/ppermute | solution.py:369
  232.6 19.5 %collective-permute-start.26 = (bf16[128,2048]{1,0:T(8,128)(2,1)}, bf16[128,2048]{1,0:T(8,128)(2,1)}, u32[]{:S(2)}, u32[]{:S(2)}) collective-permute-start(bf16[128,2048]{1,0:T(8,128)(2,1)} %add_convert_fusion.7), channel_id=1, source_target_pairs={{0,1},{1,0},{2,3},{3,2},{4,5},{5,4},{6,7},{7,6},{8,9},{9,8},{10,11... | collective-permute-start | bytes 1572872 | tf_op jit(solution)/shard_map/ppermute | solution.py:369
  234.1 19.4 %collective-permute-start.25 = (bf16[128,2048]{1,0:T(8,128)(2,1)}, bf16[128,2048]{1,0:T(8,128)(2,1)}, u32[]{:S(2)}, u32[]{:S(2)}) collective-permute-start(bf16[128,2048]{1,0:T(8,128)(2,1)} %add_convert_fusion.8), channel_id=1, source_target_pairs={{0,2},{1,3},{2,0},{3,1},{4,6},{5,7},{6,4},{7,5},{8,10},{9,11},{10,... | collective-permute-start | bytes 1572872 | tf_op jit(solution)/shard_map/ppermute | solution.py:369
  260.6 23.2 %collective-permute-start.29 = (bf16[128,2048]{1,0:T(8,128)(2,1)S(1)}, bf16[128,2048]{1,0:T(8,128)(2,1)S(1)}, u32[]{:S(2)}, u32[]{:S(2)}) collective-permute-start(bf16[128,2048]{1,0:T(8,128)(2,1)S(1)} %get-tuple-element.260), channel_id=1, source_target_pairs={{0,1},{1,0},{2,3},{3,2},{4,5},{5,4},{6,7},{7,6},{8,9},{9,8},{10,11... | collective-permute-start | bytes 1572872 | tf_op jit(solution)/shard_map/ppermute | solution.py:369
  261.2 24.1 %collective-permute-start.30 = (bf16[128,2048]{1,0:T(8,128)(2,1)S(1)}, bf16[128,2048]{1,0:T(8,128)(2,1)S(1)}, u32[]{:S(2)}, u32[]{:S(2)}) collective-permute-start(bf16[128,2048]{1,0:T(8,128)(2,1)S(1)} %get-tuple-element.261), channel_id=1, source_target_pairs={{0,2},{1,3},{2,0},{3,1},{4,6},{5,7},{6,4},{7,5},{8,10},{9,11},{10,... | collective-permute-start | bytes 1572872 | tf_op jit(solution)/shard_map/ppermute | solution.py:369
  272.5 22.0 %collective-permute-start.32 = (bf16[128,2048]{1,0:T(8,128)(2,1)S(1)}, bf16[128,2048]{1,0:T(8,128)(2,1)S(1)}, u32[]{:S(2)}, u32[]{:S(2)}) collective-permute-start(bf16[128,2048]{1,0:T(8,128)(2,1)S(1)} %collective-permute-done.28), channel_id=1, source_target_pairs={{0,2},{1,3},{2,0},{3,1},{4,6},{5,7},{6,4},{7,5},{8,10},{9,11},{10,... | collective-permute-start | bytes 1572872 | tf_op jit(solution)/shard_map/ppermute | solution.py:369
  274.0 21.4 %collective-permute-start.33 = (bf16[128,2048]{1,0:T(8,128)(2,1)S(1)}, bf16[128,2048]{1,0:T(8,128)(2,1)S(1)}, u32[]{:S(2)}, u32[]{:S(2)}) collective-permute-start(bf16[128,2048]{1,0:T(8,128)(2,1)S(1)} %collective-permute-done.31), channel_id=1, source_target_pairs={{0,1},{1,0},{2,3},{3,2},{4,5},{5,4},{6,7},{7,6},{8,9},{9,8},{10,11... | collective-permute-start | bytes 1572872 | tf_op jit(solution)/shard_map/ppermute | solution.py:369
  338.6 226.5 %reduce-scatter.8.cloned.1.call-start = ((), (), s32[]{:S(2)}) async-start(), calls=%async_computation.8 | async-start | bytes 4718592 | tf_op jit(solution)/shard_map/reduce_scatter | solution.py:544
  339.3 22.9 %collective-permute-start.34 = (bf16[128,2048]{1,0:T(8,128)(2,1)}, bf16[128,2048]{1,0:T(8,128)(2,1)S(1)}, u32[]{:S(2)}, u32[]{:S(2)}) collective-permute-start(bf16[128,2048]{1,0:T(8,128)(2,1)} %get-tuple-element.135), channel_id=1, source_target_pairs={{0,1},{1,0},{2,3},{3,2},{4,5},{5,4},{6,7},{7,6},{8,9},{9,8},{10,11... | collective-permute-start | bytes 1572872 | tf_op jit(solution)/shard_map/ppermute | solution.py:369
  342.1 19.9 %collective-permute-start.38 = (bf16[128,2048]{1,0:T(8,128)(2,1)S(1)}, bf16[128,2048]{1,0:T(8,128)(2,1)S(1)}, u32[]{:S(2)}, u32[]{:S(2)}) collective-permute-start(bf16[128,2048]{1,0:T(8,128)(2,1)S(1)} %add_convert_fusion.5), channel_id=1, source_target_pairs={{0,1},{1,0},{2,3},{3,2},{4,5},{5,4},{6,7},{7,6},{8,9},{9,8},{10,11... | collective-permute-start | bytes 1572872 | tf_op jit(solution)/shard_map/ppermute | solution.py:369
  368.8 23.2 %collective-permute-start.41 = (bf16[128,2048]{1,0:T(8,128)(2,1)S(1)}, bf16[128,2048]{1,0:T(8,128)(2,1)S(1)}, u32[]{:S(2)}, u32[]{:S(2)}) collective-permute-start(bf16[128,2048]{1,0:T(8,128)(2,1)S(1)} %get-tuple-element.258), channel_id=1, source_target_pairs={{0,1},{1,0},{2,3},{3,2},{4,5},{5,4},{6,7},{7,6},{8,9},{9,8},{10,11... | collective-permute-start | bytes 1572872 | tf_op jit(solution)/shard_map/ppermute | solution.py:369
  369.4 24.1 %collective-permute-start.42 = (bf16[128,2048]{1,0:T(8,128)(2,1)S(1)}, bf16[128,2048]{1,0:T(8,128)(2,1)S(1)}, u32[]{:S(2)}, u32[]{:S(2)}) collective-permute-start(bf16[128,2048]{1,0:T(8,128)(2,1)S(1)} %get-tuple-element.259), channel_id=1, source_target_pairs={{0,2},{1,3},{2,0},{3,1},{4,6},{5,7},{6,4},{7,5},{8,10},{9,11},{10,... | collective-permute-start | bytes 1572872 | tf_op jit(solution)/shard_map/ppermute | solution.py:369
  380.8 19.2 %collective-permute-start.44 = (bf16[128,2048]{1,0:T(8,128)(2,1)S(1)}, bf16[128,2048]{1,0:T(8,128)(2,1)S(1)}, u32[]{:S(2)}, u32[]{:S(2)}) collective-permute-start(bf16[128,2048]{1,0:T(8,128)(2,1)S(1)} %collective-permute-done.40), channel_id=1, source_target_pairs={{0,2},{1,3},{2,0},{3,1},{4,6},{5,7},{6,4},{7,5},{8,10},{9,11},{10,... | collective-permute-start | bytes 1572872 | tf_op jit(solution)/shard_map/ppermute | solution.py:369
  440.9 178.2 %reduce-scatter.6.cloned.1.call-start = ((), (), s32[]{:S(2)}) async-start(), calls=%async_computation.7 | async-start | bytes 14155776 | tf_op jit(solution)/shard_map/reduce_scatter | solution.py:545
  469.5 33.1 %collective-permute-start.47 = (bf16[128,2048]{1,0:T(8,128)(2,1)}, bf16[128,2048]{1,0:T(8,128)(2,1)}, u32[]{:S(2)}, u32[]{:S(2)}) collective-permute-start(bf16[128,2048]{1,0:T(8,128)(2,1)} %get-tuple-element.154), channel_id=1, source_target_pairs={{0,1},{1,0},{2,3},{3,2},{4,5},{5,4},{6,7},{7,6},{8,9},{9,8},{10,11... | collective-permute-start | bytes 1572872 | tf_op jit(solution)/shard_map/ppermute | solution.py:369
  471.0 32.3 %collective-permute-start.48 = (bf16[128,2048]{1,0:T(8,128)(2,1)}, bf16[128,2048]{1,0:T(8,128)(2,1)}, u32[]{:S(2)}, u32[]{:S(2)}) collective-permute-start(bf16[128,2048]{1,0:T(8,128)(2,1)} %get-tuple-element.155), channel_id=1, source_target_pairs={{0,2},{1,3},{2,0},{3,1},{4,6},{5,7},{6,4},{7,5},{8,10},{9,11},{10,... | collective-permute-start | bytes 1572872 | tf_op jit(solution)/shard_map/ppermute | solution.py:369
  495.8 58.3 %collective-permute-start.51 = (bf16[128,2048]{1,0:T(8,128)(2,1)}, bf16[128,2048]{1,0:T(8,128)(2,1)}, u32[]{:S(2)}, u32[]{:S(2)}) collective-permute-start(bf16[128,2048]{1,0:T(8,128)(2,1)} %copy-done.4), channel_id=1, source_target_pairs={{0,2},{1,3},{2,0},{3,1},{4,6},{5,7},{6,4},{7,5},{8,10},{9,11},{10,... | collective-permute-start | bytes 1572872 | tf_op jit(solution)/shard_map/ppermute | solution.py:369
  502.6 30.0 %collective-permute-start.57 = (bf16[128,2048]{1,0:T(8,128)(2,1)}, bf16[128,2048]{1,0:T(8,128)(2,1)S(1)}, u32[]{:S(2)}, u32[]{:S(2)}) collective-permute-start(bf16[128,2048]{1,0:T(8,128)(2,1)} %copy-done.6), channel_id=1, source_target_pairs={{0,2},{1,3},{2,0},{3,1},{4,6},{5,7},{6,4},{7,5},{8,10},{9,11},{10,... | collective-permute-start | bytes 1572872 | tf_op jit(solution)/shard_map/ppermute | solution.py:369
  503.3 32.5 %collective-permute-start.52 = (bf16[128,2048]{1,0:T(8,128)(2,1)}, bf16[128,2048]{1,0:T(8,128)(2,1)S(1)}, u32[]{:S(2)}, u32[]{:S(2)}) collective-permute-start(bf16[128,2048]{1,0:T(8,128)(2,1)} %copy-done.5), channel_id=1, source_target_pairs={{0,1},{1,0},{2,3},{3,2},{4,5},{5,4},{6,7},{7,6},{8,9},{9,8},{10,11... | collective-permute-start | bytes 1572872 | tf_op jit(solution)/shard_map/ppermute | solution.py:369
  511.5 22.5 %collective-permute-start.56 = (bf16[128,2048]{1,0:T(8,128)(2,1)S(1)}, bf16[128,2048]{1,0:T(8,128)(2,1)S(1)}, u32[]{:S(2)}, u32[]{:S(2)}) collective-permute-start(bf16[128,2048]{1,0:T(8,128)(2,1)S(1)} %add_convert_fusion.1), channel_id=1, source_target_pairs={{0,1},{1,0},{2,3},{3,2},{4,5},{5,4},{6,7},{7,6},{8,9},{9,8},{10,11... | collective-permute-start | bytes 1572872 | tf_op jit(solution)/shard_map/ppermute | solution.py:369
  514.5 29.4 %collective-permute-start.55 = (bf16[128,2048]{1,0:T(8,128)(2,1)S(1)}, bf16[128,2048]{1,0:T(8,128)(2,1)S(1)}, u32[]{:S(2)}, u32[]{:S(2)}) collective-permute-start(bf16[128,2048]{1,0:T(8,128)(2,1)S(1)} %add_convert_fusion.2), channel_id=1, source_target_pairs={{0,2},{1,3},{2,0},{3,1},{4,6},{5,7},{6,4},{7,5},{8,10},{9,11},{10,... | collective-permute-start | bytes 1572872 | tf_op jit(solution)/shard_map/ppermute | solution.py:369
  532.6 25.4 %collective-permute-start.46 = (bf16[128,2048]{1,0:T(8,128)(2,1)}, bf16[128,2048]{1,0:T(8,128)(2,1)}, u32[]{:S(2)}, u32[]{:S(2)}) collective-permute-start(bf16[128,2048]{1,0:T(8,128)(2,1)} %get-tuple-element.152), channel_id=1, source_target_pairs={{0,1},{1,0},{2,3},{3,2},{4,5},{5,4},{6,7},{7,6},{8,9},{9,8},{10,11... | collective-permute-start | bytes 1572872 | tf_op jit(solution)/shard_map/ppermute | solution.py:369
  534.1 20.0 %collective-permute-start.50 = (bf16[128,2048]{1,0:T(8,128)(2,1)}, bf16[128,2048]{1,0:T(8,128)(2,1)}, u32[]{:S(2)}, u32[]{:S(2)}) collective-permute-start(bf16[128,2048]{1,0:T(8,128)(2,1)} %add_convert_fusion.3), channel_id=1, source_target_pairs={{0,1},{1,0},{2,3},{3,2},{4,5},{5,4},{6,7},{7,6},{8,9},{9,8},{10,11... | collective-permute-start | bytes 1572872 | tf_op jit(solution)/shard_map/ppermute | solution.py:369
  535.8 22.2 %collective-permute-start.49 = (bf16[128,2048]{1,0:T(8,128)(2,1)}, bf16[128,2048]{1,0:T(8,128)(2,1)}, u32[]{:S(2)}, u32[]{:S(2)}) collective-permute-start(bf16[128,2048]{1,0:T(8,128)(2,1)} %add_convert_fusion.4), channel_id=1, source_target_pairs={{0,2},{1,3},{2,0},{3,1},{4,6},{5,7},{6,4},{7,5},{8,10},{9,11},{10,... | collective-permute-start | bytes 1572872 | tf_op jit(solution)/shard_map/ppermute | solution.py:369
  565.1 58.9 %collective-permute-start.69 = (f32[1,1,256]{2,1,0:T(1,128)S(1)}, f32[1,1,256]{2,1,0:T(1,128)S(1)}, u32[]{:S(2)}, u32[]{:S(2)}) collective-permute-start(f32[1,1,256]{2,1,0:T(1,128)S(1)} %constant_dynamic-slice_fusion), channel_id=1, source_target_pairs={{0,4},{4,0},{8,12},{12,8},{16,20},{20,16},{24,28},{28,24},{1,5},{5... | collective-permute-start | bytes 3080 | tf_op jit(solution)/shard_map/ppermute | solution.py:444
  565.1 60.0 %collective-permute-start.61 = (bf16[128,2048]{1,0:T(8,128)(2,1)}, bf16[128,2048]{1,0:T(8,128)(2,1)S(1)}, u32[]{:S(2)}, u32[]{:S(2)}) collective-permute-start(bf16[128,2048]{1,0:T(8,128)(2,1)} %reduce-scatter.8.cloned.1.call-done), channel_id=1, source_target_pairs={{0,0},{4,1},{8,10},{12,11},{16,16},{20,17},{24,26},{28,27},{1,4},{... | collective-permute-start | bytes 1572872 | tf_op jit(solution)/shard_map/ppermute | solution.py:416
  566.8 58.3 %collective-permute-start.62 = (bf16[128,2048]{1,0:T(8,128)(2,1)}, bf16[128,2048]{1,0:T(8,128)(2,1)S(1)}, u32[]{:S(2)}, u32[]{:S(2)}) collective-permute-start(bf16[128,2048]{1,0:T(8,128)(2,1)} %reduce-scatter.8.cloned.1.call-done), channel_id=1, source_target_pairs={{2,0},{6,1},{10,10},{14,11},{18,16},{22,17},{26,26},{30,27},{3,4},... | collective-permute-start | bytes 1572872 | tf_op jit(solution)/shard_map/ppermute | solution.py:416
  625.1 18.2 %collective-permute-start.63 = (bf16[128,2048]{1,0:T(8,128)(2,1)S(1)}, bf16[128,2048]{1,0:T(8,128)(2,1)S(1)}, u32[]{:S(2)}, u32[]{:S(2)}) collective-permute-start(bf16[128,2048]{1,0:T(8,128)(2,1)S(1)} %collective-permute-done.62), channel_id=1, source_target_pairs={{0,16},{1,17},{10,18},{11,19},{16,20},{17,21},{26,22},{27,23},{4,2... | collective-permute-start | bytes 1572872 | tf_op jit(solution)/shard_map/ppermute | solution.py:416
  (63 other events, 819.7 us)
Sparse Core Ops, SparseCore 0:
  35.3 122.7 all-gather.4
  160.3 47.1 all-gather.6
  209.7 80.7 all-gather.8
  338.7 92.7 reduce-scatter.3
  441.0 48.3 reduce-scatter.7
  491.6 127.4 reduce-scatter.5

commit v3 on v2

--- a/solution.py
+++ b/solution.py
@@ -245,23 +245,34 @@
     )(a, b)
 
 
-def feed_kernel(
-    steps, normed_ref, grad_ref, up_ref, down_ref, up_row_ref, hidden_ref, pre_ref, *out_refs
-):
+def feed_kernel(steps, parts, scale_ref, *refs):
+    normed_refs, grad_refs = refs[:parts], refs[parts : 2 * parts]
+    up_ref, down_ref, up_row_ref, hidden_ref, pre_ref = refs[2 * parts : 2 * parts + 5]
+    out_refs, (normed, grad) = refs[2 * parts + 5 : -2], refs[-2:]
     step = pl.program_id(0)
+
+    @pl.when(step == 0)
+    def _():
+        count = normed_refs[0].shape[0]
+        for n in range(parts):
+            normed[n * count : (n + 1) * count] = normed_refs[n][...]
+            grad[n * count : (n + 1) * count] = (
+                grad_refs[n][...].astype(F32) * scale_ref[0]
+            ).astype(BF16)
 
     @pl.when(step < steps)
     def _():
-        u = dot(normed_ref[...], up_ref[...])
-        d_hidden = dot(grad_ref[...], down_ref[...])
+        u = dot(normed[...], up_ref[...])
+        d_hidden = dot(grad[...], down_ref[...])
         scale = 0.7978845608028654
         square = u * u
         t = jnp.tanh(scale * u * (1.0 + 0.044715 * square))
         half = 0.5 * (1.0 + t)
-        hidden_ref[...] = (u * half).astype(BF16)
         slope = half + 0.5 * scale * u * (1.0 - t * t) * (1.0 + 3 * 0.044715 * square)
         tile = u.shape[1]
-        pre_ref[:, pl.ds(pl.multiple_of(step * tile, tile), tile)] = (d_hidden * slope).astype(BF16)
+        at = pl.ds(pl.multiple_of(step * tile, tile), tile)
+        hidden_ref[:, at] = (u * half).astype(BF16)
+        pre_ref[:, at] = (d_hidden * slope).astype(BF16)
 
     @pl.when(step >= steps)
     def _():
@@ -271,59 +282,66 @@
             out_ref[...] = result[n * count : (n + 1) * count].astype(BF16)
 
 
-def feed_call(normed, grad, both, parts):
-    rows, depth = normed.shape
-    width = both.shape[1] // 2
+def feed_call(normed, grad, row_scale, both):
+    parts, (count, depth) = len(normed), normed[0].shape
+    rows, width = parts * count, both.shape[1] // 2
     tile, out_tile = min(256, width), min(512, depth)
     steps, out_steps = width // tile, depth // out_tile
     first = lambda n: jnp.minimum(n, steps - 1)
     second = lambda n: jnp.maximum(n - steps, 0)
-    whole = pl.BlockSpec((rows, depth), lambda n: (0, 0))
+    piece = pl.BlockSpec((count, depth), lambda n: (0, 0), pipeline_mode=pl.Buffered(1))
+    whole = pl.BlockSpec((rows, width), lambda n: (0, 0))
     return pl.pallas_call(
-        functools.partial(feed_kernel, steps),
+        functools.partial(feed_kernel, steps, parts),
         grid=(steps + out_steps,),
-        in_specs=[
-            whole,
-            whole,
+        in_specs=[pl.BlockSpec(memory_space=pltpu.SMEM)]
+        + [piece] * (2 * parts)
+        + [
             pl.BlockSpec((depth, tile), lambda n: (0, first(n))),
             pl.BlockSpec((depth, tile), lambda n: (0, steps + first(n))),
             pl.BlockSpec((out_tile, width), lambda n: (second(n), 0)),
         ],
-        out_specs=[
-            pl.BlockSpec((rows, tile), lambda n: (0, first(n))),
-            pl.BlockSpec((rows, width), lambda n: (0, 0)),
-        ]
-        + [pl.BlockSpec((rows // parts, out_tile), lambda n: (0, second(n)))] * parts,
+        out_specs=[whole, whole]
+        + [pl.BlockSpec((count, out_tile), lambda n: (0, second(n)))] * parts,
         out_shape=[jax.ShapeDtypeStruct((rows, width), BF16)] * 2
-        + [jax.ShapeDtypeStruct((rows // parts, depth), BF16)] * parts,
+        + [jax.ShapeDtypeStruct((count, depth), BF16)] * parts,
+        scratch_shapes=[pltpu.VMEM((rows, depth), BF16)] * 2,
         compiler_params=pltpu.CompilerParams(vmem_limit_bytes=56 * 1024 * 1024),
         cost_estimate=pl.CostEstimate(
             flops=6 * rows * depth * width,
-            bytes_accessed=4 * (rows * depth + depth * width + rows * width),
+            bytes_accessed=4 * (rows * depth + 2 * depth * width + rows * width),
             transcendentals=rows * width,
         ),
         name="feed_forward",
-    )(normed, grad, both, both, both)
-
-
-def feed_grads_kernel(normed_ref, grad_ref, hidden_ref, pre_ref, out_ref):
-    width = hidden_ref.shape[1]
-    out_ref[:, :width] = contract_rows(normed_ref[...], pre_ref[...]).astype(BF16)
-    out_ref[:, width:] = contract_rows(grad_ref[...], hidden_ref[...]).astype(BF16)
-
-
-def feed_grads(normed, grad, hidden, d_pre):
-    rows, depth = normed.shape
-    width = hidden.shape[1]
+    )(row_scale.reshape(1), *normed, *grad, both, both, both)
+
+
+def feed_grads_kernel(parts, scale_ref, *refs):
+    normed_refs, grad_refs = refs[:parts], refs[parts : 2 * parts]
+    hidden_ref, pre_ref, out_ref, normed, grad = refs[2 * parts :]
+    count, width = normed_refs[0].shape[0], hidden_ref.shape[1]
+    for n in range(parts):
+        normed[n * count : (n + 1) * count] = normed_refs[n][...]
+        grad[n * count : (n + 1) * count] = (grad_refs[n][...].astype(F32) * scale_ref[0]).astype(
+            BF16
+        )
+    out_ref[:, :width] = contract_rows(normed[...], pre_ref[...]).astype(BF16)
+    out_ref[:, width:] = contract_rows(grad[...], hidden_ref[...]).astype(BF16)
+
+
+def feed_grads(normed, grad, row_scale, hidden, d_pre):
+    parts, (count, depth) = len(normed), normed[0].shape
+    rows, width = hidden.shape
     tile = min(512, depth)
-    slab = pl.BlockSpec((rows, tile), lambda n: (0, n))
+    slab = pl.BlockSpec((count, tile), lambda n: (0, n))
     whole = pl.BlockSpec((rows, width), lambda n: (0, 0))
     return pl.pallas_call(
-        feed_grads_kernel,
+        functools.partial(feed_grads_kernel, parts),
         grid=(depth // tile,),
-        in_specs=[slab, slab, whole, whole],
+        in_specs=[pl.BlockSpec(memory_space=pltpu.SMEM)] + [slab] * (2 * parts) + [whole, whole],
         out_specs=pl.BlockSpec((tile, 2 * width), lambda n: (n, 0)),
         out_shape=jax.ShapeDtypeStruct((depth, 2 * width), BF16),
+        scratch_shapes=[pltpu.VMEM((rows, tile), BF16)] * 2,
         compiler_params=pltpu.CompilerParams(vmem_limit_bytes=48 * 1024 * 1024),
         cost_estimate=pl.CostEstimate(
             flops=4 * rows * depth * width,
@@ -331,7 +349,7 @@
             transcendentals=0,
         ),
         name="feed_grads",
-    )(normed, grad, hidden, d_pre)
+    )(row_scale.reshape(1), *normed, *grad, hidden, d_pre)
 
 
 def on_device(
@@ -369,14 +387,22 @@
         return lax.ppermute(x, "mp", [(s, s ^ mask) for s in range(mp)])
 
     def spread(x):
+        return spread_end(spread_start(x))
+
+    def spread_start(x):
         if not square:
-            return jnp.concatenate([swap(x, m) for m in masks], axis=0)
+            return [swap(x, m) for m in masks]
         half = x.shape[0] // 2
         a, b = x[:half], x[half:]
         a1, b2 = swap(a, 1), swap(b, 2)
         a2, b1 = swap(a, 2), swap(b, 1)
-        a3, b3 = swap(a1, 2), swap(b2, 1)
-        return jnp.concatenate([a, b, a1, b1, a2, b2, a3, b3], axis=0)
+        return [a, b, a1, b1, a2, b2]
+
+    def spread_end(groups):
+        if not square:
+            return groups
+        a1, b2 = groups[2], groups[5]
+        return groups + [swap(a1, 2), swap(b2, 1)]
 
     def collect(pieces, meanwhile=()):
         if not square:
@@ -399,37 +425,38 @@
         )
         return total, meanwhile
 
-    def shuffle(x, back=False):
-        flat = [(b, (b % dp) * mp + b // dp) for b in range(dp * mp)]
-        if not (dp == 8 and square):
-            pairs = [(d, s) for s, d in flat] if back else flat
-            return lambda late: lax.ppermute(x, ("dp", "mp"), pairs)
-        first, second = ([], []), ([], [])
-        for z in range(4):
-            for c in range(2):
-                for j in range(4):
-                    plane = 2 * c + j // 2
-                    start, middle = (2 * z + c) * 4 + j, (2 * plane + z % 2) * 4 + j
-                    first[z // 2].append((start, middle))
-                    second[z // 2].append((middle, (2 * plane + j % 2) * 4 + z))
-        flipped = lambda pairs: [(d, s) for s, d in pairs]
-        move = lambda v, pairs: lax.ppermute(v, ("dp", "mp"), pairs)
-        if not back:
-            low, high = (move(x, pairs) for pairs in first)
-
-            def finish(late):
-                a, b, late = together((low, high, late))
-                return jnp.where(here < 2, move(a, second[0]), move(b, second[1]))
-
-            return finish
-        low, high = (move(x, flipped(pairs)) for pairs in second)
-        upper = lax.axis_index("dp") >= 4
-
-        def finish_back(late):
-            a, b, late = together((low, high, late))
-            return jnp.where(upper, move(b, flipped(first[1])), move(a, flipped(first[0])))
-
-        return finish_back
+    def gather_start(x):
+        if dp != 8:
+            return (x,), lambda arrived, meanwhile: (
+                lax.all_gather(arrived[0], "dp", axis=0, tiled=True),
+                meanwhile,
+            )
+        index = lax.axis_index("dp")
+        core, place = index % 2, index // 2
+        move = lambda v, pairs: lax.ppermute(
+            v, "dp", [(2 * s + c, 2 * d + c) for s, d in pairs for c in range(2)]
+        )
+        above = move(x, [(1, 0), (2, 1), (3, 2)])
+        below = move(x, [(0, 1), (1, 2), (2, 3)])
+        across = move(x, [(0, 3), (3, 0)])
+
+        def finish(arrived, meanwhile):
+            above, below, across = arrived
+            onward = jnp.where(place == 1, above, jnp.where(place == 2, below, x))
+            over = move(onward, [(0, 2), (3, 1), (2, 3), (1, 0)])
+            over, meanwhile = together((over, meanwhile))
+            by_place = []
+            for k in range(4):
+                apart = place - k
+                far = jnp.where(abs(apart) == 3, across, over)
+                near = jnp.where(apart == 1, below, jnp.where(apart == -1, above, far))
+                by_place.append(jnp.where(apart == 0, x, near))
+            mine = jnp.stack(by_place)
+            other = lax.ppermute(mine, "dp", [(s, s ^ 1) for s in range(dp)])
+            both = [jnp.where(core == 0, mine, other), jnp.where(core == 0, other, mine)]
+            return jnp.stack(both, axis=1).reshape(dp * x.shape[0], x.shape[1]), meanwhile
+
+        return (above, below, across), finish
 
     def scatter_small(x):
         cur = x.reshape(dp, mp, x.shape[-1])
@@ -454,8 +481,8 @@
         [retention_gain, retention_bias, feedfwd_gain, feedfwd_bias]
         + [jnp.broadcast_to(domain.astype(BF16), (part,))]
     )
-    thin = lax.all_gather(thin[None], "dp", axis=0, tiled=True)
-
+    strip, thin_size = output_weight.shape[0], thin.shape[0]
+    thin = jnp.pad(thin[None], ((0, 15), (0, output_weight.shape[1] - thin_size)))
     def columns(weight, target):
         width = weight.shape[1] // mp
         return lax.dynamic_slice(weight, (0, target * width), (part, width))
@@ -469,18 +496,32 @@
                 axis=1,
             )
         )
-    *pieces, thin = together((*(swap(pieces[m], m) for m in masks), thin))
+    pieces, output_weight, thin = together((pieces, output_weight, thin))
+    pieces = [swap(pieces[m], m) for m in masks]
+    arrived, finish = gather_start(jnp.concatenate([output_weight, thin], axis=0))
+    pieces, arrived = together((pieces, arrived))
     packed = jnp.concatenate(by_index(pieces), axis=0)
     w_in = lax.all_gather(packed, "dp", axis=0, tiled=True)
-
-    finish = shuffle(output_weight)
-    tokens_late, cotangent_late, packed = together((tokens, cotangent, packed))
+    tokens_late, packed = together((tokens, packed))
+    w_out, source_rows = finish(arrived, spread_start(tokens_late))
+    source_rows = spread_end(source_rows)
+    w_out = w_out.reshape(dp, strip + 16, -1)
+    thin = w_out[:, strip, :thin_size]
+    w_out = w_out[:, :strip].reshape(dp * strip, -1)
     thin = jnp.stack(by_index([swap(thin, m) for m in masks]))
-    source_rows = spread(tokens_late)
-    cotan_rows = spread(cotangent_late)
-    shuffled = finish(packed)
     thin = thin.reshape(mp, dp, 5, part).transpose(2, 1, 0, 3).reshape(5, dp * own)
     gain_one, bias_one, gain_two, bias_two = (thin[n].astype(F32)[None] for n in range(4))
+
+    w_out, *source_rows = together((w_out, *source_rows))
+    group = w_out.shape[0] // mp
+    w_out = [
+        lax.dynamic_slice_in_dim(w_out, (here ^ m) * group, group, 0) for m in masks
+    ]
+    w_out = by_index([swap(w_out[m], m) for m in masks])
+    cotangent_late, *w_out = together((cotangent, *w_out))
+    cotan_rows = spread(cotangent_late)
+    w_out = jnp.stack([w.reshape(group // strip, strip, -1) for w in w_out], axis=1)
+    w_out = w_out.reshape(group * mp, -1)
 
     domains = thin[4, ::own]
     own_count = jnp.sum((domains == domain[0].astype(BF16)).astype(F32)) * (rows * mp)
@@ -493,11 +534,9 @@
         + jnp.arange(rows // SPAN, dtype=jnp.int32)[None]
     ).reshape(-1)
 
-    normal_rows, _ = layer_stats(source_rows.astype(F32))
+    normal_rows, _ = layer_stats(jnp.concatenate(source_rows, axis=0).astype(F32))
     normed_one = (normal_rows * gain_one + bias_one).astype(BF16)
-    grad_rows = (cotan_rows.astype(F32) * row_scale).astype(BF16)
-    normed_one, grad_rows, tables, decay = together((normed_one, grad_rows, tables, decay))
-    w_out = lax.all_gather(shuffled, "dp", axis=0, tiled=True)
+    normed_one, tables, decay, w_out = together((normed_one, tables, decay, w_out))
     w_feed = lax.all_gather(
         jnp.concatenate([up_weight, down_weight.T], axis=1), "dp", axis=0, tiled=True
     )
@@ -505,14 +544,15 @@
     pre = dot(normed_one, w_in)
     gated, state_low = retention_call(heads, blocks, block_order, pre, tables, decay, ())
 
+    gated, cotan_rows = together((gated, cotan_rows))
     source = tokens.astype(F32)
     middle = source + collect(row_product(gated, w_out, False, parts))[0]
     normal_two, factor_two = layer_stats(middle)
     normed_two = (normal_two * gain_two + bias_two).astype(BF16)
     normed_rows = spread(normed_two)
-    hidden, d_pre, *pieces = feed_call(normed_rows, grad_rows, w_feed, parts)
+    hidden, d_pre, *pieces = feed_call(normed_rows, cotan_rows, row_scale, w_feed)
     *pieces, hidden, d_pre = together((*pieces, hidden, d_pre))
-    feed_part = feed_grads(normed_rows, grad_rows, hidden, d_pre)
+    feed_part = feed_grads(normed_rows, cotan_rows, row_scale, hidden, d_pre)
     d_normed_two, feed_part = collect(pieces, feed_part)
     scatter = functools.partial(
         lax.psum_scatter, axis_name="dp", scatter_dimension=0, tiled=True
@@ -521,29 +561,39 @@
 
     cotan = cotangent.astype(F32) * row_scale
     d_middle = cotan + layer_back(d_normed_two * gain_two, normal_two, factor_two)
-    branch_rows = spread(d_middle.astype(BF16))
+    branch_rows = jnp.concatenate(spread(d_middle.astype(BF16)), axis=0)
     d_gated = contract_cols(branch_rows, w_out)
     d_in = retention_call(
         heads, blocks, block_order, pre, tables, decay, (state_low, d_gated)
     )
-    d_in, branch_rows, feed_grad = together((d_in, branch_rows, feed_grad))
+    in_part = contract_rows(normed_one, d_in).astype(BF16)
+    in_part, gated, feed_grad = together((in_part, gated, feed_grad))
+    in_grad = scatter(in_part)
     output_part = contract_rows(gated, branch_rows).astype(BF16)
-    d_in, output_part = together((d_in, output_part))
-    in_part = contract_rows(normed_one, d_in).astype(BF16)
-    d_in, in_part, hidden = together((d_in, in_part, hidden))
-    d_normed_one, _ = collect(row_product(d_in, w_in, True, parts))
+    output_part = output_part.reshape(group // strip, mp, strip, -1)
+    pieces = [
+        lax.dynamic_index_in_dim(output_part, here ^ m, 1, keepdims=False).reshape(group, -1)
+        for m in masks
+    ]
+    *pieces, d_in = together((*pieces, d_in))
+    output_pieces = [swap(pieces[m], m) for m in masks]
+    *pieces, hidden = together((*row_product(d_in, w_in, True, parts), hidden))
+    feed_pieces = row_product(hidden, w_feed, True, parts, 1)
+    output_pieces, pieces, feed_pieces = together((output_pieces, pieces, feed_pieces))
+    output_part = jnp.concatenate(by_index(output_pieces), axis=0)
+    d_normed_one, output_part = collect(pieces, output_part)
+    d_normed_one, feed_pieces = together((d_normed_one, feed_pieces))
     normal_one, factor_one = layer_stats(source)
     d_tokens = d_middle + layer_back(d_normed_one * gain_one, normal_one, factor_one)
 
-    feed_sum, _ = collect(row_product(hidden, w_feed, True, parts, 1))
+    feed_sum, _ = collect(feed_pieces)
     outputs = (middle + feed_sum).astype(BF16)
 
     width = up_weight.shape[1]
     up_grad = feed_grad[:, :width].astype(F32)
     down_grad = feed_grad[:, width:].astype(F32).T
-    finish = shuffle(scatter(output_part), True)
-    in_grad = scatter(in_part)
-    output_grad = finish(in_grad).astype(F32)
+    output_part, in_grad, outputs, d_tokens = together((output_part, in_grad, outputs, d_tokens))
+    output_grad = scatter(output_part).astype(F32)
     pieces = by_index([in_grad[m * part : (m + 1) * part] for m in masks])
     pieces = by_index([swap(pieces[m], m) for m in masks])
     grads, at = [], 0

time: 662 us -> 619 us (0.935)
  blocking collectives: 16.5 us -> 0 us
  local copies, waits for them, and re-layouts: 40.3 us -> 26.9 us
  waiting for transfers between devices: 285 us -> 272 us
    ppermute x57 -> x63, waiting for transfers between devices: 176 us -> 246 us  [swap(): return lax.ppermute(x, 'mp', [(s, s ^ mask) for s in range(mp)])]
    reduce_scatter x1, waiting for transfers between devices: 51 us -> 5.75 us  [on_device(): in_grad = scatter(in_part)]
    ppermute x8 -> x5, waiting for transfers between devices: 37.6 us -> 3.39 us  [the longest x4 3.39 us: gather_start(): lax.ppermute(v, 'dp', [(2 * s + c, 2 * d + c) for s, d in pairs for c in...]
    unnamed x1 -> x0, blocking collectives: 16.5 us -> none
    unnamed x97 -> x126, local copies, waits for them, and re-layouts: 28.7 us -> 15.2 us
    another operation x0 -> x6, other arithmetic: none -> 10.6 us  [the longest x3 4.98 us: finish(): mine = jnp.stack(by_place)]
    reduce_scatter x1, waiting for transfers between devices: 9.8 us -> 0.01 us  [on_device(): feed_grad = scatter(feed_part)]
    reduce_scatter x1, waiting for transfers between devices: 0.02 us -> 8.05 us  [on_device(): output_grad = scatter(output_part).astype(F32)]
  transfers between devices with their start and end apart: 76 -> 78, of which waited for: 35 -> 41; matrix products, arithmetic and copies ran while one was open for 20% -> 20% of each run, Pallas kernels for 11% -> 12%
where the time goes in v3:
time: 619 us; the launch traced here: 613 us
  waiting for transfers between devices  272 us (44%)
  Pallas kernels  97.4 us (16%)
  starting transfers between devices  84.6 us (14%)
  other arithmetic  62.6 us (10%)
  matrix products  51.7 us (8%)
  local copies, waits for them, and re-layouts  26.9 us (4%)
  between operations  17 us (3%)
    ppermute x63, waiting for transfers between devices, swap(): return lax.ppermute(x, 'mp', [(s, s ^ mask) for s in range(mp)])  246 us
    ppermute x63, starting transfers between devices, swap(): return lax.ppermute(x, 'mp', [(s, s ^ mask) for s in range(mp)])  68.6 us
    pallas_call x3, Pallas kernels, row_product(): pl.pallas_call(functools.partial(product_kernel, ((1,), (1 if transposed...  34.5 us
    dot_general x2, matrix products, contract_rows(): lax.dot_general(left, right, (((0,), (0,)), ((), ())), preferred_element_...  25.5 us
    pallas_call x1, Pallas kernels, feed_call(): pl.pallas_call(functools.partial(feed_kernel, steps, parts), grid=(steps...  25 us
    pallas_call x2, Pallas kernels, retention_call(): pl.pallas_call(functools.partial(body, heads), grid_spec=pltpu.PrefetchSc...  23.9 us
    dot_general x1, matrix products, dot(): return jnp.dot(left, right, preferred_element_type=F32)  20.1 us
    unnamed x126, local copies, waits for them, and re-layouts  15.2 us
  transfers between devices with their start and end apart: 78, of which 41 were waited for; matrix products, arithmetic and copies ran while one was open for 20% of the time, Pallas kernels for 12%

profile of v3, /device:TPU:0, one launch (start us, length us, event | category | flops | bytes accessed | tf_op | source)
XLA Modules:
  0.0 612.7 jit_solution(1425173826767091687)
XLA Ops:
  13.9 2.9 collective-permute-start
  18.2 4.6 collective-permute-start.4
  22.8 3.3 collective-permute-start.5
  28.6 16.2 %collective-permute-done.1 = bf16[64,3072]{1,0:T(8,128)(2,1)S(1)} collective-permute-done((bf16[64,3072]{1,0:T(8,128)(2,1)}, bf16[64,3072]{1,0:T(8,128)(2,1)S(1)}, u32[]{:S(2)}, u32[]{:S(2)}) %collective-permute-start.1) | collective-permute-done | bytes 393248 | tf_op jit(solution)/shard_map/ppermute | solution.py:387
  44.8 3.4 collective-permute-done.5
  59.8 11.0 %collective-permute-done.7 = bf16[128,2048]{1,0:T(8,128)(2,1)S(1)} collective-permute-done((bf16[128,2048]{1,0:T(8,128)(2,1)}, bf16[128,2048]{1,0:T(8,128)(2,1)S(1)}, u32[]{:S(2)}, u32[]{:S(2)}) %collective-permute-start.7) | collective-permute-done | bytes 524320 | tf_op jit(solution)/shard_map/ppermute | solution.py:387
  70.8 6.6 %collective-permute-done.8 = bf16[128,2048]{1,0:T(8,128)(2,1)S(1)} collective-permute-done((bf16[128,2048]{1,0:T(8,128)(2,1)}, bf16[128,2048]{1,0:T(8,128)(2,1)S(1)}, u32[]{:S(2)}, u32[]{:S(2)}) %collective-permute-start.8) | collective-permute-done | bytes 524320 | tf_op jit(solution)/shard_map/ppermute | solution.py:387
  92.1 2.8 select_bitcast_fusion.1
  99.0 5.6 collective-permute-done.12
  118.2 37.9 %collective-permute-done.14 = bf16[8,320]{1,0:T(8,128)(2,1)S(1)} collective-permute-done((bf16[8,320]{1,0:T(8,128)(2,1)S(1)}, bf16[8,320]{1,0:T(8,128)(2,1)S(1)}, u32[]{:S(2)}, u32[]{:S(2)}) %collective-permute-start.14) | collective-permute-done | bytes 5152 | tf_op jit(solution)/shard_map/ppermute | solution.py:387
  162.1 3.2 fusion.5
  169.7 5.4 collective-permute-done.20.refs_10_
  177.1 20.1 %fusion.40.pre_ref = f32[1024,3072]{1,0:T(8,128)} fusion(bf16[1024,2048]{1,0:T(8,128)(2,1)} %fusion.5, bf16[2048,3072]{1,0:T(8,128)(2,1)} %all-gather.3.cloned.1.call-done.b_ref), kind=kOutput, calls=%fused_computation.218 | convolution fusion | flops 12884901888 | bytes 29360128 | tf_op jit(solution)/shard_map/dot_general | solution.py:50
  197.2 8.3 %retention_forward.1 = (bf16[1024,1024]{1,0:T(8,128)(2,1)S(1)}, bf16[4,2,256,512]{3,2,1,0:T(8,128)(2,1)}) custom-call(s32[4]{0:T(128)S(1)} %iota_xor_fusion.order_ref, f32[2]{0:T(128)S(1)} %get-tuple-element.206.block_ref, f32[1024,3072]{1,0:T(8,128)} %fusion.40.pre_ref, f32[1024,128]{1,0:T(8,128)S(1)} %get-tuple-element.207.cos_ref, ...), custom_call_target="tpu_custom_call" | custom-call | flops 1879048192 | bytes 15728640 | tf_op jit(solution)/shard_map/retention_forward/pallas_call | solution.py:197
  206.8 8.2 %row_product.3 = (bf16[128,2048]{1,0:T(8,128)(2,1)S(1)}, bf16[128,2048]{1,0:T(8,128)(2,1)S(1)}, bf16[128,2048]{1,0:T(8,128)(2,1)}, bf16[128,2048]{1,0:T(8,128)(2...) custom-call(bf16[1024,1024]{1,0:T(8,128)(2,1)} %copy-done.11, ...), custom_call_target="tpu_custom_call" | custom-call | flops 4294967296 | bytes 10485760 | tf_op jit(solution)/shard_map/row_product/pallas_call | solution.py:232
  219.4 10.5 %collective-permute-done.27 = bf16[128,2048]{1,0:T(8,128)(2,1)S(1)} collective-permute-done((bf16[128,2048]{1,0:T(8,128)(2,1)S(1)}, bf16[128,2048]{1,0:T(8,128)(2,1)S(1)}, u32[]{:S(2)}, u32[]{:S(2)}) %collective-permute-start.27) | collective-permute-done | bytes 524320 | tf_op jit(solution)/shard_map/ppermute | solution.py:387
  235.3 7.3 %collective-permute-done.31 = bf16[128,2048]{1,0:T(8,128)(2,1)} collective-permute-done((bf16[128,2048]{1,0:T(8,128)(2,1)}, bf16[128,2048]{1,0:T(8,128)(2,1)}, u32[]{:S(2)}, u32[]{:S(2)}) %collective-permute-start.31) | collective-permute-done | bytes 524320 | tf_op jit(solution)/shard_map/ppermute | solution.py:387
  242.6 4.7 collective-permute-done.30
  256.4 10.9 %collective-permute-done.32.refs_2_ = bf16[128,2048]{1,0:T(8,128)(2,1)} collective-permute-done((bf16[128,2048]{1,0:T(8,128)(2,1)S(1)}, bf16[128,2048]{1,0:T(8,128)(2,1)}, u32[]{:S(2)}, u32[]{:S(2)}) %collective-permute-start.32) | collective-permute-done | bytes 524320 | tf_op jit(solution)/shard_map/ppermute | solution.py:387
  271.0 7.1 %collective-permute-done.33.refs_3_ = bf16[128,2048]{1,0:T(8,128)(2,1)} collective-permute-done((bf16[128,2048]{1,0:T(8,128)(2,1)S(1)}, bf16[128,2048]{1,0:T(8,128)(2,1)}, u32[]{:S(2)}, u32[]{:S(2)}) %collective-permute-start.33) | collective-permute-done | bytes 524320 | tf_op jit(solution)/shard_map/ppermute | solution.py:387
  279.3 5.6 collective-permute-done.36.refs_6_
  285.0 25.0 %feed_forward.1 = (bf16[1024,1024]{1,0:T(8,128)(2,1)}, bf16[1024,1024]{1,0:T(8,128)(2,1)}, bf16[128,2048]{1,0:T(8,128)(2,1)}, bf16[128,2048]{1,0:T(8,128)(2,1)},...) custom-call(f32[1]{0:T(128)} %bitcast.36.scale_ref, ...), custom_call_target="tpu_custom_call" | custom-call | flops 12884901888 | bytes 29360128 | tf_op jit(solution)/shard_map/feed_forward/pallas_call | solution.py:294
  314.7 14.0 %feed_grads.1 = bf16[2048,2048]{1,0:T(8,128)(2,1)} custom-call(f32[1]{0:T(128)} %bitcast.36.scale_ref, bf16[128,2048]{1,0:T(8,128)(2,1)S(1)} %copy-done.10, bf16[128,2048]{1,0:T(8,128)(2,1)S(1)} %copy-done.8, bf16[128,2048]{1,0:T(8,128)(2,1)} %collective-permute-done.32.refs_2_, bf16[128,2048]{1,0:T(8,128)(2,1)} %collective-permute-done.33.refs_3_, ...), custom_call_target="tpu_custom_call" | custom-call | flops 8589934592 | bytes 20971520 | tf_op jit(solution)/shard_map/feed_grads/pallas_call | solution.py:338
  336.6 6.4 %collective-permute-done.43 = bf16[128,2048]{1,0:T(8,128)(2,1)S(1)} collective-permute-done((bf16[128,2048]{1,0:T(8,128)(2,1)}, bf16[128,2048]{1,0:T(8,128)(2,1)S(1)}, u32[]{:S(2)}, u32[]{:S(2)}) %collective-permute-start.43) | collective-permute-done | bytes 524320 | tf_op jit(solution)/shard_map/ppermute | solution.py:387
  343.0 6.4 %collective-permute-done.42 = bf16[128,2048]{1,0:T(8,128)(2,1)S(1)} collective-permute-done((bf16[128,2048]{1,0:T(8,128)(2,1)S(1)}, bf16[128,2048]{1,0:T(8,128)(2,1)S(1)}, u32[]{:S(2)}, u32[]{:S(2)}) %collective-permute-start.42) | collective-permute-done | bytes 524320 | tf_op jit(solution)/shard_map/ppermute | solution.py:387
  357.7 10.8 %collective-permute-done.44 = bf16[128,2048]{1,0:T(8,128)(2,1)S(1)} collective-permute-done((bf16[128,2048]{1,0:T(8,128)(2,1)S(1)}, bf16[128,2048]{1,0:T(8,128)(2,1)S(1)}, u32[]{:S(2)}, u32[]{:S(2)}) %collective-permute-start.44) | collective-permute-done | bytes 524320 | tf_op jit(solution)/shard_map/ppermute | solution.py:387
  370.8 6.0 collective-permute-done.45
  376.9 5.4 collective-permute-done.48
  382.5 6.1 fusion.41.grad_ref
  388.6 15.6 %retention_backward.1.a_ref = bf16[1024,3072]{1,0:T(8,128)(2,1)} custom-call(s32[4]{0:T(128)S(1)} %iota_xor_fusion.order_ref, f32[2]{0:T(128)S(1)} %get-tuple-element.206.block_ref, f32[1024,3072]{1,0:T(8,128)} %fusion.40.pre_ref, f32[1024,128]{1,0:T(8,128)S(1)} %get-tuple-element.207.cos_ref, f32[1024,128]{1,0:T(8,128)S(1)} %get-tuple-element.208.sin_ref, ...), custom_call_target="tpu_custom_call" | custom-call | flops 4026531840 | bytes 18874368 | tf_op jit(solution)/shard_map/retention_backward/pallas_call | solution.py:197
  404.2 18.5 %convolution_convert_fusion = bf16[2048,3072]{1,0:T(8,128)(2,1)} fusion(bf16[1024,2048]{1,0:T(8,128)(2,1)S(1)} %copy-done.35, bf16[1024,3072]{1,0:T(8,128)(2,1)} %retention_backward.1.a_ref), kind=kOutput, calls=%fused_computation | convolution fusion | flops 12891193344 | bytes 23068672 | tf_op jit(solution)/shard_map/dot_general | solution.py:54
  424.3 7.0 %convolution_convert_fusion.1 = bf16[1024,2048]{1,0:T(8,128)(2,1)S(1)} fusion(bf16[1024,1024]{1,0:T(8,128)(2,1)S(1)} %copy-done.12, bf16[1024,2048]{1,0:T(8,128)(2,1)} %copy-done.50), kind=kOutput, calls=%fused_computation.14 | convolution fusion | flops 4297064448 | bytes 10485760 | tf_op jit(solution)/shard_map/dot_general | solution.py:54
  435.2 18.5 %row_product.4 = (bf16[128,2048]{1,0:T(8,128)(2,1)S(1)}, bf16[128,2048]{1,0:T(8,128)(2,1)S(1)}, bf16[128,2048]{1,0:T(8,128)(2,1)}, bf16[128,2048]{1,0:T(8,128)(2...) custom-call(bf16[1024,3072]{1,0:T(8,128)(2,1)} %retention_backward.1, ...), custom_call_target="tpu_custom_call" | custom-call | flops 12884901888 | bytes 23068672 | tf_op jit(solution)/shard_map/row_product/pallas_call | solution.py:232
  453.7 7.8 %row_product.5 = (bf16[128,2048]{1,0:T(8,128)(2,1)S(1)}, bf16[128,2048]{1,0:T(8,128)(2,1)S(1)}, bf16[128,2048]{1,0:T(8,128)(2,1)S(1)}, bf16[128,2048]{1,0:T(8,12...) custom-call(bf16[1024,1024]{1,0:T(8,128)(2,1)} %get-tuple-element.28, ...), custom_call_target="tpu_custom_call" | custom-call | flops 4294967296 | bytes 10485760 | tf_op jit(solution)/shard_map/row_product/pallas_call | solution.py:232
  461.6 8.2 %collective-permute-done.51 = bf16[256,2048]{1,0:T(8,128)(2,1)S(1)} collective-permute-done((bf16[256,2048]{1,0:T(8,128)(2,1)S(1)}, bf16[256,2048]{1,0:T(8,128)(2,1)S(1)}, u32[]{:S(2)}, u32[]{:S(2)}) %collective-permute-start.51) | collective-permute-done | bytes 1048608 | tf_op jit(solution)/shard_map/ppermute | solution.py:387
  469.8 8.3 %collective-permute-done.52 = bf16[256,2048]{1,0:T(8,128)(2,1)S(1)} collective-permute-done((bf16[256,2048]{1,0:T(8,128)(2,1)S(1)}, bf16[256,2048]{1,0:T(8,128)(2,1)S(1)}, u32[]{:S(2)}, u32[]{:S(2)}) %collective-permute-start.52) | collective-permute-done | bytes 1048608 | tf_op jit(solution)/shard_map/ppermute | solution.py:387
  485.9 7.4 %collective-permute-done.53 = bf16[128,2048]{1,0:T(8,128)(2,1)} collective-permute-done((bf16[128,2048]{1,0:T(8,128)(2,1)}, bf16[128,2048]{1,0:T(8,128)(2,1)}, u32[]{:S(2)}, u32[]{:S(2)}) %collective-permute-start.53) | collective-permute-done | bytes 524320 | tf_op jit(solution)/shard_map/ppermute | solution.py:387
  498.1 3.5 collective-permute-done.58
  501.6 4.5 collective-permute-done.57
  507.4 3.7 collective-permute-done.56
  518.6 4.2 collective-permute-done.60
  522.8 12.1 %collective-permute-done.61 = bf16[128,2048]{1,0:T(8,128)(2,1)S(1)} collective-permute-done((bf16[128,2048]{1,0:T(8,128)(2,1)S(1)}, bf16[128,2048]{1,0:T(8,128)(2,1)S(1)}, u32[]{:S(2)}, u32[]{:S(2)}) %collective-permute-start.61) | collective-permute-done | bytes 524320 | tf_op jit(solution)/shard_map/ppermute | solution.py:387
  538.7 5.6 collective-permute-done.63
  547.5 5.7 reduce-scatter.6.cloned.1.call-done
  561.6 4.6 collective-permute-done.70
  574.8 8.8 %collective-permute-done.67 = bf16[64,3072]{1,0:T(8,128)(2,1)S(1)} collective-permute-done((bf16[64,3072]{1,0:T(8,128)(2,1)S(1)}, bf16[64,3072]{1,0:T(8,128)(2,1)S(1)}, u32[]{:S(2)}, u32[]{:S(2)}) %collective-permute-start.67) | collective-permute-done | bytes 393248 | tf_op jit(solution)/shard_map/ppermute | solution.py:387
  583.5 8.0 %collective-permute-done.66 = bf16[64,3072]{1,0:T(8,128)(2,1)S(1)} collective-permute-done((bf16[64,3072]{1,0:T(8,128)(2,1)S(1)}, bf16[64,3072]{1,0:T(8,128)(2,1)S(1)}, u32[]{:S(2)}, u32[]{:S(2)}) %collective-permute-start.66) | collective-permute-done | bytes 393248 | tf_op jit(solution)/shard_map/ppermute | solution.py:387
  595.8 8.0 %reduce-scatter.8.cloned.1.call-done = bf16[128,2048]{1,0:T(8,128)(2,1)} async-done(((bf16[1024,2048]{1,0:T(8,128)(2,1)}), bf16[128,2048]{1,0:T(8,128)(2,1)}) %reduce-scatter.8.cloned.1.call-update) | async-done | bytes 524304 | tf_op jit(solution)/shard_map/reduce_scatter | solution.py:596
  (392 shorter events, 170.1 us)
Async XLA Ops:
  7.2 169.9 %all-gather.3.cloned.1.call-start = ((), (), s32[]{:S(2)}) async-start(), calls=%async_computation.3 | async-start | bytes 14155776 | tf_op jit(solution)/shard_map/all_gather | solution.py:504
  16.9 27.9 %collective-permute-start.3 = (bf16[144,2048]{1,0:T(8,128)(2,1)S(1)}, bf16[144,2048]{1,0:T(8,128)(2,1)S(1)}, u32[]{:S(2)}, u32[]{:S(2)}) collective-permute-start(bf16[144,2048]{1,0:T(8,128)(2,1)S(1)} %constant_dynamic-update-slice_fusion), channel_id=1, source_target_pairs={{8,0},{12,4},{16,8},{20,12},{24,16},{28,20},{9,1},{13,5},{17,9},{2... | collective-permute-start | bytes 1769480 | tf_op jit(solution)/shard_map/ppermute | solution.py:436
  18.2 26.6 %collective-permute-start.4 = (bf16[144,2048]{1,0:T(8,128)(2,1)S(1)}, bf16[144,2048]{1,0:T(8,128)(2,1)S(1)}, u32[]{:S(2)}, u32[]{:S(2)}) collective-permute-start(bf16[144,2048]{1,0:T(8,128)(2,1)S(1)} %constant_dynamic-update-slice_fusion), channel_id=1, source_target_pairs={{0,8},{4,12},{8,16},{12,20},{16,24},{20,28},{1,9},{5,13},{9,17},{1... | collective-permute-start | bytes 1769480 | tf_op jit(solution)/shard_map/ppermute | solution.py:436
  22.8 25.5 %collective-permute-start.5 = (bf16[144,2048]{1,0:T(8,128)(2,1)S(1)}, bf16[144,2048]{1,0:T(8,128)(2,1)S(1)}, u32[]{:S(2)}, u32[]{:S(2)}) collective-permute-start(bf16[144,2048]{1,0:T(8,128)(2,1)S(1)} %constant_dynamic-update-slice_fusion), channel_id=1, source_target_pairs={{0,24},{4,28},{24,0},{28,4},{1,25},{5,29},{25,1},{29,5},{2,26},{6,... | collective-permute-start | bytes 1769480 | tf_op jit(solution)/shard_map/ppermute | solution.py:436
  26.1 18.7 %collective-permute-start.1 = (bf16[64,3072]{1,0:T(8,128)(2,1)}, bf16[64,3072]{1,0:T(8,128)(2,1)S(1)}, u32[]{:S(2)}, u32[]{:S(2)}) collective-permute-start(bf16[64,3072]{1,0:T(8,128)(2,1)} %pad_maximum_fusion.15), channel_id=1, source_target_pairs={{0,2},{1,3},{2,0},{3,1},{4,6},{5,7},{6,4},{7,5},{8,10},{9,11},{10,... | collective-permute-start | bytes 1179656 | tf_op jit(solution)/shard_map/ppermute | solution.py:387
  27.7 17.1 %collective-permute-start.2 = (bf16[64,3072]{1,0:T(8,128)(2,1)}, bf16[64,3072]{1,0:T(8,128)(2,1)}, u32[]{:S(2)}, u32[]{:S(2)}) collective-permute-start(bf16[64,3072]{1,0:T(8,128)(2,1)} %pad_maximum_fusion.16), channel_id=1, source_target_pairs={{0,3},{1,2},{2,1},{3,0},{4,7},{5,6},{6,5},{7,4},{8,11},{9,10},{10,... | collective-permute-start | bytes 1179656 | tf_op jit(solution)/shard_map/ppermute | solution.py:387
  51.0 220.0 %all-gather.5.cloned.1.call-start = ((), (), s32[]{:S(2)}) async-start(), calls=%async_computation.4 | async-start | bytes 9437184 | tf_op jit(solution)/shard_map/all_gather | solution.py:540
  52.0 27.0 %collective-permute-start.6 = (bf16[144,2048]{1,0:T(8,128)(2,1)}, bf16[144,2048]{1,0:T(8,128)(2,1)}, u32[]{:S(2)}, u32[]{:S(2)}) collective-permute-start(bf16[144,2048]{1,0:T(8,128)(2,1)} %select_select_fusion), channel_id=1, source_target_pairs={{0,16},{4,20},{24,8},{28,12},{16,24},{20,28},{8,0},{12,4},{1,17},{... | collective-permute-start | bytes 1769480 | tf_op jit(solution)/shard_map/ppermute | solution.py:436
  56.3 21.1 %collective-permute-start.8 = (bf16[128,2048]{1,0:T(8,128)(2,1)}, bf16[128,2048]{1,0:T(8,128)(2,1)S(1)}, u32[]{:S(2)}, u32[]{:S(2)}) collective-permute-start(bf16[128,2048]{1,0:T(8,128)(2,1)} %get-tuple-element.193), channel_id=1, source_target_pairs={{0,1},{1,0},{2,3},{3,2},{4,5},{5,4},{6,7},{7,6},{8,9},{9,8},{10,11... | collective-permute-start | bytes 1572872 | tf_op jit(solution)/shard_map/ppermute | solution.py:387
  57.8 19.6 %collective-permute-start.9 = (bf16[128,2048]{1,0:T(8,128)(2,1)}, bf16[128,2048]{1,0:T(8,128)(2,1)}, u32[]{:S(2)}, u32[]{:S(2)}) collective-permute-start(bf16[128,2048]{1,0:T(8,128)(2,1)} %get-tuple-element.192), channel_id=1, source_target_pairs={{0,2},{1,3},{2,0},{3,1},{4,6},{5,7},{6,4},{7,5},{8,10},{9,11},{10,... | collective-permute-start | bytes 1572872 | tf_op jit(solution)/shard_map/ppermute | solution.py:387
  59.3 19.7 %collective-permute-start.10 = (bf16[128,2048]{1,0:T(8,128)(2,1)}, bf16[128,2048]{1,0:T(8,128)(2,1)}, u32[]{:S(2)}, u32[]{:S(2)}) collective-permute-start(bf16[128,2048]{1,0:T(8,128)(2,1)} %get-tuple-element.193), channel_id=1, source_target_pairs={{0,2},{1,3},{2,0},{3,1},{4,6},{5,7},{6,4},{7,5},{8,10},{9,11},{10,... | collective-permute-start | bytes 1572872 | tf_op jit(solution)/shard_map/ppermute | solution.py:387
  87.4 335.3 %reduce-scatter.4.cloned.1.call-start = ((), (), s32[]{:S(2)}) async-start(), calls=%async_computation.5 | async-start | bytes 9437184 | tf_op jit(solution)/shard_map/reduce_scatter | solution.py:560
  96.0 21.7 %collective-permute-start.16 = (bf16[8,320]{1,0:T(8,128)(2,1)S(1)}, bf16[8,320]{1,0:T(8,128)(2,1)S(1)}, u32[]{:S(2)}, u32[]{:S(2)}) collective-permute-start(bf16[8,320]{1,0:T(8,128)(2,1)S(1)} %bitcast.149), channel_id=1, source_target_pairs={{0,3},{1,2},{2,1},{3,0},{4,7},{5,6},{6,5},{7,4},{8,11},{9,10},{10,... | collective-permute-start | bytes 15368 | tf_op jit(solution)/shard_map/ppermute | solution.py:387
  97.4 20.8 %collective-permute-start.15 = (bf16[8,320]{1,0:T(8,128)(2,1)S(1)}, bf16[8,320]{1,0:T(8,128)(2,1)S(1)}, u32[]{:S(2)}, u32[]{:S(2)}) collective-permute-start(bf16[8,320]{1,0:T(8,128)(2,1)S(1)} %bitcast.150), channel_id=1, source_target_pairs={{0,2},{1,3},{2,0},{3,1},{4,6},{5,7},{6,4},{7,5},{8,10},{9,11},{10,... | collective-permute-start | bytes 15368 | tf_op jit(solution)/shard_map/ppermute | solution.py:387
  108.7 47.8 %collective-permute-start.19 = (bf16[256,2048]{1,0:T(8,128)(2,1)}, bf16[256,2048]{1,0:T(8,128)(2,1)}, u32[]{:S(2)}, u32[]{:S(2)}) collective-permute-start(bf16[256,2048]{1,0:T(8,128)(2,1)} %get-tuple-element.401), channel_id=1, source_target_pairs={{0,3},{1,2},{2,1},{3,0},{4,7},{5,6},{6,5},{7,4},{8,11},{9,10},{10,... | collective-permute-start | bytes 3145736 | tf_op jit(solution)/shard_map/ppermute | solution.py:387
  109.2 47.3 %collective-permute-start.18 = (bf16[256,2048]{1,0:T(8,128)(2,1)}, bf16[256,2048]{1,0:T(8,128)(2,1)}, u32[]{:S(2)}, u32[]{:S(2)}) collective-permute-start(bf16[256,2048]{1,0:T(8,128)(2,1)} %get-tuple-element.402), channel_id=1, source_target_pairs={{0,2},{1,3},{2,0},{3,1},{4,6},{5,7},{6,4},{7,5},{8,10},{9,11},{10,... | collective-permute-start | bytes 3145736 | tf_op jit(solution)/shard_map/ppermute | solution.py:387
  110.7 45.8 %collective-permute-start.17 = (bf16[256,2048]{1,0:T(8,128)(2,1)}, bf16[256,2048]{1,0:T(8,128)(2,1)}, u32[]{:S(2)}, u32[]{:S(2)}) collective-permute-start(bf16[256,2048]{1,0:T(8,128)(2,1)} %get-tuple-element.403), channel_id=1, source_target_pairs={{0,1},{1,0},{2,3},{3,2},{4,5},{5,4},{6,7},{7,6},{8,9},{9,8},{10,11... | collective-permute-start | bytes 3145736 | tf_op jit(solution)/shard_map/ppermute | solution.py:387
  117.7 38.5 %collective-permute-start.14 = (bf16[8,320]{1,0:T(8,128)(2,1)S(1)}, bf16[8,320]{1,0:T(8,128)(2,1)S(1)}, u32[]{:S(2)}, u32[]{:S(2)}) collective-permute-start(bf16[8,320]{1,0:T(8,128)(2,1)S(1)} %bitcast.151), channel_id=1, source_target_pairs={{0,1},{1,0},{2,3},{3,2},{4,5},{5,4},{6,7},{7,6},{8,9},{9,8},{10,11... | collective-permute-start | bytes 15368 | tf_op jit(solution)/shard_map/ppermute | solution.py:387
  161.0 15.5 %collective-permute-start.23 = (bf16[128,2048]{1,0:T(8,128)(2,1)S(1)}, bf16[128,2048]{1,0:T(8,128)(2,1)}, u32[]{:S(2)}, u32[]{:S(2)}) collective-permute-start(bf16[128,2048]{1,0:T(8,128)(2,1)S(1)} %get-tuple-element.228.refs_9_), channel_id=1, source_target_pairs={{0,2},{1,3},{2,0},{3,1},{4,6},{5,7},{6,4},{7,5},{8,10},{9,11},{10,... | collective-permute-start | bytes 1572872 | tf_op jit(solution)/shard_map/ppermute | solution.py:387
  165.2 41.5 %collective-permute-start.21 = (bf16[128,2048]{1,0:T(8,128)(2,1)S(1)}, bf16[128,2048]{1,0:T(8,128)(2,1)}, u32[]{:S(2)}, u32[]{:S(2)}) collective-permute-start(bf16[128,2048]{1,0:T(8,128)(2,1)S(1)} %get-tuple-element.228.refs_9_), channel_id=1, source_target_pairs={{0,1},{1,0},{2,3},{3,2},{4,5},{5,4},{6,7},{7,6},{8,9},{9,8},{10,11... | collective-permute-start | bytes 1572872 | tf_op jit(solution)/shard_map/ppermute | solution.py:387
  166.7 40.0 %collective-permute-start.22 = (bf16[128,2048]{1,0:T(8,128)(2,1)S(1)}, bf16[128,2048]{1,0:T(8,128)(2,1)}, u32[]{:S(2)}, u32[]{:S(2)}) collective-permute-start(bf16[128,2048]{1,0:T(8,128)(2,1)S(1)} %get-tuple-element.227.refs_8_), channel_id=1, source_target_pairs={{0,2},{1,3},{2,0},{3,1},{4,6},{5,7},{6,4},{7,5},{8,10},{9,11},{10,... | collective-permute-start | bytes 1572872 | tf_op jit(solution)/shard_map/ppermute | solution.py:387
  175.1 31.7 %collective-permute-start.24 = (bf16[128,2048]{1,0:T(8,128)(2,1)}, bf16[128,2048]{1,0:T(8,128)(2,1)}, u32[]{:S(2)}, u32[]{:S(2)}) collective-permute-start(bf16[128,2048]{1,0:T(8,128)(2,1)} %collective-permute-done.20.refs_10_), channel_id=1, source_target_pairs={{0,2},{1,3},{2,0},{3,1},{4,6},{5,7},{6,4},{7,5},{8,10},{9,11},{10,... | collective-permute-start | bytes 1572872 | tf_op jit(solution)/shard_map/ppermute | solution.py:387
  176.5 30.3 %collective-permute-start.25 = (bf16[128,2048]{1,0:T(8,128)(2,1)}, bf16[128,2048]{1,0:T(8,128)(2,1)}, u32[]{:S(2)}, u32[]{:S(2)}) collective-permute-start(bf16[128,2048]{1,0:T(8,128)(2,1)} %collective-permute-done.23.refs_13_), channel_id=1, source_target_pairs={{0,1},{1,0},{2,3},{3,2},{4,5},{5,4},{6,7},{7,6},{8,9},{9,8},{10,11... | collective-permute-start | bytes 1572872 | tf_op jit(solution)/shard_map/ppermute | solution.py:387
  216.8 25.8 %collective-permute-start.31 = (bf16[128,2048]{1,0:T(8,128)(2,1)}, bf16[128,2048]{1,0:T(8,128)(2,1)}, u32[]{:S(2)}, u32[]{:S(2)}) collective-permute-start(bf16[128,2048]{1,0:T(8,128)(2,1)} %get-tuple-element.226), channel_id=1, source_target_pairs={{0,2},{1,3},{2,0},{3,1},{4,6},{5,7},{6,4},{7,5},{8,10},{9,11},{10,... | collective-permute-start | bytes 1572872 | tf_op jit(solution)/shard_map/ppermute | solution.py:387
  218.7 30.1 %collective-permute-start.26 = (bf16[128,2048]{1,0:T(8,128)(2,1)}, bf16[128,2048]{1,0:T(8,128)(2,1)}, u32[]{:S(2)}, u32[]{:S(2)}) collective-permute-start(bf16[128,2048]{1,0:T(8,128)(2,1)} %get-tuple-element.218), channel_id=1, source_target_pairs={{0,1},{1,0},{2,3},{3,2},{4,5},{5,4},{6,7},{7,6},{8,9},{9,8},{10,11... | collective-permute-start | bytes 1572872 | tf_op jit(solution)/shard_map/ppermute | solution.py:387
  254.5 23.6 %collective-permute-start.33 = (bf16[128,2048]{1,0:T(8,128)(2,1)S(1)}, bf16[128,2048]{1,0:T(8,128)(2,1)}, u32[]{:S(2)}, u32[]{:S(2)}) collective-permute-start(bf16[128,2048]{1,0:T(8,128)(2,1)S(1)} %get-tuple-element.428.refs_1_), channel_id=1, source_target_pairs={{0,1},{1,0},{2,3},{3,2},{4,5},{5,4},{6,7},{7,6},{8,9},{9,8},{10,11... | collective-permute-start | bytes 1572872 | tf_op jit(solution)/shard_map/ppermute | solution.py:387
  256.2 23.1 %collective-permute-start.34 = (bf16[128,2048]{1,0:T(8,128)(2,1)S(1)}, bf16[128,2048]{1,0:T(8,128)(2,1)}, u32[]{:S(2)}, u32[]{:S(2)}) collective-permute-start(bf16[128,2048]{1,0:T(8,128)(2,1)S(1)} %get-tuple-element.429.refs_0_), channel_id=1, source_target_pairs={{0,2},{1,3},{2,0},{3,1},{4,6},{5,7},{6,4},{7,5},{8,10},{9,11},{10,... | collective-permute-start | bytes 1572872 | tf_op jit(solution)/shard_map/ppermute | solution.py:387
  267.3 17.6 %collective-permute-start.36 = (bf16[128,2048]{1,0:T(8,128)(2,1)}, bf16[128,2048]{1,0:T(8,128)(2,1)}, u32[]{:S(2)}, u32[]{:S(2)}) collective-permute-start(bf16[128,2048]{1,0:T(8,128)(2,1)} %collective-permute-done.32.refs_2_), channel_id=1, source_target_pairs={{0,2},{1,3},{2,0},{3,1},{4,6},{5,7},{6,4},{7,5},{8,10},{9,11},{10,... | collective-permute-start | bytes 1572872 | tf_op jit(solution)/shard_map/ppermute | solution.py:387
  269.1 15.8 %collective-permute-start.37 = (bf16[128,2048]{1,0:T(8,128)(2,1)}, bf16[128,2048]{1,0:T(8,128)(2,1)}, u32[]{:S(2)}, u32[]{:S(2)}) collective-permute-start(bf16[128,2048]{1,0:T(8,128)(2,1)} %collective-permute-done.35.refs_5_), channel_id=1, source_target_pairs={{0,1},{1,0},{2,3},{3,2},{4,5},{5,4},{6,7},{7,6},{8,9},{9,8},{10,11... | collective-permute-start | bytes 1572872 | tf_op jit(solution)/shard_map/ppermute | solution.py:387
  310.0 18.7 %collective-permute-start.39 = (bf16[128,2048]{1,0:T(8,128)(2,1)}, bf16[128,2048]{1,0:T(8,128)(2,1)S(1)}, u32[]{:S(2)}, u32[]{:S(2)}) collective-permute-start(bf16[128,2048]{1,0:T(8,128)(2,1)} %get-tuple-element.248), channel_id=1, source_target_pairs={{0,1},{1,0},{2,3},{3,2},{4,5},{5,4},{6,7},{7,6},{8,9},{9,8},{10,11... | collective-permute-start | bytes 1572872 | tf_op jit(solution)/shard_map/ppermute | solution.py:387
  310.9 17.8 %collective-permute-start.40 = (bf16[128,2048]{1,0:T(8,128)(2,1)}, bf16[128,2048]{1,0:T(8,128)(2,1)}, u32[]{:S(2)}, u32[]{:S(2)}) collective-permute-start(bf16[128,2048]{1,0:T(8,128)(2,1)} %get-tuple-element.249), channel_id=1, source_target_pairs={{0,2},{1,3},{2,0},{3,1},{4,6},{5,7},{6,4},{7,5},{8,10},{9,11},{10,... | collective-permute-start | bytes 1572872 | tf_op jit(solution)/shard_map/ppermute | solution.py:387
  329.5 223.7 %reduce-scatter.6.cloned.1.call-start = ((), (), s32[]{:S(2)}) async-start(), calls=%async_computation.6 | async-start | bytes 14155776 | tf_op jit(solution)/shard_map/reduce_scatter | solution.py:571
  330.2 19.5 %collective-permute-start.38 = (bf16[128,2048]{1,0:T(8,128)(2,1)}, bf16[128,2048]{1,0:T(8,128)(2,1)S(1)}, u32[]{:S(2)}, u32[]{:S(2)}) collective-permute-start(bf16[128,2048]{1,0:T(8,128)(2,1)} %get-tuple-element.246), channel_id=1, source_target_pairs={{0,1},{1,0},{2,3},{3,2},{4,5},{5,4},{6,7},{7,6},{8,9},{9,8},{10,11... | collective-permute-start | bytes 1572872 | tf_op jit(solution)/shard_map/ppermute | solution.py:387
  332.7 16.8 %collective-permute-start.42 = (bf16[128,2048]{1,0:T(8,128)(2,1)S(1)}, bf16[128,2048]{1,0:T(8,128)(2,1)S(1)}, u32[]{:S(2)}, u32[]{:S(2)}) collective-permute-start(bf16[128,2048]{1,0:T(8,128)(2,1)S(1)} %add_convert_fusion.5), channel_id=1, source_target_pairs={{0,1},{1,0},{2,3},{3,2},{4,5},{5,4},{6,7},{7,6},{8,9},{9,8},{10,11... | collective-permute-start | bytes 1572872 | tf_op jit(solution)/shard_map/ppermute | solution.py:387
  354.3 15.9 %collective-permute-start.47 = (bf16[128,2048]{1,0:T(8,128)(2,1)S(1)}, bf16[128,2048]{1,0:T(8,128)(2,1)S(1)}, u32[]{:S(2)}, u32[]{:S(2)}) collective-permute-start(bf16[128,2048]{1,0:T(8,128)(2,1)S(1)} %get-tuple-element.426), channel_id=1, source_target_pairs={{0,2},{1,3},{2,0},{3,1},{4,6},{5,7},{6,4},{7,5},{8,10},{9,11},{10,... | collective-permute-start | bytes 1572872 | tf_op jit(solution)/shard_map/ppermute | solution.py:387
  355.9 20.9 %collective-permute-start.45 = (bf16[128,2048]{1,0:T(8,128)(2,1)S(1)}, bf16[128,2048]{1,0:T(8,128)(2,1)S(1)}, u32[]{:S(2)}, u32[]{:S(2)}) collective-permute-start(bf16[128,2048]{1,0:T(8,128)(2,1)S(1)} %get-tuple-element.426), channel_id=1, source_target_pairs={{0,1},{1,0},{2,3},{3,2},{4,5},{5,4},{6,7},{7,6},{8,9},{9,8},{10,11... | collective-permute-start | bytes 1572872 | tf_op jit(solution)/shard_map/ppermute | solution.py:387
  357.4 19.5 %collective-permute-start.46 = (bf16[128,2048]{1,0:T(8,128)(2,1)S(1)}, bf16[128,2048]{1,0:T(8,128)(2,1)S(1)}, u32[]{:S(2)}, u32[]{:S(2)}) collective-permute-start(bf16[128,2048]{1,0:T(8,128)(2,1)S(1)} %get-tuple-element.427), channel_id=1, source_target_pairs={{0,2},{1,3},{2,0},{3,1},{4,6},{5,7},{6,4},{7,5},{8,10},{9,11},{10,... | collective-permute-start | bytes 1572872 | tf_op jit(solution)/shard_map/ppermute | solution.py:387
  422.8 181.1 %reduce-scatter.8.cloned.1.call-start = ((), (), s32[]{:S(2)}) async-start(), calls=%async_computation.7 | async-start | bytes 4718592 | tf_op jit(solution)/shard_map/reduce_scatter | solution.py:596
  431.6 30.0 %collective-permute-start.50 = (bf16[256,2048]{1,0:T(8,128)(2,1)S(1)}, bf16[256,2048]{1,0:T(8,128)(2,1)S(1)}, u32[]{:S(2)}, u32[]{:S(2)}) collective-permute-start(bf16[256,2048]{1,0:T(8,128)(2,1)S(1)} %bitcast.138), channel_id=1, source_target_pairs={{0,1},{1,0},{2,3},{3,2},{4,5},{5,4},{6,7},{7,6},{8,9},{9,8},{10,11... | collective-permute-start | bytes 3145736 | tf_op jit(solution)/shard_map/ppermute | solution.py:387
  432.8 37.0 %collective-permute-start.51 = (bf16[256,2048]{1,0:T(8,128)(2,1)S(1)}, bf16[256,2048]{1,0:T(8,128)(2,1)S(1)}, u32[]{:S(2)}, u32[]{:S(2)}) collective-permute-start(bf16[256,2048]{1,0:T(8,128)(2,1)S(1)} %bitcast.137), channel_id=1, source_target_pairs={{0,2},{1,3},{2,0},{3,1},{4,6},{5,7},{6,4},{7,5},{8,10},{9,11},{10,... | collective-permute-start | bytes 3145736 | tf_op jit(solution)/shard_map/ppermute | solution.py:387
  434.4 43.7 %collective-permute-start.52 = (bf16[256,2048]{1,0:T(8,128)(2,1)S(1)}, bf16[256,2048]{1,0:T(8,128)(2,1)S(1)}, u32[]{:S(2)}, u32[]{:S(2)}) collective-permute-start(bf16[256,2048]{1,0:T(8,128)(2,1)S(1)} %bitcast.136), channel_id=1, source_target_pairs={{0,3},{1,2},{2,1},{3,0},{4,7},{5,6},{6,5},{7,4},{8,11},{9,10},{10,... | collective-permute-start | bytes 3145736 | tf_op jit(solution)/shard_map/ppermute | solution.py:387
  480.4 21.2 %collective-permute-start.58 = (bf16[128,2048]{1,0:T(8,128)(2,1)}, bf16[128,2048]{1,0:T(8,128)(2,1)}, u32[]{:S(2)}, u32[]{:S(2)}) collective-permute-start(bf16[128,2048]{1,0:T(8,128)(2,1)} %get-tuple-element.304), channel_id=1, source_target_pairs={{0,2},{1,3},{2,0},{3,1},{4,6},{5,7},{6,4},{7,5},{8,10},{9,11},{10,... | collective-permute-start | bytes 1572872 | tf_op jit(solution)/shard_map/ppermute | solution.py:387
  482.5 25.0 %collective-permute-start.55 = (bf16[128,2048]{1,0:T(8,128)(2,1)}, bf16[128,2048]{1,0:T(8,128)(2,1)}, u32[]{:S(2)}, u32[]{:S(2)}) collective-permute-start(bf16[128,2048]{1,0:T(8,128)(2,1)} %get-tuple-element.298), channel_id=1, source_target_pairs={{0,1},{1,0},{2,3},{3,2},{4,5},{5,4},{6,7},{7,6},{8,9},{9,8},{10,11... | collective-permute-start | bytes 1572872 | tf_op jit(solution)/shard_map/ppermute | solution.py:387
  513.4 25.2 %collective-permute-start.64 = (bf16[128,2048]{1,0:T(8,128)(2,1)S(1)}, bf16[128,2048]{1,0:T(8,128)(2,1)S(1)}, u32[]{:S(2)}, u32[]{:S(2)}) collective-permute-start(bf16[128,2048]{1,0:T(8,128)(2,1)S(1)} %copy-done.16), channel_id=1, source_target_pairs={{0,2},{1,3},{2,0},{3,1},{4,6},{5,7},{6,4},{7,5},{8,10},{9,11},{10,... | collective-permute-start | bytes 1572872 | tf_op jit(solution)/shard_map/ppermute | solution.py:387
  514.1 20.8 %collective-permute-start.61 = (bf16[128,2048]{1,0:T(8,128)(2,1)S(1)}, bf16[128,2048]{1,0:T(8,128)(2,1)S(1)}, u32[]{:S(2)}, u32[]{:S(2)}) collective-permute-start(bf16[128,2048]{1,0:T(8,128)(2,1)S(1)} %copy-done.18), channel_id=1, source_target_pairs={{0,2},{1,3},{2,0},{3,1},{4,6},{5,7},{6,4},{7,5},{8,10},{9,11},{10,... | collective-permute-start | bytes 1572872 | tf_op jit(solution)/shard_map/ppermute | solution.py:387
  516.0 28.5 %collective-permute-start.59 = (bf16[128,2048]{1,0:T(8,128)(2,1)S(1)}, bf16[128,2048]{1,0:T(8,128)(2,1)S(1)}, u32[]{:S(2)}, u32[]{:S(2)}) collective-permute-start(bf16[128,2048]{1,0:T(8,128)(2,1)S(1)} %copy-done.14), channel_id=1, source_target_pairs={{0,1},{1,0},{2,3},{3,2},{4,5},{5,4},{6,7},{7,6},{8,9},{9,8},{10,11... | collective-permute-start | bytes 1572872 | tf_op jit(solution)/shard_map/ppermute | solution.py:387
  573.1 18.5 %collective-permute-start.66 = (bf16[64,3072]{1,0:T(8,128)(2,1)S(1)}, bf16[64,3072]{1,0:T(8,128)(2,1)S(1)}, u32[]{:S(2)}, u32[]{:S(2)}) collective-permute-start(bf16[64,3072]{1,0:T(8,128)(2,1)S(1)} %get-tuple-element.413), channel_id=1, source_target_pairs={{0,2},{1,3},{2,0},{3,1},{4,6},{5,7},{6,4},{7,5},{8,10},{9,11},{10,... | collective-permute-start | bytes 1179656 | tf_op jit(solution)/shard_map/ppermute | solution.py:387
  573.6 18.0 %collective-permute-start.65 = (bf16[64,3072]{1,0:T(8,128)(2,1)S(1)}, bf16[64,3072]{1,0:T(8,128)(2,1)S(1)}, u32[]{:S(2)}, u32[]{:S(2)}) collective-permute-start(bf16[64,3072]{1,0:T(8,128)(2,1)S(1)} %get-tuple-element.414), channel_id=1, source_target_pairs={{0,1},{1,0},{2,3},{3,2},{4,5},{5,4},{6,7},{7,6},{8,9},{9,8},{10,11... | collective-permute-start | bytes 1179656 | tf_op jit(solution)/shard_map/ppermute | solution.py:387
  (85 other events, 889.2 us)
Sparse Core Ops, SparseCore 0:
  51.1 119.6 all-gather.2
  172.9 80.3 all-gather.4
  329.7 88.9 reduce-scatter.3
  422.9 130.3 reduce-scatter.5
  555.4 48.4 reduce-scatter.7

commit v4 on v3

--- a/solution.py
+++ b/solution.py
@@ -245,10 +245,54 @@
     )(a, b)
 
 
-def feed_kernel(steps, parts, scale_ref, *refs):
-    normed_refs, grad_refs = refs[:parts], refs[parts : 2 * parts]
-    up_ref, down_ref, up_row_ref, hidden_ref, pre_ref = refs[2 * parts : 2 * parts + 5]
-    out_refs, (normed, grad) = refs[2 * parts + 5 : -2], refs[-2:]
+def feed_before_kernel(parts, scale_ref, *refs):
+    grad_refs, (down_ref, hidden_ref, grad_ref) = refs[:parts], refs[parts:]
+
+    @pl.when(pl.program_id(0) == 0)
+    def _():
+        count = grad_refs[0].shape[0]
+        for n in range(parts):
+            grad_ref[n * count : (n + 1) * count] = (
+                grad_refs[n][...].astype(F32) * scale_ref[0]
+            ).astype(BF16)
+
+    hidden_ref[...] = dot(grad_ref[...], down_ref[...])
+
+
+def feed_before(grad, row_scale, both):
+    parts, (count, depth) = len(grad), grad[0].shape
+    rows, width = parts * count, both.shape[1] // 2
+    tile = min(256, width)
+    steps = width // tile
+    piece = pl.BlockSpec((count, depth), lambda n: (0, 0), pipeline_mode=pl.Buffered(1))
+    return pl.pallas_call(
+        functools.partial(feed_before_kernel, parts),
+        grid=(steps,),
+        in_specs=[pl.BlockSpec(memory_space=pltpu.SMEM)]
+        + [piece] * parts
+        + [pl.BlockSpec((depth, tile), lambda n: (0, steps + n))],
+        out_specs=[
+            pl.BlockSpec((rows, tile), lambda n: (0, n)),
+            pl.BlockSpec((rows, depth), lambda n: (0, 0)),
+        ],
+        out_shape=[
+            jax.ShapeDtypeStruct((rows, width), F32),
+            jax.ShapeDtypeStruct((rows, depth), BF16),
+        ],
+        compiler_params=pltpu.CompilerParams(vmem_limit_bytes=48 * 1024 * 1024),
+        cost_estimate=pl.CostEstimate(
+            flops=2 * rows * depth * width,
+            bytes_accessed=4 * (rows * depth + depth * width + rows * width),
+            transcendentals=0,
+        ),
+        name="feed_before",
+    )(row_scale.reshape(1), *grad, both)
+
+
+def feed_kernel(steps, parts, *refs):
+    normed_refs = refs[:parts]
+    d_hidden_ref, up_ref, up_row_ref, hidden_ref, pre_ref = refs[parts : parts + 5]
+    out_refs, normed = refs[parts + 5 : -1], refs[-1]
     step = pl.program_id(0)
 
     @pl.when(step == 0)
@@ -256,14 +300,10 @@
         count = normed_refs[0].shape[0]
         for n in range(parts):
             normed[n * count : (n + 1) * count] = normed_refs[n][...]
-            grad[n * count : (n + 1) * count] = (
-                grad_refs[n][...].astype(F32) * scale_ref[0]
-            ).astype(BF16)
 
     @pl.when(step < steps)
     def _():
         u = dot(normed[...], up_ref[...])
-        d_hidden = dot(grad[...], down_ref[...])
         scale = 0.7978845608028654
         square = u * u
         t = jnp.tanh(scale * u * (1.0 + 0.044715 * square))
@@ -272,7 +312,7 @@
         tile = u.shape[1]
         at = pl.ds(pl.multiple_of(step * tile, tile), tile)
         hidden_ref[:, at] = (u * half).astype(BF16)
-        pre_ref[:, at] = (d_hidden * slope).astype(BF16)
+        pre_ref[:, at] = (d_hidden_ref[...] * slope).astype(BF16)
 
     @pl.when(step >= steps)
     def _():
@@ -282,9 +322,9 @@
             out_ref[...] = result[n * count : (n + 1) * count].astype(BF16)
 
 
-def feed_call(normed, grad, row_scale, both):
+def feed_call(normed, d_hidden, both):
     parts, (count, depth) = len(normed), normed[0].shape
-    rows, width = parts * count, both.shape[1] // 2
+    rows, width = d_hidden.shape
     tile, out_tile = min(256, width), min(512, depth)
     steps, out_steps = width // tile, depth // out_tile
     first = lambda n: jnp.minimum(n, steps - 1)
@@ -294,54 +334,49 @@
     return pl.pallas_call(
         functools.partial(feed_kernel, steps, parts),
         grid=(steps + out_steps,),
-        in_specs=[pl.BlockSpec(memory_space=pltpu.SMEM)]
-        + [piece] * (2 * parts)
+        in_specs=[piece] * parts
         + [
+            pl.BlockSpec((rows, tile), lambda n: (0, first(n))),
             pl.BlockSpec((depth, tile), lambda n: (0, first(n))),
-            pl.BlockSpec((depth, tile), lambda n: (0, steps + first(n))),
             pl.BlockSpec((out_tile, width), lambda n: (second(n), 0)),
         ],
         out_specs=[whole, whole]
         + [pl.BlockSpec((count, out_tile), lambda n: (0, second(n)))] * parts,
         out_shape=[jax.ShapeDtypeStruct((rows, width), BF16)] * 2
         + [jax.ShapeDtypeStruct((count, depth), BF16)] * parts,
-        scratch_shapes=[pltpu.VMEM((rows, depth), BF16)] * 2,
-        compiler_params=pltpu.CompilerParams(vmem_limit_bytes=56 * 1024 * 1024),
+        scratch_shapes=[pltpu.VMEM((rows, depth), BF16)],
+        compiler_params=pltpu.CompilerParams(vmem_limit_bytes=58 * 1024 * 1024),
         cost_estimate=pl.CostEstimate(
-            flops=6 * rows * depth * width,
-            bytes_accessed=4 * (rows * depth + 2 * depth * width + rows * width),
+            flops=4 * rows * depth * width,
+            bytes_accessed=2 * (3 * rows * depth + 2 * depth * width + rows * width),
             transcendentals=rows * width,
         ),
         name="feed_forward",
-    )(row_scale.reshape(1), *normed, *grad, both, both, both)
-
-
-def feed_grads_kernel(parts, scale_ref, *refs):
-    normed_refs, grad_refs = refs[:parts], refs[parts : 2 * parts]
-    hidden_ref, pre_ref, out_ref, normed, grad = refs[2 * parts :]
+    )(*normed, d_hidden, both, both)
+
+
+def feed_grads_kernel(parts, *refs):
+    normed_refs, (grad_ref, hidden_ref, pre_ref, out_ref, normed) = refs[:parts], refs[parts:]
     count, width = normed_refs[0].shape[0], hidden_ref.shape[1]
     for n in range(parts):
         normed[n * count : (n + 1) * count] = normed_refs[n][...]
-        grad[n * count : (n + 1) * count] = (grad_refs[n][...].astype(F32) * scale_ref[0]).astype(
-            BF16
-        )
     out_ref[:, :width] = contract_rows(normed[...], pre_ref[...]).astype(BF16)
-    out_ref[:, width:] = contract_rows(grad[...], hidden_ref[...]).astype(BF16)
-
-
-def feed_grads(normed, grad, row_scale, hidden, d_pre):
+    out_ref[:, width:] = contract_rows(grad_ref[...], hidden_ref[...]).astype(BF16)
+
+
+def feed_grads(normed, grad, hidden, d_pre):
     parts, (count, depth) = len(normed), normed[0].shape
     rows, width = hidden.shape
     tile = min(512, depth)
-    slab = pl.BlockSpec((count, tile), lambda n: (0, n))
     whole = pl.BlockSpec((rows, width), lambda n: (0, 0))
     return pl.pallas_call(
         functools.partial(feed_grads_kernel, parts),
         grid=(depth // tile,),
-        in_specs=[pl.BlockSpec(memory_space=pltpu.SMEM)] + [slab] * (2 * parts) + [whole, whole],
+        in_specs=[pl.BlockSpec((count, tile), lambda n: (0, n))] * parts
+        + [pl.BlockSpec((rows, tile), lambda n: (0, n)), whole, whole],
         out_specs=pl.BlockSpec((tile, 2 * width), lambda n: (n, 0)),
         out_shape=jax.ShapeDtypeStruct((depth, 2 * width), BF16),
-        scratch_shapes=[pltpu.VMEM((rows, tile), BF16)] * 2,
+        scratch_shapes=[pltpu.VMEM((rows, tile), BF16)],
         compiler_params=pltpu.CompilerParams(vmem_limit_bytes=48 * 1024 * 1024),
         cost_estimate=pl.CostEstimate(
             flops=4 * rows * depth * width,
@@ -349,7 +384,7 @@
             transcendentals=0,
         ),
         name="feed_grads",
-    )(row_scale.reshape(1), *normed, *grad, hidden, d_pre)
+    )(*normed, grad, hidden, d_pre)
 
 
 def on_device(
@@ -549,10 +584,13 @@
     middle = source + collect(row_product(gated, w_out, False, parts))[0]
     normal_two, factor_two = layer_stats(middle)
     normed_two = (normal_two * gain_two + bias_two).astype(BF16)
-    normed_rows = spread(normed_two)
-    hidden, d_pre, *pieces = feed_call(normed_rows, cotan_rows, row_scale, w_feed)
+    normed_rows = spread_start(normed_two)
+    d_hidden, grad_rows = feed_before(cotan_rows, row_scale, w_feed)
+    normed_rows, d_hidden = together((normed_rows, d_hidden))
+    normed_rows = spread_end(normed_rows)
+    hidden, d_pre, *pieces = feed_call(normed_rows, d_hidden, w_feed)
     *pieces, hidden, d_pre = together((*pieces, hidden, d_pre))
-    feed_part = feed_grads(normed_rows, cotan_rows, row_scale, hidden, d_pre)
+    feed_part = feed_grads(normed_rows, grad_rows, hidden, d_pre)
     d_normed_two, feed_part = collect(pieces, feed_part)
     scatter = functools.partial(
         lax.psum_scatter, axis_name="dp", scatter_dimension=0, tiled=True
@@ -592,7 +630,7 @@
     width = up_weight.shape[1]
     up_grad = feed_grad[:, :width].astype(F32)
     down_grad = feed_grad[:, width:].astype(F32).T
-    output_part, in_grad, outputs, d_tokens = together((output_part, in_grad, outputs, d_tokens))
+    output_part, in_grad, d_tokens = together((output_part, in_grad, d_tokens))
     output_grad = scatter(output_part).astype(F32)
     pieces = by_index([in_grad[m * part : (m + 1) * part] for m in masks])
     pieces = by_index([swap(pieces[m], m) for m in masks])

time: 619 us -> 614 us (level)
  waiting for transfers between devices: 272 us -> 249 us
  other arithmetic: 62.6 us -> 70.6 us
    ppermute x63, waiting for transfers between devices: 246 us -> 217 us  [swap(): return lax.ppermute(x, 'mp', [(s, s ^ mask) for s in range(mp)])]
    pallas_call x0 -> x1, Pallas kernels: none -> 10.2 us  [feed_before(): pl.pallas_call(functools.partial(feed_before_kernel, parts), grid=(steps,...]
    pallas_call x1, Pallas kernels: 25 us -> 18.8 us  [feed_call(): pl.pallas_call(functools.partial(feed_kernel, steps, parts), grid=(steps...]
  transfers between devices with their start and end apart: 78 -> 78, of which waited for: 41 -> 39; matrix products, arithmetic and copies ran while one was open for 20% -> 22% of each run, Pallas kernels for 12% -> 14%
where the time goes in v4:
time: 614 us; the launch traced here: 607 us
  waiting for transfers between devices  249 us (41%)
  Pallas kernels  101 us (16%)
  starting transfers between devices  89.6 us (15%)
  other arithmetic  70.6 us (11%)
  matrix products  50.6 us (8%)
  local copies, waits for them, and re-layouts  29 us (5%)
  between operations  16.9 us (3%)
    ppermute x63, waiting for transfers between devices, swap(): return lax.ppermute(x, 'mp', [(s, s ^ mask) for s in range(mp)])  217 us
    ppermute x63, starting transfers between devices, swap(): return lax.ppermute(x, 'mp', [(s, s ^ mask) for s in range(mp)])  70 us
    pallas_call x3, Pallas kernels, row_product(): pl.pallas_call(functools.partial(product_kernel, ((1,), (1 if transposed...  34.6 us
    dot_general x2, matrix products, contract_rows(): lax.dot_general(left, right, (((0,), (0,)), ((), ())), preferred_element_...  25.5 us
    pallas_call x2, Pallas kernels, retention_call(): pl.pallas_call(functools.partial(body, heads), grid_spec=pltpu.PrefetchSc...  23.8 us
    dot_general x1, matrix products, dot(): return jnp.dot(left, right, preferred_element_type=F32)  19 us
    pallas_call x1, Pallas kernels, feed_call(): pl.pallas_call(functools.partial(feed_kernel, steps, parts), grid=(steps...  18.8 us
    unnamed x126, local copies, waits for them, and re-layouts  16.4 us
  transfers between devices with their start and end apart: 78, of which 39 were waited for; matrix products, arithmetic and copies ran while one was open for 22% of the time, Pallas kernels for 14%

profile of v4, /device:TPU:0, one launch (start us, length us, event | category | flops | bytes accessed | tf_op | source)
XLA Modules:
  0.0 606.9 jit_solution(6808967344280849797)
XLA Ops:
  13.9 2.9 collective-permute-start
  18.2 4.6 collective-permute-start.4
  22.8 3.3 collective-permute-start.5
  28.7 16.1 %collective-permute-done.1 = bf16[64,3072]{1,0:T(8,128)(2,1)S(1)} collective-permute-done((bf16[64,3072]{1,0:T(8,128)(2,1)}, bf16[64,3072]{1,0:T(8,128)(2,1)S(1)}, u32[]{:S(2)}, u32[]{:S(2)}) %collective-permute-start.1) | collective-permute-done | bytes 393248 | tf_op jit(solution)/shard_map/ppermute | solution.py:422
  44.8 3.4 collective-permute-done.5
  52.1 2.9 collective-permute-start.6
  60.1 11.0 %collective-permute-done.7 = bf16[128,2048]{1,0:T(8,128)(2,1)S(1)} collective-permute-done((bf16[128,2048]{1,0:T(8,128)(2,1)}, bf16[128,2048]{1,0:T(8,128)(2,1)S(1)}, u32[]{:S(2)}, u32[]{:S(2)}) %collective-permute-start.7) | collective-permute-done | bytes 524320 | tf_op jit(solution)/shard_map/ppermute | solution.py:422
  71.1 6.4 %collective-permute-done.8 = bf16[128,2048]{1,0:T(8,128)(2,1)S(1)} collective-permute-done((bf16[128,2048]{1,0:T(8,128)(2,1)}, bf16[128,2048]{1,0:T(8,128)(2,1)S(1)}, u32[]{:S(2)}, u32[]{:S(2)}) %collective-permute-start.8) | collective-permute-done | bytes 524320 | tf_op jit(solution)/shard_map/ppermute | solution.py:422
  97.0 5.7 collective-permute-done.12
  116.3 36.9 %collective-permute-done.14 = bf16[8,320]{1,0:T(8,128)(2,1)S(1)} collective-permute-done((bf16[8,320]{1,0:T(8,128)(2,1)S(1)}, bf16[8,320]{1,0:T(8,128)(2,1)S(1)}, u32[]{:S(2)}, u32[]{:S(2)}) %collective-permute-start.14) | collective-permute-done | bytes 5152 | tf_op jit(solution)/shard_map/ppermute | solution.py:422
  159.0 3.2 fusion.5
  166.6 5.4 collective-permute-done.20.refs_2_
  174.0 19.0 %fusion.40.pre_ref = f32[1024,3072]{1,0:T(8,128)} fusion(bf16[1024,2048]{1,0:T(8,128)(2,1)} %fusion.5, bf16[2048,3072]{1,0:T(8,128)(2,1)} %all-gather.3.cloned.1.call-done.b_ref), kind=kOutput, calls=%fused_computation.218 | convolution fusion | flops 12884901888 | bytes 29360128 | tf_op jit(solution)/shard_map/dot_general | solution.py:50
  193.0 8.3 %retention_forward.1 = (bf16[1024,1024]{1,0:T(8,128)(2,1)S(1)}, bf16[4,2,256,512]{3,2,1,0:T(8,128)(2,1)}) custom-call(s32[4]{0:T(128)S(1)} %iota_xor_fusion.order_ref, f32[2]{0:T(128)S(1)} %get-tuple-element.213.block_ref, f32[1024,3072]{1,0:T(8,128)} %fusion.40.pre_ref, f32[1024,128]{1,0:T(8,128)S(1)} %get-tuple-element.215.cos_ref, ...), custom_call_target="tpu_custom_call" | custom-call | flops 1879048192 | bytes 15728640 | tf_op jit(solution)/shard_map/retention_forward/pallas_call | solution.py:197
  202.6 8.2 %row_product.3 = (bf16[128,2048]{1,0:T(8,128)(2,1)S(1)}, bf16[128,2048]{1,0:T(8,128)(2,1)S(1)}, bf16[128,2048]{1,0:T(8,128)(2,1)}, bf16[128,2048]{1,0:T(8,128)(2...) custom-call(bf16[1024,1024]{1,0:T(8,128)(2,1)} %copy-done.7, ...), custom_call_target="tpu_custom_call" | custom-call | flops 4294967296 | bytes 10485760 | tf_op jit(solution)/shard_map/row_product/pallas_call | solution.py:232
  215.2 10.5 %collective-permute-done.27 = bf16[128,2048]{1,0:T(8,128)(2,1)S(1)} collective-permute-done((bf16[128,2048]{1,0:T(8,128)(2,1)S(1)}, bf16[128,2048]{1,0:T(8,128)(2,1)S(1)}, u32[]{:S(2)}, u32[]{:S(2)}) %collective-permute-start.27) | collective-permute-done | bytes 524320 | tf_op jit(solution)/shard_map/ppermute | solution.py:422
  231.2 7.3 %collective-permute-done.31 = bf16[128,2048]{1,0:T(8,128)(2,1)} collective-permute-done((bf16[128,2048]{1,0:T(8,128)(2,1)}, bf16[128,2048]{1,0:T(8,128)(2,1)}, u32[]{:S(2)}, u32[]{:S(2)}) %collective-permute-start.31) | collective-permute-done | bytes 524320 | tf_op jit(solution)/shard_map/ppermute | solution.py:422
  238.5 5.9 collective-permute-done.30
  256.0 10.2 %feed_before.1 = (f32[1024,1024]{1,0:T(8,128)}, bf16[1024,2048]{1,0:T(8,128)(2,1)}) custom-call(f32[1]{0:T(128)} %bitcast.36.scale_ref, bf16[128,2048]{1,0:T(8,128)(2,1)S(1)} %copy-done.6, bf16[128,2048]{1,0:T(8,128)(2,1)S(1)} %copy-done.4, bf16[128,2048]{1,0:T(8,128)(2,1)} %collective-permute-done.20.refs_2_, ...), custom_call_target="tpu_custom_call" | custom-call | flops 4294967296 | bytes 20971520 | tf_op jit(solution)/shard_map/feed_before/pallas_call | solution.py:268
  266.1 5.8 collective-permute-done.33.refs_3_
  271.9 3.8 collective-permute-done.35.refs_5_
  277.7 7.3 %collective-permute-done.36.refs_6_ = bf16[128,2048]{1,0:T(8,128)(2,1)S(1)} collective-permute-done((bf16[128,2048]{1,0:T(8,128)(2,1)}, bf16[128,2048]{1,0:T(8,128)(2,1)S(1)}, u32[]{:S(2)}, u32[]{:S(2)}) %collective-permute-start.36) | collective-permute-done | bytes 524320 | tf_op jit(solution)/shard_map/ppermute | solution.py:422
  287.4 18.8 %feed_forward.1 = (bf16[1024,1024]{1,0:T(8,128)(2,1)}, bf16[1024,1024]{1,0:T(8,128)(2,1)}, bf16[128,2048]{1,0:T(8,128)(2,1)}, bf16[128,2048]{1,0:T(8,128)(2,1)},...) custom-call(bf16[128,2048]{1,0:T(8,128)(2,1)} %get-tuple-element.244, ...), custom_call_target="tpu_custom_call" | custom-call | flops 8589934592 | bytes 23068672 | tf_op jit(solution)/shard_map/feed_forward/pallas_call | solution.py:334
  309.6 13.9 %feed_grads.1 = bf16[2048,2048]{1,0:T(8,128)(2,1)} custom-call(bf16[128,2048]{1,0:T(8,128)(2,1)} %get-tuple-element.244.refs_0_, bf16[128,2048]{1,0:T(8,128)(2,1)} %get-tuple-element.245.refs_1_, bf16[128,2048]{1,0:T(8,128)(2,1)} %collective-permute-done.32.refs_2_, bf16[128,2048]{1,0:T(8,128)(2,1)} %collective-permute-done.33.refs_3_, ...), custom_call_target="tpu_custom_call" | custom-call | flops 8589934592 | bytes 20971520 | tf_op jit(solution)/shard_map/feed_grads/pallas_call | solution.py:372
  331.4 6.0 collective-permute-done.43
  337.4 7.3 %collective-permute-done.42 = bf16[128,2048]{1,0:T(8,128)(2,1)S(1)} collective-permute-done((bf16[128,2048]{1,0:T(8,128)(2,1)S(1)}, bf16[128,2048]{1,0:T(8,128)(2,1)S(1)}, u32[]{:S(2)}, u32[]{:S(2)}) %collective-permute-start.42) | collective-permute-done | bytes 524320 | tf_op jit(solution)/shard_map/ppermute | solution.py:422
  352.8 10.8 %collective-permute-done.44 = bf16[128,2048]{1,0:T(8,128)(2,1)S(1)} collective-permute-done((bf16[128,2048]{1,0:T(8,128)(2,1)S(1)}, bf16[128,2048]{1,0:T(8,128)(2,1)S(1)}, u32[]{:S(2)}, u32[]{:S(2)}) %collective-permute-start.44) | collective-permute-done | bytes 524320 | tf_op jit(solution)/shard_map/ppermute | solution.py:422
  366.5 4.8 collective-permute-done.45
  371.5 5.4 collective-permute-done.48
  377.0 6.1 %fusion.41.grad_ref = f32[1024,1024]{1,0:T(8,128)} fusion(bf16[1024,2048]{1,0:T(8,128)(2,1)S(1)} %constant_dynamic-update-slice_fusion.10, bf16[1024,2048]{1,0:T(8,128)(2,1)S(1)} %bitcast.128), kind=kOutput, calls=%fused_computation.219 | convolution fusion | flops 4294967296 | bytes 12582912 | tf_op jit(solution)/shard_map/dot_general | solution.py:60
  383.1 15.6 %retention_backward.1.a_ref = bf16[1024,3072]{1,0:T(8,128)(2,1)} custom-call(s32[4]{0:T(128)S(1)} %iota_xor_fusion.order_ref, f32[2]{0:T(128)S(1)} %get-tuple-element.213.block_ref, f32[1024,3072]{1,0:T(8,128)} %fusion.40.pre_ref, f32[1024,128]{1,0:T(8,128)S(1)} %get-tuple-element.215.cos_ref, f32[1024,128]{1,0:T(8,128)S(1)} %get-tuple-element.216.sin_ref, ...), custom_call_target="tpu_custom_call" | custom-call | flops 4026531840 | bytes 18874368 | tf_op jit(solution)/shard_map/retention_backward/pallas_call | solution.py:197
  398.7 18.6 %convolution_convert_fusion = bf16[2048,3072]{1,0:T(8,128)(2,1)} fusion(bf16[1024,2048]{1,0:T(8,128)(2,1)S(1)} %copy-done.33, bf16[1024,3072]{1,0:T(8,128)(2,1)} %retention_backward.1.a_ref), kind=kOutput, calls=%fused_computation | convolution fusion | flops 12891193344 | bytes 23068672 | tf_op jit(solution)/shard_map/dot_general | solution.py:54
  418.9 7.0 %convolution_convert_fusion.1 = bf16[1024,2048]{1,0:T(8,128)(2,1)S(1)} fusion(bf16[1024,1024]{1,0:T(8,128)(2,1)S(1)} %copy-done.8, bf16[1024,2048]{1,0:T(8,128)(2,1)} %copy-done.50), kind=kOutput, calls=%fused_computation.14 | convolution fusion | flops 4297064448 | bytes 10485760 | tf_op jit(solution)/shard_map/dot_general | solution.py:54
  429.7 18.5 %row_product.4 = (bf16[128,2048]{1,0:T(8,128)(2,1)S(1)}, bf16[128,2048]{1,0:T(8,128)(2,1)S(1)}, bf16[128,2048]{1,0:T(8,128)(2,1)}, bf16[128,2048]{1,0:T(8,128)(2...) custom-call(bf16[1024,3072]{1,0:T(8,128)(2,1)} %retention_backward.1, ...), custom_call_target="tpu_custom_call" | custom-call | flops 12884901888 | bytes 23068672 | tf_op jit(solution)/shard_map/row_product/pallas_call | solution.py:232
  448.3 7.9 %row_product.5 = (bf16[128,2048]{1,0:T(8,128)(2,1)S(1)}, bf16[128,2048]{1,0:T(8,128)(2,1)S(1)}, bf16[128,2048]{1,0:T(8,128)(2,1)S(1)}, bf16[128,2048]{1,0:T(8,12...) custom-call(bf16[1024,1024]{1,0:T(8,128)(2,1)} %get-tuple-element.29, ...), custom_call_target="tpu_custom_call" | custom-call | flops 4294967296 | bytes 10485760 | tf_op jit(solution)/shard_map/row_product/pallas_call | solution.py:232
  456.2 11.7 %collective-permute-done.51 = bf16[256,2048]{1,0:T(8,128)(2,1)S(1)} collective-permute-done((bf16[256,2048]{1,0:T(8,128)(2,1)S(1)}, bf16[256,2048]{1,0:T(8,128)(2,1)S(1)}, u32[]{:S(2)}, u32[]{:S(2)}) %collective-permute-start.51) | collective-permute-done | bytes 1048608 | tf_op jit(solution)/shard_map/ppermute | solution.py:422
  467.9 3.9 collective-permute-done.52
  479.6 5.2 collective-permute-done.54
  484.7 6.8 %collective-permute-done.55 = bf16[128,2048]{1,0:T(8,128)(2,1)} collective-permute-done((bf16[128,2048]{1,0:T(8,128)(2,1)}, bf16[128,2048]{1,0:T(8,128)(2,1)}, u32[]{:S(2)}, u32[]{:S(2)}) %collective-permute-start.55) | collective-permute-done | bytes 524320 | tf_op jit(solution)/shard_map/ppermute | solution.py:422
  498.0 5.2 collective-permute-done.57
  511.7 3.1 collective-permute-done.68
  524.9 3.0 collective-permute-start.70
  533.9 4.4 fusion.14
  538.3 9.2 %reduce-scatter.6.cloned.1.call-done = bf16[256,3072]{1,0:T(8,128)(2,1)} async-done(((bf16[2048,3072]{1,0:T(8,128)(2,1)}), bf16[256,3072]{1,0:T(8,128)(2,1)}) %reduce-scatter.6.cloned.1.call-update) | async-done | bytes 1572880 | tf_op jit(solution)/shard_map/reduce_scatter | solution.py:609
  553.6 6.8 %collective-permute-done.63 = bf16[128,2048]{1,0:T(8,128)(2,1)S(1)} collective-permute-done((bf16[128,2048]{1,0:T(8,128)(2,1)S(1)}, bf16[128,2048]{1,0:T(8,128)(2,1)S(1)}, u32[]{:S(2)}, u32[]{:S(2)}) %collective-permute-start.63) | collective-permute-done | bytes 524320 | tf_op jit(solution)/shard_map/ppermute | solution.py:422
  569.3 8.1 %collective-permute-done.67 = bf16[64,3072]{1,0:T(8,128)(2,1)S(1)} collective-permute-done((bf16[64,3072]{1,0:T(8,128)(2,1)S(1)}, bf16[64,3072]{1,0:T(8,128)(2,1)S(1)}, u32[]{:S(2)}, u32[]{:S(2)}) %collective-permute-start.67) | collective-permute-done | bytes 393248 | tf_op jit(solution)/shard_map/ppermute | solution.py:422
  577.4 4.2 collective-permute-done.66
  585.8 12.2 %reduce-scatter.8.cloned.1.call-done = bf16[128,2048]{1,0:T(8,128)(2,1)} async-done(((bf16[1024,2048]{1,0:T(8,128)(2,1)}), bf16[128,2048]{1,0:T(8,128)(2,1)}) %reduce-scatter.8.cloned.1.call-update) | async-done | bytes 524304 | tf_op jit(solution)/shard_map/reduce_scatter | solution.py:634
  (393 shorter events, 177.9 us)
Async XLA Ops:
  7.2 166.8 %all-gather.3.cloned.1.call-start = ((), (), s32[]{:S(2)}) async-start(), calls=%async_computation.3 | async-start | bytes 14155776 | tf_op jit(solution)/shard_map/all_gather | solution.py:539
  16.9 27.9 %collective-permute-start.3 = (bf16[144,2048]{1,0:T(8,128)(2,1)S(1)}, bf16[144,2048]{1,0:T(8,128)(2,1)S(1)}, u32[]{:S(2)}, u32[]{:S(2)}) collective-permute-start(bf16[144,2048]{1,0:T(8,128)(2,1)S(1)} %constant_dynamic-update-slice_fusion), channel_id=1, source_target_pairs={{8,0},{12,4},{16,8},{20,12},{24,16},{28,20},{9,1},{13,5},{17,9},{2... | collective-permute-start | bytes 1769480 | tf_op jit(solution)/shard_map/ppermute | solution.py:471
  18.2 26.6 %collective-permute-start.4 = (bf16[144,2048]{1,0:T(8,128)(2,1)S(1)}, bf16[144,2048]{1,0:T(8,128)(2,1)S(1)}, u32[]{:S(2)}, u32[]{:S(2)}) collective-permute-start(bf16[144,2048]{1,0:T(8,128)(2,1)S(1)} %constant_dynamic-update-slice_fusion), channel_id=1, source_target_pairs={{0,8},{4,12},{8,16},{12,20},{16,24},{20,28},{1,9},{5,13},{9,17},{1... | collective-permute-start | bytes 1769480 | tf_op jit(solution)/shard_map/ppermute | solution.py:471
  22.8 25.5 %collective-permute-start.5 = (bf16[144,2048]{1,0:T(8,128)(2,1)S(1)}, bf16[144,2048]{1,0:T(8,128)(2,1)S(1)}, u32[]{:S(2)}, u32[]{:S(2)}) collective-permute-start(bf16[144,2048]{1,0:T(8,128)(2,1)S(1)} %constant_dynamic-update-slice_fusion), channel_id=1, source_target_pairs={{0,24},{4,28},{24,0},{28,4},{1,25},{5,29},{25,1},{29,5},{2,26},{6,... | collective-permute-start | bytes 1769480 | tf_op jit(solution)/shard_map/ppermute | solution.py:471
  26.1 18.7 %collective-permute-start.1 = (bf16[64,3072]{1,0:T(8,128)(2,1)}, bf16[64,3072]{1,0:T(8,128)(2,1)S(1)}, u32[]{:S(2)}, u32[]{:S(2)}) collective-permute-start(bf16[64,3072]{1,0:T(8,128)(2,1)} %pad_maximum_fusion.15), channel_id=1, source_target_pairs={{0,2},{1,3},{2,0},{3,1},{4,6},{5,7},{6,4},{7,5},{8,10},{9,11},{10,... | collective-permute-start | bytes 1179656 | tf_op jit(solution)/shard_map/ppermute | solution.py:422
  27.7 17.1 %collective-permute-start.2 = (bf16[64,3072]{1,0:T(8,128)(2,1)}, bf16[64,3072]{1,0:T(8,128)(2,1)}, u32[]{:S(2)}, u32[]{:S(2)}) collective-permute-start(bf16[64,3072]{1,0:T(8,128)(2,1)} %pad_maximum_fusion.16), channel_id=1, source_target_pairs={{0,3},{1,2},{2,1},{3,0},{4,7},{5,6},{6,5},{7,4},{8,11},{9,10},{10,... | collective-permute-start | bytes 1179656 | tf_op jit(solution)/shard_map/ppermute | solution.py:422
  51.1 204.8 %all-gather.5.cloned.1.call-start = ((), (), s32[]{:S(2)}) async-start(), calls=%async_computation.4 | async-start | bytes 9437184 | tf_op jit(solution)/shard_map/all_gather | solution.py:575
  52.1 27.0 %collective-permute-start.6 = (bf16[144,2048]{1,0:T(8,128)(2,1)}, bf16[144,2048]{1,0:T(8,128)(2,1)}, u32[]{:S(2)}, u32[]{:S(2)}) collective-permute-start(bf16[144,2048]{1,0:T(8,128)(2,1)} %select_select_fusion), channel_id=1, source_target_pairs={{0,16},{4,20},{24,8},{28,12},{16,24},{20,28},{8,0},{12,4},{1,17},{... | collective-permute-start | bytes 1769480 | tf_op jit(solution)/shard_map/ppermute | solution.py:471
  56.5 21.0 %collective-permute-start.8 = (bf16[128,2048]{1,0:T(8,128)(2,1)}, bf16[128,2048]{1,0:T(8,128)(2,1)S(1)}, u32[]{:S(2)}, u32[]{:S(2)}) collective-permute-start(bf16[128,2048]{1,0:T(8,128)(2,1)} %get-tuple-element.201), channel_id=1, source_target_pairs={{0,1},{1,0},{2,3},{3,2},{4,5},{5,4},{6,7},{7,6},{8,9},{9,8},{10,11... | collective-permute-start | bytes 1572872 | tf_op jit(solution)/shard_map/ppermute | solution.py:422
  58.0 19.5 %collective-permute-start.9 = (bf16[128,2048]{1,0:T(8,128)(2,1)}, bf16[128,2048]{1,0:T(8,128)(2,1)}, u32[]{:S(2)}, u32[]{:S(2)}) collective-permute-start(bf16[128,2048]{1,0:T(8,128)(2,1)} %get-tuple-element.200), channel_id=1, source_target_pairs={{0,2},{1,3},{2,0},{3,1},{4,6},{5,7},{6,4},{7,5},{8,10},{9,11},{10,... | collective-permute-start | bytes 1572872 | tf_op jit(solution)/shard_map/ppermute | solution.py:422
  59.5 19.5 %collective-permute-start.10 = (bf16[128,2048]{1,0:T(8,128)(2,1)}, bf16[128,2048]{1,0:T(8,128)(2,1)}, u32[]{:S(2)}, u32[]{:S(2)}) collective-permute-start(bf16[128,2048]{1,0:T(8,128)(2,1)} %get-tuple-element.201), channel_id=1, source_target_pairs={{0,2},{1,3},{2,0},{3,1},{4,6},{5,7},{6,4},{7,5},{8,10},{9,11},{10,... | collective-permute-start | bytes 1572872 | tf_op jit(solution)/shard_map/ppermute | solution.py:422
  85.5 331.8 %reduce-scatter.4.cloned.1.call-start = ((), (), s32[]{:S(2)}) async-start(), calls=%async_computation.5 | async-start | bytes 9437184 | tf_op jit(solution)/shard_map/reduce_scatter | solution.py:598
  94.0 21.8 %collective-permute-start.16 = (bf16[8,320]{1,0:T(8,128)(2,1)S(1)}, bf16[8,320]{1,0:T(8,128)(2,1)S(1)}, u32[]{:S(2)}, u32[]{:S(2)}) collective-permute-start(bf16[8,320]{1,0:T(8,128)(2,1)S(1)} %bitcast.148), channel_id=1, source_target_pairs={{0,3},{1,2},{2,1},{3,0},{4,7},{5,6},{6,5},{7,4},{8,11},{9,10},{10,... | collective-permute-start | bytes 15368 | tf_op jit(solution)/shard_map/ppermute | solution.py:422
  95.5 20.8 %collective-permute-start.15 = (bf16[8,320]{1,0:T(8,128)(2,1)S(1)}, bf16[8,320]{1,0:T(8,128)(2,1)S(1)}, u32[]{:S(2)}, u32[]{:S(2)}) collective-permute-start(bf16[8,320]{1,0:T(8,128)(2,1)S(1)} %bitcast.149), channel_id=1, source_target_pairs={{0,2},{1,3},{2,0},{3,1},{4,6},{5,7},{6,4},{7,5},{8,10},{9,11},{10,... | collective-permute-start | bytes 15368 | tf_op jit(solution)/shard_map/ppermute | solution.py:422
  105.7 47.8 %collective-permute-start.19 = (bf16[256,2048]{1,0:T(8,128)(2,1)}, bf16[256,2048]{1,0:T(8,128)(2,1)}, u32[]{:S(2)}, u32[]{:S(2)}) collective-permute-start(bf16[256,2048]{1,0:T(8,128)(2,1)} %get-tuple-element.417), channel_id=1, source_target_pairs={{0,3},{1,2},{2,1},{3,0},{4,7},{5,6},{6,5},{7,4},{8,11},{9,10},{10,... | collective-permute-start | bytes 3145736 | tf_op jit(solution)/shard_map/ppermute | solution.py:422
  106.2 47.3 %collective-permute-start.18 = (bf16[256,2048]{1,0:T(8,128)(2,1)}, bf16[256,2048]{1,0:T(8,128)(2,1)}, u32[]{:S(2)}, u32[]{:S(2)}) collective-permute-start(bf16[256,2048]{1,0:T(8,128)(2,1)} %get-tuple-element.418), channel_id=1, source_target_pairs={{0,2},{1,3},{2,0},{3,1},{4,6},{5,7},{6,4},{7,5},{8,10},{9,11},{10,... | collective-permute-start | bytes 3145736 | tf_op jit(solution)/shard_map/ppermute | solution.py:422
  107.7 45.8 %collective-permute-start.17 = (bf16[256,2048]{1,0:T(8,128)(2,1)}, bf16[256,2048]{1,0:T(8,128)(2,1)}, u32[]{:S(2)}, u32[]{:S(2)}) collective-permute-start(bf16[256,2048]{1,0:T(8,128)(2,1)} %get-tuple-element.419), channel_id=1, source_target_pairs={{0,1},{1,0},{2,3},{3,2},{4,5},{5,4},{6,7},{7,6},{8,9},{9,8},{10,11... | collective-permute-start | bytes 3145736 | tf_op jit(solution)/shard_map/ppermute | solution.py:422
  115.7 37.4 %collective-permute-start.14 = (bf16[8,320]{1,0:T(8,128)(2,1)S(1)}, bf16[8,320]{1,0:T(8,128)(2,1)S(1)}, u32[]{:S(2)}, u32[]{:S(2)}) collective-permute-start(bf16[8,320]{1,0:T(8,128)(2,1)S(1)} %bitcast.150), channel_id=1, source_target_pairs={{0,1},{1,0},{2,3},{3,2},{4,5},{5,4},{6,7},{7,6},{8,9},{9,8},{10,11... | collective-permute-start | bytes 15368 | tf_op jit(solution)/shard_map/ppermute | solution.py:422
  162.2 40.4 %collective-permute-start.21 = (bf16[128,2048]{1,0:T(8,128)(2,1)S(1)}, bf16[128,2048]{1,0:T(8,128)(2,1)}, u32[]{:S(2)}, u32[]{:S(2)}) collective-permute-start(bf16[128,2048]{1,0:T(8,128)(2,1)S(1)} %get-tuple-element.236.refs_1_), channel_id=1, source_target_pairs={{0,1},{1,0},{2,3},{3,2},{4,5},{5,4},{6,7},{7,6},{8,9},{9,8},{10,11... | collective-permute-start | bytes 1572872 | tf_op jit(solution)/shard_map/ppermute | solution.py:422
  163.7 38.9 %collective-permute-start.22 = (bf16[128,2048]{1,0:T(8,128)(2,1)S(1)}, bf16[128,2048]{1,0:T(8,128)(2,1)}, u32[]{:S(2)}, u32[]{:S(2)}) collective-permute-start(bf16[128,2048]{1,0:T(8,128)(2,1)S(1)} %get-tuple-element.235.refs_0_), channel_id=1, source_target_pairs={{0,2},{1,3},{2,0},{3,1},{4,6},{5,7},{6,4},{7,5},{8,10},{9,11},{10,... | collective-permute-start | bytes 1572872 | tf_op jit(solution)/shard_map/ppermute | solution.py:422
  172.0 30.6 %collective-permute-start.24 = (bf16[128,2048]{1,0:T(8,128)(2,1)}, bf16[128,2048]{1,0:T(8,128)(2,1)}, u32[]{:S(2)}, u32[]{:S(2)}) collective-permute-start(bf16[128,2048]{1,0:T(8,128)(2,1)} %collective-permute-done.20.refs_2_), channel_id=1, source_target_pairs={{0,2},{1,3},{2,0},{3,1},{4,6},{5,7},{6,4},{7,5},{8,10},{9,11},{10,... | collective-permute-start | bytes 1572872 | tf_op jit(solution)/shard_map/ppermute | solution.py:422
  173.4 29.2 %collective-permute-start.25 = (bf16[128,2048]{1,0:T(8,128)(2,1)}, bf16[128,2048]{1,0:T(8,128)(2,1)}, u32[]{:S(2)}, u32[]{:S(2)}) collective-permute-start(bf16[128,2048]{1,0:T(8,128)(2,1)} %collective-permute-done.23.refs_5_), channel_id=1, source_target_pairs={{0,1},{1,0},{2,3},{3,2},{4,5},{5,4},{6,7},{7,6},{8,9},{9,8},{10,11... | collective-permute-start | bytes 1572872 | tf_op jit(solution)/shard_map/ppermute | solution.py:422
  213.2 25.3 %collective-permute-start.31 = (bf16[128,2048]{1,0:T(8,128)(2,1)}, bf16[128,2048]{1,0:T(8,128)(2,1)}, u32[]{:S(2)}, u32[]{:S(2)}) collective-permute-start(bf16[128,2048]{1,0:T(8,128)(2,1)} %get-tuple-element.233), channel_id=1, source_target_pairs={{0,2},{1,3},{2,0},{3,1},{4,6},{5,7},{6,4},{7,5},{8,10},{9,11},{10,... | collective-permute-start | bytes 1572872 | tf_op jit(solution)/shard_map/ppermute | solution.py:422
  214.6 31.3 %collective-permute-start.26 = (bf16[128,2048]{1,0:T(8,128)(2,1)}, bf16[128,2048]{1,0:T(8,128)(2,1)}, u32[]{:S(2)}, u32[]{:S(2)}) collective-permute-start(bf16[128,2048]{1,0:T(8,128)(2,1)} %get-tuple-element.225), channel_id=1, source_target_pairs={{0,1},{1,0},{2,3},{3,2},{4,5},{5,4},{6,7},{7,6},{8,9},{9,8},{10,11... | collective-permute-start | bytes 1572872 | tf_op jit(solution)/shard_map/ppermute | solution.py:422
  228.1 16.3 %collective-permute-start.30 = (bf16[128,2048]{1,0:T(8,128)(2,1)}, bf16[128,2048]{1,0:T(8,128)(2,1)}, u32[]{:S(2)}, u32[]{:S(2)}) collective-permute-start(bf16[128,2048]{1,0:T(8,128)(2,1)} %add_convert_fusion.7), channel_id=1, source_target_pairs={{0,1},{1,0},{2,3},{3,2},{4,5},{5,4},{6,7},{7,6},{8,9},{9,8},{10,11... | collective-permute-start | bytes 1572872 | tf_op jit(solution)/shard_map/ppermute | solution.py:422
  229.6 16.3 %collective-permute-start.29 = (bf16[128,2048]{1,0:T(8,128)(2,1)}, bf16[128,2048]{1,0:T(8,128)(2,1)}, u32[]{:S(2)}, u32[]{:S(2)}) collective-permute-start(bf16[128,2048]{1,0:T(8,128)(2,1)} %add_convert_fusion.8), channel_id=1, source_target_pairs={{0,2},{1,3},{2,0},{3,1},{4,6},{5,7},{6,4},{7,5},{8,10},{9,11},{10,... | collective-permute-start | bytes 1572872 | tf_op jit(solution)/shard_map/ppermute | solution.py:422
  250.3 15.8 %collective-permute-start.32 = (bf16[128,2048]{1,0:T(8,128)(2,1)}, bf16[128,2048]{1,0:T(8,128)(2,1)}, u32[]{:S(2)}, u32[]{:S(2)}) collective-permute-start(bf16[128,2048]{1,0:T(8,128)(2,1)} %get-tuple-element.244.refs_0_), channel_id=1, source_target_pairs={{0,1},{1,0},{2,3},{3,2},{4,5},{5,4},{6,7},{7,6},{8,9},{9,8},{10,11... | collective-permute-start | bytes 1572872 | tf_op jit(solution)/shard_map/ppermute | solution.py:422
  251.3 20.6 %collective-permute-start.33 = (bf16[128,2048]{1,0:T(8,128)(2,1)}, bf16[128,2048]{1,0:T(8,128)(2,1)}, u32[]{:S(2)}, u32[]{:S(2)}) collective-permute-start(bf16[128,2048]{1,0:T(8,128)(2,1)} %get-tuple-element.245.refs_1_), channel_id=1, source_target_pairs={{0,1},{1,0},{2,3},{3,2},{4,5},{5,4},{6,7},{7,6},{8,9},{9,8},{10,11... | collective-permute-start | bytes 1572872 | tf_op jit(solution)/shard_map/ppermute | solution.py:422
  252.3 19.6 %collective-permute-start.34 = (bf16[128,2048]{1,0:T(8,128)(2,1)}, bf16[128,2048]{1,0:T(8,128)(2,1)}, u32[]{:S(2)}, u32[]{:S(2)}) collective-permute-start(bf16[128,2048]{1,0:T(8,128)(2,1)} %get-tuple-element.244.refs_0_), channel_id=1, source_target_pairs={{0,2},{1,3},{2,0},{3,1},{4,6},{5,7},{6,4},{7,5},{8,10},{9,11},{10,... | collective-permute-start | bytes 1572872 | tf_op jit(solution)/shard_map/ppermute | solution.py:422
  253.9 21.8 %collective-permute-start.35 = (bf16[128,2048]{1,0:T(8,128)(2,1)}, bf16[128,2048]{1,0:T(8,128)(2,1)}, u32[]{:S(2)}, u32[]{:S(2)}) collective-permute-start(bf16[128,2048]{1,0:T(8,128)(2,1)} %get-tuple-element.245.refs_1_), channel_id=1, source_target_pairs={{0,2},{1,3},{2,0},{3,1},{4,6},{5,7},{6,4},{7,5},{8,10},{9,11},{10,... | collective-permute-start | bytes 1572872 | tf_op jit(solution)/shard_map/ppermute | solution.py:422
  306.2 17.4 %collective-permute-start.39 = (bf16[128,2048]{1,0:T(8,128)(2,1)}, bf16[128,2048]{1,0:T(8,128)(2,1)S(1)}, u32[]{:S(2)}, u32[]{:S(2)}) collective-permute-start(bf16[128,2048]{1,0:T(8,128)(2,1)} %get-tuple-element.264), channel_id=1, source_target_pairs={{0,1},{1,0},{2,3},{3,2},{4,5},{5,4},{6,7},{7,6},{8,9},{9,8},{10,11... | collective-permute-start | bytes 1572872 | tf_op jit(solution)/shard_map/ppermute | solution.py:422
  306.8 16.8 %collective-permute-start.40 = (bf16[128,2048]{1,0:T(8,128)(2,1)}, bf16[128,2048]{1,0:T(8,128)(2,1)}, u32[]{:S(2)}, u32[]{:S(2)}) collective-permute-start(bf16[128,2048]{1,0:T(8,128)(2,1)} %get-tuple-element.265), channel_id=1, source_target_pairs={{0,2},{1,3},{2,0},{3,1},{4,6},{5,7},{6,4},{7,5},{8,10},{9,11},{10,... | collective-permute-start | bytes 1572872 | tf_op jit(solution)/shard_map/ppermute | solution.py:422
  324.4 223.2 %reduce-scatter.6.cloned.1.call-start = ((), (), s32[]{:S(2)}) async-start(), calls=%async_computation.6 | async-start | bytes 14155776 | tf_op jit(solution)/shard_map/reduce_scatter | solution.py:609
  325.9 19.0 %collective-permute-start.38 = (bf16[128,2048]{1,0:T(8,128)(2,1)}, bf16[128,2048]{1,0:T(8,128)(2,1)S(1)}, u32[]{:S(2)}, u32[]{:S(2)}) collective-permute-start(bf16[128,2048]{1,0:T(8,128)(2,1)} %get-tuple-element.262), channel_id=1, source_target_pairs={{0,1},{1,0},{2,3},{3,2},{4,5},{5,4},{6,7},{7,6},{8,9},{9,8},{10,11... | collective-permute-start | bytes 1572872 | tf_op jit(solution)/shard_map/ppermute | solution.py:422
  328.8 15.9 %collective-permute-start.42 = (bf16[128,2048]{1,0:T(8,128)(2,1)S(1)}, bf16[128,2048]{1,0:T(8,128)(2,1)S(1)}, u32[]{:S(2)}, u32[]{:S(2)}) collective-permute-start(bf16[128,2048]{1,0:T(8,128)(2,1)S(1)} %add_convert_fusion.5), channel_id=1, source_target_pairs={{0,1},{1,0},{2,3},{3,2},{4,5},{5,4},{6,7},{7,6},{8,9},{9,8},{10,11... | collective-permute-start | bytes 1572872 | tf_op jit(solution)/shard_map/ppermute | solution.py:422
  351.6 19.7 %collective-permute-start.45 = (bf16[128,2048]{1,0:T(8,128)(2,1)S(1)}, bf16[128,2048]{1,0:T(8,128)(2,1)S(1)}, u32[]{:S(2)}, u32[]{:S(2)}) collective-permute-start(bf16[128,2048]{1,0:T(8,128)(2,1)S(1)} %get-tuple-element.442), channel_id=1, source_target_pairs={{0,1},{1,0},{2,3},{3,2},{4,5},{5,4},{6,7},{7,6},{8,9},{9,8},{10,11... | collective-permute-start | bytes 1572872 | tf_op jit(solution)/shard_map/ppermute | solution.py:422
  352.1 19.3 %collective-permute-start.46 = (bf16[128,2048]{1,0:T(8,128)(2,1)S(1)}, bf16[128,2048]{1,0:T(8,128)(2,1)S(1)}, u32[]{:S(2)}, u32[]{:S(2)}) collective-permute-start(bf16[128,2048]{1,0:T(8,128)(2,1)S(1)} %get-tuple-element.443), channel_id=1, source_target_pairs={{0,2},{1,3},{2,0},{3,1},{4,6},{5,7},{6,4},{7,5},{8,10},{9,11},{10,... | collective-permute-start | bytes 1572872 | tf_op jit(solution)/shard_map/ppermute | solution.py:422
  417.3 180.7 %reduce-scatter.8.cloned.1.call-start = ((), (), s32[]{:S(2)}) async-start(), calls=%async_computation.7 | async-start | bytes 4718592 | tf_op jit(solution)/shard_map/reduce_scatter | solution.py:634
  426.2 30.0 %collective-permute-start.50 = (bf16[256,2048]{1,0:T(8,128)(2,1)S(1)}, bf16[256,2048]{1,0:T(8,128)(2,1)S(1)}, u32[]{:S(2)}, u32[]{:S(2)}) collective-permute-start(bf16[256,2048]{1,0:T(8,128)(2,1)S(1)} %bitcast.138), channel_id=1, source_target_pairs={{0,1},{1,0},{2,3},{3,2},{4,5},{5,4},{6,7},{7,6},{8,9},{9,8},{10,11... | collective-permute-start | bytes 3145736 | tf_op jit(solution)/shard_map/ppermute | solution.py:422
  427.8 40.0 %collective-permute-start.51 = (bf16[256,2048]{1,0:T(8,128)(2,1)S(1)}, bf16[256,2048]{1,0:T(8,128)(2,1)S(1)}, u32[]{:S(2)}, u32[]{:S(2)}) collective-permute-start(bf16[256,2048]{1,0:T(8,128)(2,1)S(1)} %bitcast.137), channel_id=1, source_target_pairs={{0,2},{1,3},{2,0},{3,1},{4,6},{5,7},{6,4},{7,5},{8,10},{9,11},{10,... | collective-permute-start | bytes 3145736 | tf_op jit(solution)/shard_map/ppermute | solution.py:422
  429.4 42.4 %collective-permute-start.52 = (bf16[256,2048]{1,0:T(8,128)(2,1)S(1)}, bf16[256,2048]{1,0:T(8,128)(2,1)S(1)}, u32[]{:S(2)}, u32[]{:S(2)}) collective-permute-start(bf16[256,2048]{1,0:T(8,128)(2,1)S(1)} %bitcast.136), channel_id=1, source_target_pairs={{0,3},{1,2},{2,1},{3,0},{4,7},{5,6},{6,5},{7,4},{8,11},{9,10},{10,... | collective-permute-start | bytes 3145736 | tf_op jit(solution)/shard_map/ppermute | solution.py:422
  471.8 26.2 %collective-permute-start.58 = (bf16[128,2048]{1,0:T(8,128)(2,1)}, bf16[128,2048]{1,0:T(8,128)(2,1)}, u32[]{:S(2)}, u32[]{:S(2)}) collective-permute-start(bf16[128,2048]{1,0:T(8,128)(2,1)} %get-tuple-element.319), channel_id=1, source_target_pairs={{0,2},{1,3},{2,0},{3,1},{4,6},{5,7},{6,4},{7,5},{8,10},{9,11},{10,... | collective-permute-start | bytes 1572872 | tf_op jit(solution)/shard_map/ppermute | solution.py:422
  473.6 17.9 %collective-permute-start.55 = (bf16[128,2048]{1,0:T(8,128)(2,1)}, bf16[128,2048]{1,0:T(8,128)(2,1)}, u32[]{:S(2)}, u32[]{:S(2)}) collective-permute-start(bf16[128,2048]{1,0:T(8,128)(2,1)} %get-tuple-element.310), channel_id=1, source_target_pairs={{0,2},{1,3},{2,0},{3,1},{4,6},{5,7},{6,4},{7,5},{8,10},{9,11},{10,... | collective-permute-start | bytes 1572872 | tf_op jit(solution)/shard_map/ppermute | solution.py:422
  476.4 28.2 %collective-permute-start.53 = (bf16[128,2048]{1,0:T(8,128)(2,1)}, bf16[128,2048]{1,0:T(8,128)(2,1)}, u32[]{:S(2)}, u32[]{:S(2)}) collective-permute-start(bf16[128,2048]{1,0:T(8,128)(2,1)} %get-tuple-element.307), channel_id=1, source_target_pairs={{0,1},{1,0},{2,3},{3,2},{4,5},{5,4},{6,7},{7,6},{8,9},{9,8},{10,11... | collective-permute-start | bytes 1572872 | tf_op jit(solution)/shard_map/ppermute | solution.py:422
  520.8 32.8 %collective-permute-start.64 = (bf16[128,2048]{1,0:T(8,128)(2,1)S(1)}, bf16[128,2048]{1,0:T(8,128)(2,1)}, u32[]{:S(2)}, u32[]{:S(2)}) collective-permute-start(bf16[128,2048]{1,0:T(8,128)(2,1)S(1)} %copy-done.12), channel_id=1, source_target_pairs={{0,2},{1,3},{2,0},{3,1},{4,6},{5,7},{6,4},{7,5},{8,10},{9,11},{10,... | collective-permute-start | bytes 1572872 | tf_op jit(solution)/shard_map/ppermute | solution.py:422
  522.3 25.3 %collective-permute-start.60 = (bf16[128,2048]{1,0:T(8,128)(2,1)}, bf16[128,2048]{1,0:T(8,128)(2,1)}, u32[]{:S(2)}, u32[]{:S(2)}) collective-permute-start(bf16[128,2048]{1,0:T(8,128)(2,1)} %copy-done.14), channel_id=1, source_target_pairs={{0,1},{1,0},{2,3},{3,2},{4,5},{5,4},{6,7},{7,6},{8,9},{9,8},{10,11... | collective-permute-start | bytes 1572872 | tf_op jit(solution)/shard_map/ppermute | solution.py:422
  522.9 24.7 %collective-permute-start.61 = (bf16[128,2048]{1,0:T(8,128)(2,1)}, bf16[128,2048]{1,0:T(8,128)(2,1)}, u32[]{:S(2)}, u32[]{:S(2)}) collective-permute-start(bf16[128,2048]{1,0:T(8,128)(2,1)} %copy-done.13), channel_id=1, source_target_pairs={{0,2},{1,3},{2,0},{3,1},{4,6},{5,7},{6,4},{7,5},{8,10},{9,11},{10,... | collective-permute-start | bytes 1572872 | tf_op jit(solution)/shard_map/ppermute | solution.py:422
  524.2 37.4 %collective-permute-start.59 = (bf16[128,2048]{1,0:T(8,128)(2,1)S(1)}, bf16[128,2048]{1,0:T(8,128)(2,1)}, u32[]{:S(2)}, u32[]{:S(2)}) collective-permute-start(bf16[128,2048]{1,0:T(8,128)(2,1)S(1)} %copy-done.10), channel_id=1, source_target_pairs={{0,1},{1,0},{2,3},{3,2},{4,5},{5,4},{6,7},{7,6},{8,9},{9,8},{10,11... | collective-permute-start | bytes 1572872 | tf_op jit(solution)/shard_map/ppermute | solution.py:422
  (85 other events, 793.8 us)
Sparse Core Ops, SparseCore 0:
  51.2 119.6 all-gather.2
  173.1 80.3 all-gather.4
  324.5 90.0 reduce-scatter.3
  417.4 130.0 reduce-scatter.5
  549.7 48.3 reduce-scatter.7
